TPU v7x, 256 devices: a whole 4x4x8 slice. The times are simulated.
256 devices in a mesh: lat: 8 (over x, y_lo), lon: 32 (over z, y_hi, core).
Axes of the slice: x: 4, y: 4 (y_hi: 2, y_lo: 2; y = y_hi * 2 + y_lo), z: 8, core: 2. Of those that a mesh axis runs over, the one named last changes fastest.
Arguments:
- tokens: bfloat16 [2, 96, 768, 512], P(None, 'lat', 'lon'), may hold values from -6 to 6
- cotangent: bfloat16 [2, 96, 768, 512], P(None, 'lat', 'lon'), may hold values from -6 to 6
- qkv_weights: bfloat16 [2, 512, 1536], replicated, may hold values from -0.25 to 0.25
- proj_weights: bfloat16 [2, 512, 512], replicated, may hold values from -0.25 to 0.25
Outputs:
- d_tokens: bfloat16 [2, 96, 768, 512], P(None, 'lat', 'lon')
- d_qkv: float32 [2, 512, 1536], P(None, 'lat', 'lon')
- d_proj: float32 [2, 512, 512], P(None, 'lat', 'lon')
All inputs are finite; a program needn't handle non-finite values.
Results may differ from a plain program's by a relative error of at most 0.03.
Values may be sent and summed in bfloat16 or wider, within the bound.
No kernel may reach another device: no remote copies, remote signals or barrier semaphores. Data moves between devices by JAX's collectives and lax.ppermute only.
A program may use at most 128 MiB of HBM per device.

v0:
```python
import jax
import jax.numpy as jnp
from jax import lax
from jax.sharding import PartitionSpec as P

D = 512
HEADS = 8
HEAD_DIM = 64
WIN_LAT = 12
WIN_LON = 6


EPSILON = 1e-05
MASKED = -1000000000.0


def shifted(block, axis, distance):
    devices = range(lax.axis_size(axis))
    route = [((i - distance) % len(devices), i) for i in devices]
    return lax.ppermute(block, axis, route)


def to_windows(field):
    n_levels, n_rows, n_cols, feature = field.shape
    blocks = field.reshape(
        n_levels, n_rows // WIN_LAT, WIN_LAT, n_cols // WIN_LON, WIN_LON, feature
    )
    blocks = blocks.transpose(1, 3, 0, 2, 4, 5)
    return blocks.reshape(
        n_rows // WIN_LAT * (n_cols // WIN_LON), n_levels * WIN_LAT * WIN_LON, feature
    )


def from_windows(blocks, n_levels, n_rows, n_cols):
    feature = blocks.shape[-1]
    field = blocks.reshape(
        n_rows // WIN_LAT, n_cols // WIN_LON, n_levels, WIN_LAT, WIN_LON, feature
    )
    return field.transpose(2, 0, 3, 1, 4, 5).reshape(n_levels, n_rows, n_cols, feature)


def layer_norm(inputs):
    values_f = inputs.astype(jnp.float32)
    centred = values_f - jnp.mean(values_f, axis=-1, keepdims=True)
    inverse = lax.rsqrt(jnp.mean(centred * centred, axis=-1, keepdims=True) + EPSILON)
    return (centred * inverse, inverse)


def split_heads(part):
    return part.reshape(part.shape[0], part.shape[1], HEADS, -1)


def attend(normed, w_qkv, labels):
    packed = jnp.dot(normed, w_qkv, preferred_element_type=jnp.float32).astype(jnp.bfloat16)
    queries = split_heads(packed[..., :D])
    keys_h = split_heads(packed[..., D : 2 * D])
    values_h = split_heads(packed[..., 2 * D :])
    score_scale = HEAD_DIM ** (-0.5)
    scores = (
        jnp.einsum("wqhd,wkhd->whqk", queries, keys_h, preferred_element_type=jnp.float32)
        * score_scale
    )
    same_group = labels[:, None, :, None] == labels[:, None, None, :]
    scores = jnp.where(same_group, scores, MASKED)
    soft_probs = jax.nn.softmax(scores, axis=-1)
    probs_low = soft_probs.astype(jnp.bfloat16)
    mixed_out = jnp.einsum(
        "whqk,wkhd->wqhd", probs_low, values_h, preferred_element_type=jnp.float32
    ).astype(jnp.bfloat16)
    mixed_out = mixed_out.reshape(mixed_out.shape[0], mixed_out.shape[1], -1)
    return ((queries, keys_h, values_h), soft_probs, probs_low, mixed_out)


def block_forward(inputs, labels, w_qkv, w_proj):
    standard = layer_norm(inputs)[0]
    normed = standard.astype(jnp.bfloat16)
    mixed_out = attend(normed, w_qkv, labels)[3]
    return (
        inputs.astype(jnp.float32) + jnp.dot(mixed_out, w_proj, preferred_element_type=jnp.float32)
    ).astype(jnp.bfloat16)


def block_backward(inputs, upstream, labels, w_qkv, w_proj):
    standard, inverse = layer_norm(inputs)
    normed = standard.astype(jnp.bfloat16)
    heads, soft_probs, probs_low, mixed_out = attend(normed, w_qkv, labels)
    queries, keys_h, values_h = heads
    feature = inputs.shape[-1]
    grad_proj = jnp.dot(
        mixed_out.reshape(-1, feature).T,
        upstream.reshape(-1, feature),
        preferred_element_type=jnp.float32,
    )
    d_mixed = jnp.dot(upstream, w_proj.T, preferred_element_type=jnp.float32).astype(jnp.bfloat16)
    d_heads = split_heads(d_mixed)
    d_probs = jnp.einsum("wqhd,wkhd->whqk", d_heads, values_h, preferred_element_type=jnp.float32)
    d_values = jnp.einsum("whqk,wqhd->wkhd", probs_low, d_heads, preferred_element_type=jnp.float32)
    score_scale = HEAD_DIM ** (-0.5)
    d_scores = (
        soft_probs * (d_probs - jnp.sum(soft_probs * d_probs, axis=-1, keepdims=True)) * score_scale
    ).astype(jnp.bfloat16)
    d_queries = jnp.einsum("whqk,wkhd->wqhd", d_scores, keys_h, preferred_element_type=jnp.float32)
    d_keys = jnp.einsum("whqk,wqhd->wkhd", d_scores, queries, preferred_element_type=jnp.float32)
    n_win, n_tok = (inputs.shape[0], inputs.shape[1])
    d_packed = jnp.concatenate(
        [
            d_queries.reshape(n_win, n_tok, -1),
            d_keys.reshape(n_win, n_tok, -1),
            d_values.reshape(n_win, n_tok, -1),
        ],
        axis=-1,
    ).astype(jnp.bfloat16)
    grad_qkv = jnp.dot(
        normed.reshape(-1, feature).T,
        d_packed.reshape(-1, 3 * feature),
        preferred_element_type=jnp.float32,
    )
    d_normed = jnp.dot(d_packed, w_qkv.T, preferred_element_type=jnp.float32)
    d_input = inverse * (
        d_normed
        - jnp.mean(d_normed, axis=-1, keepdims=True)
        - standard * jnp.mean(d_normed * standard, axis=-1, keepdims=True)
    )
    result = (upstream.astype(jnp.float32) + d_input).astype(jnp.bfloat16)
    return (result, grad_qkv, grad_proj)


def reduce_grads(grad_qkv, grad_proj):
    partial_sums = (
        lax.psum_scatter(
            grad_qkv.astype(jnp.bfloat16), "lat", scatter_dimension=0, tiled=True
        ).astype(jnp.float32),
        lax.psum_scatter(
            grad_proj.astype(jnp.bfloat16), "lat", scatter_dimension=0, tiled=True
        ).astype(jnp.float32),
    )
    return (
        lax.psum_scatter(
            partial_sums[0].astype(jnp.bfloat16), "lon", scatter_dimension=1, tiled=True
        ).astype(jnp.float32),
        lax.psum_scatter(
            partial_sums[1].astype(jnp.bfloat16), "lon", scatter_dimension=1, tiled=True
        ).astype(jnp.float32),
    )


def body(tokens, cotangent, qkv_weights, proj_weights):
    n_levels, n_rows, n_cols, feature = tokens.shape
    half_lat = WIN_LAT // 2
    half_lon = WIN_LON // 2
    plain_tokens = to_windows(tokens)
    plain_labels = jnp.zeros(plain_tokens.shape[:2], jnp.int32)
    first_out = from_windows(
        block_forward(plain_tokens, plain_labels, qkv_weights[0], proj_weights[0]),
        n_levels,
        n_rows,
        n_cols,
    )
    stacked = jnp.stack([first_out, cotangent])
    below_rows = shifted(stacked[:, :, :half_lat], "lat", -1)
    tall_block = jnp.concatenate([stacked[:, :, half_lat:], below_rows], axis=2)
    beside = shifted(tall_block[:, :, :, :half_lon], "lon", -1)
    moved_pair = jnp.concatenate([tall_block[:, :, :, half_lon:], beside], axis=3)
    row_index = lax.broadcasted_iota(jnp.int32, (n_levels, n_rows, n_cols, 1), 1)
    last_lat = lax.axis_index("lat") == lax.axis_size("lat") - 1
    wrapped = jnp.where(last_lat & (row_index >= n_rows - half_lat), 1, 0).astype(jnp.int32)
    shifted_labels = to_windows(wrapped)[..., 0]
    d_moved, grad_qkv_two, grad_proj_two = block_backward(
        to_windows(moved_pair[0]),
        to_windows(moved_pair[1]),
        shifted_labels,
        qkv_weights[1],
        proj_weights[1],
    )
    reduced_two = reduce_grads(grad_qkv_two, grad_proj_two)
    d_shifted = from_windows(d_moved, n_levels, n_rows, n_cols)
    returned_cols = shifted(d_shifted[:, :, n_cols - half_lon :], "lon", 1)
    d_tall = jnp.concatenate([returned_cols, d_shifted[:, :, : n_cols - half_lon]], axis=2)
    returned_rows = shifted(d_tall[:, n_rows - half_lat :], "lat", 1)
    d_first = jnp.concatenate([returned_rows, d_tall[:, : n_rows - half_lat]], axis=1)
    d_plain, grad_qkv_one, grad_proj_one = block_backward(
        plain_tokens, to_windows(d_first), plain_labels, qkv_weights[0], proj_weights[0]
    )
    reduced_one = reduce_grads(grad_qkv_one, grad_proj_one)
    d_tokens = from_windows(d_plain, n_levels, n_rows, n_cols)
    return (
        d_tokens,
        jnp.stack([reduced_one[0], reduced_two[0]]),
        jnp.stack([reduced_one[1], reduced_two[1]]),
    )


def solution(mesh):
    return jax.shard_map(
        body,
        mesh=mesh,
        in_specs=(P(None, "lat", "lon", None), P(None, "lat", "lon", None), P(), P()),
        out_specs=(P(None, "lat", "lon", None), P(None, "lat", "lon"), P(None, "lat", "lon")),
        check_vma=False,
    )
```

profile of v0, /device:TPU:2, one launch (start us, length us, event | category | flops | bytes accessed | tf_op | source)
XLA Modules:
  0.0 761.6 jit_solution(10526620395820428170)
XLA Ops:
  7.2 1.7 copy.176
  13.1 1.3 copy.268
  14.4 1.3 copy.269
  16.2 5.9 fusion.112
  22.1 2.9 convolution_convert_fusion.5
  27.5 1.9 pad_maximum_fusion.8
  29.3 1.6 collective-permute-start
  31.3 13.2 %collective-permute-done = bf16[2,2,6,24,512]{4,1,3,2,0:T(2,128)(2,1)S(1)} collective-permute-done((bf16[2,2,6,24,512]{4,1,3,2,0:T(2,128)(2,1)S(1)}, bf16[2,2,6,24,512]{4,1,3,2,0:T(2,128)(2,1)S(1)}, u32[]{:S(2)}, u32[]{:S(2)}) %collective-permute-start) | collective-permute-done | bytes 589856 | tf_op jit(solution)/shard_map/ppermute | solution.py:20
  44.7 7.3 collective-permute-start.1
  52.0 1.4 fusion.65
  53.3 1.3 collective-permute-done.1
  54.6 1.6 pad_maximum_fusion.7
  58.8 1.1 multiply_reduce_fusion.5
  62.1 1.2 fusion.110
  63.4 2.2 copy.270
  65.5 2.2 copy.271
  67.7 1.3 copy.273
  69.0 2.6 convolution_convert_fusion.7
  71.5 1.6 copy.272
  73.2 4.3 fusion.114
  77.5 5.6 fusion.113
  83.0 4.2 fusion.58
  87.2 9.4 %fusion.48 = bf16[4,8,64,144]{3,2,1,0:T(8,128)(2,1)} fusion(bf16[4,144,8,64]{1,3,2,0:T(8,128)(2,1)} %bitcast.197, f32[4,8,144,144]{2,3,1,0:T(8,128)} %fusion.114, f32[4,8,144,144]{2,3,1,0:T(8,128)} %get-tuple-element.32, f32[4,8,144]{2,1,0:T(8,128)S(1)} %get-tuple-element.31), kind=kOutput, calls=%fused_computation.46 | convolution fusion | flops 89879184 | bytes 6506496 | tf_op jit(solution)/shard_map/whqk,wkhd->wqhd/dot_general | solution.py:102
  96.6 9.3 %fusion.51 = bf16[4,8,64,144]{3,2,1,0:T(8,128)(2,1)} fusion(bf16[4,144,8,64]{1,3,2,0:T(8,128)(2,1)} %bitcast.199, f32[4,8,144,144]{2,3,1,0:T(8,128)} %fusion.114, f32[4,8,144,144]{2,3,1,0:T(8,128)} %get-tuple-element.32, f32[4,8,144]{2,1,0:T(8,128)S(1)} %get-tuple-element.31), kind=kOutput, calls=%fused_computation.47 | convolution fusion | flops 89879184 | bytes 6506496 | tf_op jit(solution)/shard_map/whqk,wqhd->wkhd/dot_general | solution.py:103
  106.0 4.2 convolution_convert_fusion.4
  110.2 1.5 convert_bitcast_fusion
  112.8 1.1 copy.217
  113.9 2.0 copy.244
  116.7 1.4 reshape_reshape.15
  118.1 1.4 convolution_convert_fusion.8
  119.6 1.6 copy.213
  121.2 2.2 copy.214
  123.4 1.2 copy.215
  126.9 3.7 fusion.109
  132.9 7.6 collective-permute-done.2
  140.9 2.1 collective-permute-start.3
  142.9 1.8 copy.240
  144.8 3.0 reshape_reshape.12
  147.7 1.9 collective-permute-done.3
  149.6 1.8 fusion.73
  152.3 1.3 reshape_reshape.13
  153.7 2.5 convolution_convert_fusion.9
  156.2 4.3 fusion.15
  163.1 2.4 convolution_convert_fusion.6
  165.4 1.4 copy.274
  166.9 3.0 fusion.115
  169.9 9.4 %fusion.42 = bf16[4,8,64,144]{3,2,1,0:T(8,128)(2,1)} fusion(bf16[4,144,8,64]{1,3,2,0:T(8,128)(2,1)} %bitcast.192, f32[4,8,144,144]{2,3,1,0:T(8,128)} %fusion.115, f32[4,8,144,144]{2,3,1,0:T(8,128)} %get-tuple-element.30, f32[4,8,144]{2,1,0:T(8,128)S(1)} %copy-done.23), kind=kOutput, calls=%fused_computation.44 | convolution fusion | flops 89879184 | bytes 6506496 | tf_op jit(solution)/shard_map/whqk,wkhd->wqhd/dot_general | solution.py:102
  179.3 2.2 copy.233
  181.5 9.1 %fusion.45 = bf16[4,8,64,144]{3,2,1,0:T(8,128)(2,1)} fusion(bf16[4,144,8,64]{1,3,2,0:T(8,128)(2,1)S(1)} %bitcast.190, f32[4,8,144,144]{2,3,1,0:T(8,128)} %fusion.115, f32[4,8,144,144]{2,3,1,0:T(8,128)} %get-tuple-element.30, f32[4,8,144]{2,1,0:T(8,128)S(1)} %copy-done.23), kind=kOutput, calls=%fused_computation.45 | convolution fusion | flops 89879184 | bytes 6506496 | tf_op jit(solution)/shard_map/whqk,wqhd->wkhd/dot_general | solution.py:103
  190.6 2.1 copy.234
  192.7 3.3 convolution_convert_fusion.3
  196.5 4.3 fusion.14
  200.9 1.6 copy.265
  202.6 2.4 reduce-scatter.21.cloned.1.call-done
  205.0 1.6 copy.263
  206.6 3.2 fusion.108
  209.9 44.2 %reduce-scatter.19.cloned.1.call-done = bf16[64,1536]{1,0:T(8,128)(2,1)} async-done(((bf16[512,1536]{1,0:T(8,128)(2,1)}), bf16[64,1536]{1,0:T(8,128)(2,1)}) %reduce-scatter.19.cloned.1.call-update) | async-done | bytes 196624 | tf_op jit(solution)/shard_map/reduce_scatter | solution.py:130
  254.1 1.8 copy.261
  256.0 46.4 %reduce-scatter.17.cloned.1.call-done = bf16[64,1536]{1,0:T(8,128)(2,1)} async-done(((bf16[512,1536]{1,0:T(8,128)(2,1)}), bf16[64,1536]{1,0:T(8,128)(2,1)}) %reduce-scatter.17.cloned.1.call-update) | async-done | bytes 196624 | tf_op jit(solution)/shard_map/reduce_scatter | solution.py:130
  302.4 1.8 copy.259
  306.8 108.6 %reduce-scatter.31.cloned.1.call-done = bf16[16,64]{1,0:T(8,128)(2,1)} async-done(((bf16[512,64]{1,0:T(8,128)(2,1)}), bf16[16,64]{1,0:T(8,128)(2,1)}) %reduce-scatter.31.cloned.1.call-update) | async-done | bytes 2064
  416.3 110.4 %reduce-scatter.29.cloned.1.call-done = bf16[16,64]{1,0:T(8,128)(2,1)} async-done(((bf16[512,64]{1,0:T(8,128)(2,1)}), bf16[16,64]{1,0:T(8,128)(2,1)}) %reduce-scatter.29.cloned.1.call-update) | async-done | bytes 2064
  528.2 111.8 %reduce-scatter.27.cloned.1.call-done = bf16[48,64]{1,0:T(8,128)(2,1)} async-done(((bf16[1536,64]{1,0:T(8,128)(2,1)}), bf16[48,64]{1,0:T(8,128)(2,1)}) %reduce-scatter.27.cloned.1.call-update) | async-done | bytes 6160
  640.8 112.3 %reduce-scatter.25.cloned.1.call-done = bf16[48,64]{1,0:T(8,128)(2,1)} async-done(((bf16[1536,64]{1,0:T(8,128)(2,1)}), bf16[48,64]{1,0:T(8,128)(2,1)}) %reduce-scatter.25.cloned.1.call-update) | async-done | bytes 6160
  (127 shorter events, 30.5 us)
Async XLA Ops:
  7.2 193.7 %reduce-scatter.23.cloned.1.call-start = ((), (), s32[]{:S(2)}) async-start(), calls=%async_computation.11 | async-start | bytes 589824 | tf_op jit(solution)/shard_map/reduce_scatter | solution.py:133
  9.8 2.0 copy-start.5
  9.8 2.1 copy-start.20
  10.7 1.1 copy-start.10
  16.2 5.9 copy-start.3
  22.1 2.9 copy-start.22
  22.1 3.0 copy-start.19
  25.0 1.8 copy-start.1
  25.1 1.8 copy-start.18
  29.3 15.1 %collective-permute-start = (bf16[2,2,6,24,512]{4,1,3,2,0:T(2,128)(2,1)S(1)}, bf16[2,2,6,24,512]{4,1,3,2,0:T(2,128)(2,1)S(1)}, u32[]{:S(2)}, u32[]{:S(2)}) collective-permute-start(bf16[2,2,6,24,512]{4,1,3,2,0:T(2,128)(2,1)S(1)} %get-tuple-element.27), channel_id=1, source_target_pairs={{32,0},{64,32},{96,64},{128,96},{160,128},{192,160},{224,192},{0,2... | collective-permute-start | bytes 1769480 | tf_op jit(solution)/shard_map/ppermute | solution.py:20
  44.7 10.0 %collective-permute-start.1 = (bf16[2,2,12,3,512]{4,1,3,2,0:T(2,128)(2,1)S(1)}, bf16[2,2,12,3,512]{4,1,3,2,0:T(2,128)(2,1)S(1)}, u32[]{:S(2)}, u32[]{:S(2)}) collective-permute-start(bf16[2,2,12,3,512]{4,1,3,2,0:T(2,128)(2,1)S(1)} %pad_maximum_fusion.9), channel_id=1, source_target_pairs={{1,0},{2,1},{3,2},{4,3},{5,4},{6,5},{7,6},{8,7},{9,8},{10,9},{11,1... | collective-permute-start | bytes 442376 | tf_op jit(solution)/shard_map/ppermute | solution.py:20
  58.7 2.3 copy-start.21
  116.7 2.9 copy-start.13
  119.5 85.4 %reduce-scatter.21.cloned.1.call-start = ((), (), s32[]{:S(2)}) async-start(), calls=%async_computation.10 | async-start | bytes 589824 | tf_op jit(solution)/shard_map/reduce_scatter | solution.py:133
  119.6 5.0 copy-start
  121.2 2.2 copy-start.14
  126.9 3.7 copy-start.9
  131.3 11.7 %copy-start.2 = (bf16[4,8,64,144]{3,2,1,0:T(8,128)(2,1)S(1)}, bf16[4,8,64,144]{3,2,1,0:T(8,128)(2,1)}, u32[]{:S(2)}) copy-start(bf16[4,8,64,144]{3,2,1,0:T(8,128)(2,1)} %copy-done.1) | copy-start | bytes 1769476
  132.4 8.1 %collective-permute-start.2 = (bf16[2,12,3,512]{3,0,2,1:T(2,128)(2,1)S(1)}, bf16[2,12,3,512]{3,0,2,1:T(2,128)(2,1)S(1)}, u32[]{:S(2)}, u32[]{:S(2)}) collective-permute-start(bf16[2,12,3,512]{3,0,2,1:T(2,128)(2,1)S(1)} %slice.97), channel_id=1, source_target_pairs={{31,0},{0,1},{1,2},{2,3},{3,4},{4,5},{5,6},{6,7},{7,8},{8,9},{9,10... | collective-permute-start | bytes 221192 | tf_op jit(solution)/shard_map/ppermute | solution.py:20
  140.9 8.7 %collective-permute-start.3 = (bf16[2,6,24,512]{3,0,2,1:T(2,128)(2,1)S(1)}, bf16[2,6,24,512]{3,0,2,1:T(2,128)(2,1)}, u32[]{:S(2)}, u32[]{:S(2)}) collective-permute-start(bf16[2,6,24,512]{3,0,2,1:T(2,128)(2,1)S(1)} %fusion.90), channel_id=1, source_target_pairs={{224,0},{0,32},{32,64},{64,96},{96,128},{128,160},{160,192},{192,2... | collective-permute-start | bytes 884744 | tf_op jit(solution)/shard_map/ppermute | solution.py:20
  156.2 4.7 copy-start.11
  156.2 5.1 copy-start.6
  156.2 97.9 %reduce-scatter.19.cloned.1.call-start = ((), (), s32[]{:S(2)}) async-start(), calls=%async_computation.9 | async-start | bytes 1769472 | tf_op jit(solution)/shard_map/reduce_scatter | solution.py:130
  160.6 141.8 %reduce-scatter.17.cloned.1.call-start = ((), (), s32[]{:S(2)}) async-start(), calls=%async_computation.8 | async-start | bytes 1769472 | tf_op jit(solution)/shard_map/reduce_scatter | solution.py:130
  162.0 4.8 copy-start.4
  162.3 0.8 copy-start.7
  166.9 3.0 copy-start.23
  169.9 11.6 %copy-start.12 = (bf16[4,144,512]{1,2,0:T(8,128)(2,1)S(1)}, bf16[4,144,512]{1,2,0:T(8,128)(2,1)}, u32[]{:S(2)}) copy-start(bf16[4,144,512]{1,2,0:T(8,128)(2,1)} %copy.268) | copy-start | bytes 1769476
  196.5 4.3 copy-start.17
  196.5 10.1 %copy-start.15 = (bf16[4,144,512]{2,1,0:T(8,128)(2,1)S(1)}, bf16[4,144,512]{2,1,0:T(8,128)(2,1)}, u32[]{:S(2)}) copy-start(bf16[4,144,512]{2,1,0:T(8,128)(2,1)} %copy.233) | copy-start | bytes 1769476
  196.5 10.1 %copy-start.16 = (bf16[4,144,512]{2,1,0:T(8,128)(2,1)S(1)}, bf16[4,144,512]{2,1,0:T(8,128)(2,1)}, u32[]{:S(2)}) copy-start(bf16[4,144,512]{2,1,0:T(8,128)(2,1)} %copy.234) | copy-start | bytes 1769476
  200.8 214.6 %reduce-scatter.31.cloned.1.call-start = ((), (), s32[]{:S(2)}) async-start(), calls=%async_computation.15 | async-start | bytes 135168
  202.5 324.2 %reduce-scatter.29.cloned.1.call-start = ((), (), s32[]{:S(2)}) async-start(), calls=%async_computation.14 | async-start | bytes 135168
  206.6 433.4 %reduce-scatter.27.cloned.1.call-start = ((), (), s32[]{:S(2)}) async-start(), calls=%async_computation.13 | async-start | bytes 405504
  209.9 94.4 %copy-start.8 = (bf16[1,4,2,12,6,512]{5,1,4,3,2,0:T(4,128)(2,1)S(1)}, bf16[1,4,2,12,6,512]{5,1,4,3,2,0:T(4,128)(2,1)}, u32[]{:S(2)}) copy-start(bf16[1,4,2,12,6,512]{5,1,4,3,2,0:T(4,128)(2,1)} %copy-done.7) | copy-start | bytes 1769476
  255.9 497.2 %reduce-scatter.25.cloned.1.call-start = ((), (), s32[]{:S(2)}) async-start(), calls=%async_computation.12 | async-start | bytes 405504
Sparse Core Ops, SparseCore 0:
  119.6 39.5 reduce-scatter.22
  161.9 42.9 reduce-scatter.20
  207.5 46.4 reduce-scatter.18
  256.5 45.8 reduce-scatter.16
  306.1 109.2 reduce-scatter.30
  419.7 106.9 reduce-scatter.28
  530.7 109.2 reduce-scatter.26
  644.0 109.0 reduce-scatter.24
where the time goes:
time: 771 us; the launch traced here: 762 us
  waiting for transfers between devices  560 us (73%)
  matrix products  97.8 us (13%)
  local copies, waits for them, and re-layouts  61.6 us (8%)
  other arithmetic  15.4 us (2%)
  between operations  15 us (2%)
  starting transfers between devices  11.5 us (1%)
    unnamed x12, waiting for transfers between devices  443 us
    reduce_scatter x2, waiting for transfers between devices, reduce_grads(): lax.psum_scatter(grad_qkv.astype(jnp.bfloat16), 'lat', scatter_dimension=...  90.6 us
    ppermute x4, waiting for transfers between devices, shifted(): return lax.ppermute(block, axis, route)  24 us
    dot_general x2, matrix products, block_backward(): jnp.einsum('whqk,wkhd->wqhd', d_scores, keys_h, preferred_element_type=jn...  18.8 us
    dot_general x2, matrix products, block_backward(): jnp.einsum('whqk,wqhd->wkhd', d_scores, queries, preferred_element_type=j...  18.5 us
  transfers between devices with their start and end apart: 12, of which 11 were waited for; matrix products, arithmetic and copies ran while one was open for 11% of the time, Pallas kernels for 0%

commit v1 on v0

v1 whole, which is shorter than its diff:
```python
import functools

import jax
import jax.numpy as jnp
import numpy as np
from jax import lax
from jax.experimental import pallas as pl
from jax.experimental.pallas import tpu as pltpu
from jax.sharding import PartitionSpec as P

D = 512
HEADS = 8
HEAD_DIM = 64
LEVELS = 2
WIN_LAT = 12
WIN_LON = 6
HALF_LAT = 6
HALF_LON = 3
ROWS = 12
COLS = 24
TOKENS = LEVELS * ROWS * COLS
WINDOW = LEVELS * WIN_LAT * WIN_LON
WINDOWS = TOKENS // WINDOW
HALF = TOKENS // 2
STRIP = LEVELS * HALF_LAT * HALF_LON
SOURCE = 2 * HALF + 2 * STRIP
QUAD = 4 * HEAD_DIM
EPSILON = 1e-05
MASKED = -1000000000.0
SCALE = HEAD_DIM ** (-0.5)
F32 = jnp.float32
BF16 = jnp.bfloat16


def window_order(level, row, col):
    return (col // WIN_LON) * WINDOW + (level * WIN_LAT + row) * WIN_LON + col % WIN_LON


def plain_matrix():
    out = np.zeros((TOKENS, TOKENS), np.float32)
    for level, row, col in np.ndindex(LEVELS, ROWS, COLS):
        out[window_order(level, row, col), (level * ROWS + row) * COLS + col] = 1
    return out


def piece_index(level, row, col, narrow):
    upper = row < HALF_LAT
    at = level * HALF_LAT + row % HALF_LAT
    if narrow:
        return 2 * HALF + (STRIP if upper else 0) + at * HALF_LON + col
    return (HALF if upper else 0) + at * COLS + col


def cut_matrix():
    out = np.zeros((SOURCE, TOKENS), np.float32)
    for level, row, col in np.ndindex(LEVELS, ROWS, COLS):
        out[piece_index(level, row, col, False), window_order(level, row, col)] = 1
        if col < HALF_LON:
            out[piece_index(level, row, col, True), window_order(level, row, col)] = 1
    return out


def shifted_matrix():
    out = np.zeros((TOKENS, SOURCE), np.float32)
    for level, row, col in np.ndindex(LEVELS, ROWS, COLS):
        from_row, from_col = (row + HALF_LAT) % ROWS, col + HALF_LON
        place = piece_index(level, from_row, from_col % COLS, from_col >= COLS)
        out[window_order(level, row, col), place] = 1
    return out


def joined_matrix():
    out = np.zeros((TOKENS, SOURCE), np.float32)
    for level, row, col in np.ndindex(LEVELS, ROWS, COLS):
        out[window_order(level, row, col), piece_index(level, row, col, col < HALF_LON)] = 1
    return out


def dot(a, b):
    return lax.dot_general(a, b, (((1,), (0,)), ((), ())), preferred_element_type=F32)


def dot_nt(a, b):
    return lax.dot_general(a, b, (((1,), (1,)), ((), ())), preferred_element_type=F32)


def dot_tn(a, b):
    return lax.dot_general(a, b, (((0,), (0,)), ((), ())), preferred_element_type=F32)


def layer_norm(values):
    centred = values - jnp.mean(values, axis=-1, keepdims=True)
    inverse = lax.rsqrt(jnp.mean(centred * centred, axis=-1, keepdims=True) + EPSILON)
    return centred * inverse, inverse


def head_of_lane(rows):
    return lax.broadcasted_iota(jnp.int32, (rows, QUAD), 1) // HEAD_DIM


def stacked(part, scale):
    lane = head_of_lane(1)
    wide = [part * jnp.where(lane == h, scale, 0.0).astype(BF16) for h in range(4)]
    return jnp.concatenate(wide, axis=0)


def unstacked(product):
    lane = head_of_lane(WINDOW)
    out = product[:WINDOW]
    for h in range(1, 4):
        out = jnp.where(lane == h, product[h * WINDOW : (h + 1) * WINDOW], out)
    return out


def soft(keys_stacked, queries, bias):
    scores = dot_nt(keys_stacked, queries).reshape(4, WINDOW, WINDOW)
    if bias is not None:
        scores = scores + bias[None]
    top = jnp.max(scores, axis=1, keepdims=True)
    raised = jnp.exp(scores - top)
    return raised * (1.0 / jnp.sum(raised, axis=1, keepdims=True))


def forward_kernel(tokens, w_qkv, w_proj, plain, cut, pieces, packed_out):
    values = dot(plain[...], tokens[...])
    normed = layer_norm(values)[0].astype(BF16)
    packed = dot(normed, w_qkv[...]).astype(BF16)
    packed_out[...] = packed
    rows = []
    for w in range(WINDOWS):
        cols = []
        for quad in range(2):
            part = [
                packed_out[w * WINDOW : (w + 1) * WINDOW, n * D + quad * QUAD : n * D + (quad + 1) * QUAD]
                for n in range(3)
            ]
            probs = soft(stacked(part[1], SCALE), part[0], None).astype(BF16)
            cols.append(dot_tn(probs.reshape(4 * WINDOW, WINDOW), stacked(part[2], 1.0)).astype(BF16))
        rows.append(jnp.concatenate(cols, axis=1))
    mixed = jnp.concatenate(rows, axis=0)
    first = (values + dot(mixed, w_proj[...])).astype(BF16)
    pieces[...] = dot(cut[...], first).astype(BF16)


def backward_kernel(*refs, masked, saved):
    refs = list(refs)
    inputs, upstream, w_qkv, w_proj, gather_u, gather_g, scatter = refs[:7]
    refs = refs[7:]
    bias = refs.pop(0)[...] if masked else None
    packed_in = refs.pop(0) if saved else None
    d_out, grad_qkv, grad_proj, mixed_ref, d_mixed_ref, d_packed_ref = refs[:6]
    values = dot(gather_u[...], inputs[...])
    standard, inverse = layer_norm(values)
    normed = standard.astype(BF16)
    if saved:
        packed_ref = packed_in
    else:
        packed_ref = refs[6]
        packed_ref[...] = dot(normed, w_qkv[...]).astype(BF16)
    gradient = dot(gather_g[...], upstream[...])
    low = gradient.astype(BF16)
    d_mixed_ref[...] = dot_nt(low, w_proj[...]).astype(BF16)
    for w in range(WINDOWS):
        span = slice(w * WINDOW, (w + 1) * WINDOW)
        for quad in range(2):
            at = [slice(n * D + quad * QUAD, n * D + (quad + 1) * QUAD) for n in range(3)]
            queries, keys, vals = [packed_ref[span, at[n]] for n in range(3)]
            d_mixed = d_mixed_ref[span, at[0]]
            keys_stacked, vals_stacked = stacked(keys, SCALE), stacked(vals, 1.0)
            probs = soft(keys_stacked, queries, bias)
            probs_low = probs.astype(BF16).reshape(4 * WINDOW, WINDOW)
            mixed_ref[span, at[0]] = dot_tn(probs_low, vals_stacked).astype(BF16)
            d_probs = dot_nt(vals_stacked, d_mixed).reshape(4, WINDOW, WINDOW)
            inner = jnp.sum(probs * d_probs, axis=1, keepdims=True)
            d_scores = (probs * (d_probs - inner)).astype(BF16).reshape(4 * WINDOW, WINDOW)
            d_packed_ref[span, at[0]] = dot_tn(d_scores, keys_stacked).astype(BF16)
            d_packed_ref[span, at[1]] = (unstacked(dot(d_scores, queries)) * SCALE).astype(BF16)
            d_packed_ref[span, at[2]] = unstacked(dot(probs_low, d_mixed)).astype(BF16)
    d_packed = d_packed_ref[...]
    grad_proj[...] = dot_tn(mixed_ref[...], low).astype(BF16)
    grad_qkv[...] = dot_tn(normed, d_packed).astype(BF16)
    d_normed = dot_nt(d_packed, w_qkv[...])
    d_input = inverse * (
        d_normed
        - jnp.mean(d_normed, axis=-1, keepdims=True)
        - standard * jnp.mean(d_normed * standard, axis=-1, keepdims=True)
    )
    d_out[...] = dot_tn(scatter[...], (gradient + d_input).astype(BF16)).astype(BF16)


def shape(*dims, kind=BF16):
    return jax.ShapeDtypeStruct(dims, kind)


PARAMS = pltpu.CompilerParams(vmem_limit_bytes=48 * 1024 * 1024)


def forward(tokens, w_qkv, w_proj, plain, cut):
    return pl.pallas_call(
        forward_kernel,
        out_shape=(shape(SOURCE, D), shape(TOKENS, 3 * D)),
        compiler_params=PARAMS,
        name="forward",
    )(tokens, w_qkv, w_proj, plain, cut)


def backward(inputs, upstream, w_qkv, w_proj, gather_u, gather_g, scatter, bias=None, packed=None):
    extra = [x for x in (bias, packed) if x is not None]
    scratch = [pltpu.VMEM((TOKENS, D), BF16), pltpu.VMEM((TOKENS, D), BF16), pltpu.VMEM((TOKENS, 3 * D), BF16)]
    if packed is None:
        scratch.append(pltpu.VMEM((TOKENS, 3 * D), BF16))
    return pl.pallas_call(
        functools.partial(backward_kernel, masked=bias is not None, saved=packed is not None),
        out_shape=(shape(scatter.shape[1], D), shape(D, 3 * D), shape(D, D)),
        scratch_shapes=scratch,
        compiler_params=PARAMS,
        name="backward_shifted" if packed is None else "backward_plain",
    )(inputs, upstream, w_qkv, w_proj, gather_u, gather_g, scatter, *extra)


def moved(piece, lat, lon):
    axes, n_lat, n_lon = ("lat", "lon"), lax.axis_size("lat"), lax.axis_size("lon")
    route = [
        (a * n_lon + b, (a + lat) % n_lat * n_lon + (b + lon) % n_lon)
        for a in range(n_lat)
        for b in range(n_lon)
    ]
    return lax.ppermute(piece, axes, route)


def exchanged(pieces, step):
    tall = moved(pieces[1], step, 0)
    side = moved(pieces[2], 0, step)
    corner = moved(pieces[3], step, step)
    return jnp.concatenate([pieces[0], tall, side, corner], axis=0)


def cut_pieces(joint):
    return [joint[:HALF], joint[HALF : 2 * HALF], joint[2 * HALF : 2 * HALF + STRIP], joint[2 * HALF + STRIP :]]


def field_pieces(field):
    low, up = field[:, HALF_LAT:], field[:, :HALF_LAT]
    parts = [low, up, low[:, :, :HALF_LON], up[:, :, :HALF_LON]]
    return [part.reshape(-1, D) for part in parts]


def reduce_grads(grad_qkv, grad_proj):
    parts = [lax.psum_scatter(x, "lat", scatter_dimension=0, tiled=True) for x in (grad_qkv, grad_proj)]
    return [lax.psum_scatter(x, "lon", scatter_dimension=1, tiled=True).astype(F32) for x in parts]


def body(tokens, cotangent, qkv_weights, proj_weights):
    plain, cut, shift, join = [
        jnp.asarray(make(), BF16) for make in (plain_matrix, cut_matrix, shifted_matrix, joined_matrix)
    ]
    upstream = exchanged(field_pieces(cotangent), -1)
    flat = tokens.reshape(TOKENS, D)
    pieces, packed = forward(flat, qkv_weights[0], proj_weights[0], plain, cut)
    first = exchanged(cut_pieces(pieces), -1)
    last_lat = lax.axis_index("lat") == lax.axis_size("lat") - 1
    label = (np.arange(WINDOW) // WIN_LON % WIN_LAT >= HALF_LAT).astype(np.int32)
    bias = jnp.where(last_lat & (label[:, None] != label[None, :]), MASKED, 0.0).astype(F32)
    d_moved, grad_qkv_two, grad_proj_two = backward(
        first, upstream, qkv_weights[1], proj_weights[1], shift, shift, shift, bias=bias
    )
    reduced_two = reduce_grads(grad_qkv_two, grad_proj_two)
    d_first = exchanged(cut_pieces(d_moved), 1)
    d_tokens, grad_qkv_one, grad_proj_one = backward(
        flat, d_first, qkv_weights[0], proj_weights[0], plain, join, plain, packed=packed
    )
    reduced_one = reduce_grads(grad_qkv_one, grad_proj_one)
    return (
        d_tokens.reshape(tokens.shape),
        jnp.stack([reduced_one[0], reduced_two[0]]),
        jnp.stack([reduced_one[1], reduced_two[1]]),
    )


def solution(mesh):
    return jax.shard_map(
        body,
        mesh=mesh,
        in_specs=(P(None, "lat", "lon", None), P(None, "lat", "lon", None), P(), P()),
        out_specs=(P(None, "lat", "lon", None), P(None, "lat", "lon"), P(None, "lat", "lon")),
        check_vma=False,
    )
```

time: 771 us -> 693 us (0.90); the launches traced: 762 us -> 693 us
  matrix products: 97.8 us -> 0 us
  local copies, waits for them, and re-layouts: 61.6 us -> 16.6 us
  waiting for transfers between devices: 560 us -> 604 us
  Pallas kernels: 0 us -> 38.4 us
  other arithmetic: 15.4 us -> 2.56 us
    dot_general x21 -> x0, matrix products: 86.3 us -> none  [the longest x2 18.8 us: block_backward(): jnp.einsum('whqk,wkhd->wqhd', d_scores, keys_h, preferred_element_type=jn...]
    reduce_scatter x4, waiting for transfers between devices: 93 us -> 141 us  [reduce_grads(): lax.psum_scatter(x, 'lat', scatter_dimension=0, tiled=True)]
    pallas_call x0 -> x3, Pallas kernels: none -> 38.4 us  [the longest x2 32 us: backward(): pl.pallas_call(functools.partial(backward_kernel, masked=bias is not None...]
    reshape x14 -> x2, local copies, waits for them, and re-layouts: 21.5 us -> 0.08 us  [field_pieces(): return [part.reshape(-1, D) for part in parts]]
    sub x2 -> x0, matrix products: 11.5 us -> none  [attend(): soft_probs = jax.nn.softmax(scores, axis=-1)]
    ppermute x4 -> x9, waiting for transfers between devices: 24 us -> 15.5 us  [moved(): return lax.ppermute(piece, axes, route)]
    convert_element_type x10 -> x0, local copies, waits for them, and re-layouts: 8.29 us -> none  [the longest x2 3.87 us: attend(): mixed_out = jnp.einsum('whqk,wkhd->wqhd', probs_low, values_h, preferred_...]
    ppermute x4 -> x9, starting transfers between devices: 11 us -> 16 us  [moved(): return lax.ppermute(piece, axes, route)]
  transfers between devices with their start and end apart: 12 -> 17, of which waited for: 11 -> 13; matrix products, arithmetic and copies ran while one was open for 11% -> 2% of each run, Pallas kernels for 0% -> 3%
where the time goes in v1:
time: 693 us
  waiting for transfers between devices  604 us (87%)
  Pallas kernels  38.4 us (6%)
  local copies, waits for them, and re-layouts  16.6 us (2%)
  starting transfers between devices  16.3 us (2%)
  between operations  14.3 us (2%)
    unnamed x12, waiting for transfers between devices  448 us
    reduce_scatter x4, waiting for transfers between devices, reduce_grads(): lax.psum_scatter(x, 'lat', scatter_dimension=0, tiled=True)  141 us
    pallas_call x2, Pallas kernels, backward(): pl.pallas_call(functools.partial(backward_kernel, masked=bias is not None...  32 us
    ppermute x9, starting transfers between devices, moved(): return lax.ppermute(piece, axes, route)  16 us
    ppermute x9, waiting for transfers between devices, moved(): return lax.ppermute(piece, axes, route)  15.5 us
  transfers between devices with their start and end apart: 17, of which 13 were waited for; matrix products, arithmetic and copies ran while one was open for 2% of the time, Pallas kernels for 3%

profile of v1, /device:TPU:2, one launch (start us, length us, event | category | flops | bytes accessed | tf_op | source)
XLA Modules:
  0.0 692.6 jit_solution(13440126510986601663)
XLA Ops:
  7.2 0.0 reduce-scatter.23.cloned.1.call-start
  7.2 1.0 fusion.5
  8.2 7.8 %collective-permute-start.5 = (bf16[36,512]{1,0:T(8,128)(2,1)S(1)}, bf16[36,512]{1,0:T(8,128)(2,1)S(1)}, u32[]{:S(2)}, u32[]{:S(2)}) collective-permute-start(bf16[36,512]{1,0:T(8,128)(2,1)S(1)} %reshape.28), channel_id=1, source_target_pairs={{0,255},{1,224},{2,225},{3,226},{4,227},{5,228},{6,229},{7,230},{8... | collective-permute-start | bytes 110600 | tf_op jit(solution)/shard_map/ppermute | solution.py:228
  16.1 1.8 collective-permute-start.4
  17.9 2.1 fusion.4
  20.0 0.1 collective-permute-start.3
  20.1 2.1 slice_bitcast_fusion.2
  22.2 1.3 slice_bitcast_fusion
  23.5 0.4 copy-done.3
  23.9 0.4 copy-done.6
  24.3 6.4 forward.1
  30.7 0.0 copy-start.9
  30.7 0.4 collective-permute-start.1
  31.2 3.8 collective-permute-start
  35.1 0.0 collective-permute-done.5
  35.1 0.3 collective-permute-start.2
  35.4 0.0 collective-permute-done.4
  35.4 0.0 copy-start.1
  35.4 0.0 copy-start.4
  35.4 1.1 pad_maximum_fusion.1.refs_1_
  36.5 4.2 collective-permute-done.2
  40.8 1.6 collective-permute-done
  42.4 0.1 pad_maximum_fusion.refs_0_
  42.4 16.0 %backward_shifted.1 = (bf16[648,512]{1,0:T(8,128)(2,1)S(1)}, bf16[512,1536]{1,0:T(8,128)(2,1)}, bf16[512,512]{1,0:T(8,128)(2,1)}) custom-call(bf16[648,512]{1,0:T(8,128)(2,1)S(1)} %pad_maximum_fusion.refs_0_, bf16[648,512]{1,0:T(8,128)(2,1)S(1)} %pad_maximum_fusion.1.refs_1_, bf16[512,1536]{1,0:T(8,128)(2,1)} %get-tuple-element.28.refs_2_, ...), custom_call_target="tpu_custom_call" | custom-call | tf_op jit(solution)/shard_map/backward_shifted/pallas_call | solution.py:212
  58.5 0.0 reduce-scatter.23.cloned.1.call-update
  58.5 0.0 reduce-scatter.21.cloned.1.call-start
  58.5 0.0 copy-start.5
  58.6 1.5 collective-permute-start.6
  60.2 0.1 collective-permute-start.7
  60.2 0.1 collective-permute-start.8
  60.3 6.9 %collective-permute-done.7 = bf16[36,512]{1,0:T(8,128)(2,1)S(1)} collective-permute-done((bf16[36,512]{1,0:T(8,128)(2,1)S(1)}, bf16[36,512]{1,0:T(8,128)(2,1)S(1)}, u32[]{:S(2)}, u32[]{:S(2)}) %collective-permute-start.7) | collective-permute-done | bytes 36896 | tf_op jit(solution)/shard_map/ppermute | solution.py:228
  67.3 1.8 collective-permute-done.8
  69.1 0.9 collective-permute-done.6
  70.0 0.1 pad_maximum_fusion.2.refs_1_
  70.1 16.0 %backward_plain.1 = (bf16[576,512]{1,0:T(8,128)(2,1)}, bf16[512,1536]{1,0:T(8,128)(2,1)}, bf16[512,512]{1,0:T(8,128)(2,1)}) custom-call(bf16[576,512]{1,0:T(8,128)(2,1)S(1)} %bitcast.27, bf16[648,512]{1,0:T(8,128)(2,1)S(1)} %pad_maximum_fusion.2.refs_1_, bf16[512,1536]{1,0:T(8,128)(2,1)} %copy-done, bf16[512,512]{1,0:T(8,128)(2,1)S(1)} %get-tuple-element.31.w_proj.refs_3_, ...), custom_call_target="tpu_custom_call" | custom-call | tf_op jit(solution)/shard_map/backward_plain/pallas_call | solution.py:212
  86.1 0.0 reduce-scatter.21.cloned.1.call-update
  86.1 0.0 reduce-scatter.19.cloned.1.call-start
  86.2 0.7 reduce-scatter.19.cloned.1.call-update
  86.8 0.0 reduce-scatter.17.cloned.1.call-start
  86.9 0.5 reduce-scatter.17.cloned.1.call-update
  87.4 0.0 reduce-scatter.31.cloned.1.call-start
  87.5 6.9 reduce-scatter.23.cloned.1.call-done
  94.3 1.6 copy.25
  95.9 0.0 reduce-scatter.31.cloned.1.call-update
  95.9 0.0 reduce-scatter.29.cloned.1.call-start
  96.0 39.7 %reduce-scatter.21.cloned.1.call-done = bf16[64,512]{1,0:T(8,128)(2,1)} async-done(((bf16[512,512]{1,0:T(8,128)(2,1)}), bf16[64,512]{1,0:T(8,128)(2,1)}) %reduce-scatter.21.cloned.1.call-update) | async-done | bytes 65552 | tf_op jit(solution)/shard_map/reduce_scatter | solution.py:249
  135.7 1.6 copy.23
  137.3 0.0 reduce-scatter.29.cloned.1.call-update
  137.3 0.0 reduce-scatter.27.cloned.1.call-start
  137.4 47.6 %reduce-scatter.19.cloned.1.call-done = bf16[64,1536]{1,0:T(8,128)(2,1)} async-done(((bf16[512,1536]{1,0:T(8,128)(2,1)}), bf16[64,1536]{1,0:T(8,128)(2,1)}) %reduce-scatter.19.cloned.1.call-update) | async-done | bytes 196624 | tf_op jit(solution)/shard_map/reduce_scatter | solution.py:249
  185.0 1.9 copy.21
  186.8 0.0 reduce-scatter.27.cloned.1.call-update
  186.9 0.0 reduce-scatter.25.cloned.1.call-start
  186.9 46.5 %reduce-scatter.17.cloned.1.call-done = bf16[64,1536]{1,0:T(8,128)(2,1)} async-done(((bf16[512,1536]{1,0:T(8,128)(2,1)}), bf16[64,1536]{1,0:T(8,128)(2,1)}) %reduce-scatter.17.cloned.1.call-update) | async-done | bytes 196624 | tf_op jit(solution)/shard_map/reduce_scatter | solution.py:249
  233.4 1.9 copy.19
  235.3 0.0 reduce-scatter.25.cloned.1.call-update
  235.3 111.0 %reduce-scatter.31.cloned.1.call-done = bf16[16,64]{1,0:T(8,128)(2,1)} async-done(((bf16[512,64]{1,0:T(8,128)(2,1)}), bf16[16,64]{1,0:T(8,128)(2,1)}) %reduce-scatter.31.cloned.1.call-update) | async-done | bytes 2064
  346.3 111.5 %reduce-scatter.29.cloned.1.call-done = bf16[16,64]{1,0:T(8,128)(2,1)} async-done(((bf16[512,64]{1,0:T(8,128)(2,1)}), bf16[16,64]{1,0:T(8,128)(2,1)}) %reduce-scatter.29.cloned.1.call-update) | async-done | bytes 2064
  457.8 1.3 maximum_convert_fusion.1
  459.1 112.0 %reduce-scatter.27.cloned.1.call-done = bf16[48,64]{1,0:T(8,128)(2,1)} async-done(((bf16[1536,64]{1,0:T(8,128)(2,1)}), bf16[48,64]{1,0:T(8,128)(2,1)}) %reduce-scatter.27.cloned.1.call-update) | async-done | bytes 6160
  571.1 0.8 copy.22
  571.9 112.3 %reduce-scatter.25.cloned.1.call-done = bf16[48,64]{1,0:T(8,128)(2,1)} async-done(((bf16[1536,64]{1,0:T(8,128)(2,1)}), bf16[48,64]{1,0:T(8,128)(2,1)}) %reduce-scatter.25.cloned.1.call-update) | async-done | bytes 6160
  684.3 0.8 copy.20
  685.1 0.7 copy.18
  (24 shorter events, 0.3 us)
Async XLA Ops:
  7.2 87.2 %reduce-scatter.23.cloned.1.call-start = ((), (), s32[]{:S(2)}) async-start(), calls=%async_computation.11 | async-start | bytes 589824 | tf_op jit(solution)/shard_map/reduce_scatter | solution.py:249
  8.2 26.8 %collective-permute-start.5 = (bf16[36,512]{1,0:T(8,128)(2,1)S(1)}, bf16[36,512]{1,0:T(8,128)(2,1)S(1)}, u32[]{:S(2)}, u32[]{:S(2)}) collective-permute-start(bf16[36,512]{1,0:T(8,128)(2,1)S(1)} %reshape.28), channel_id=1, source_target_pairs={{0,255},{1,224},{2,225},{3,226},{4,227},{5,228},{6,229},{7,230},{8... | collective-permute-start | bytes 110600 | tf_op jit(solution)/shard_map/ppermute | solution.py:228
  16.1 19.3 %collective-permute-start.4 = (bf16[36,512]{1,0:T(8,128)(2,1)S(1)}, bf16[36,512]{1,0:T(8,128)(2,1)S(1)}, u32[]{:S(2)}, u32[]{:S(2)}) collective-permute-start(bf16[36,512]{1,0:T(8,128)(2,1)S(1)} %reshape.27), channel_id=1, source_target_pairs={{0,31},{1,0},{2,1},{3,2},{4,3},{5,4},{6,5},{7,6},{8,7},{9,8},{10,9... | collective-permute-start | bytes 110600 | tf_op jit(solution)/shard_map/ppermute | solution.py:228
  17.9 4.3 copy-start.7
  20.0 15.4 %collective-permute-start.3 = (bf16[288,512]{1,0:T(8,128)(2,1)}, bf16[288,512]{1,0:T(8,128)(2,1)}, u32[]{:S(2)}, u32[]{:S(2)}) collective-permute-start(bf16[288,512]{1,0:T(8,128)(2,1)} %bitcast.12), channel_id=1, source_target_pairs={{0,224},{1,225},{2,226},{3,227},{4,228},{5,229},{6,230},{7,231},{8... | collective-permute-start | bytes 884744 | tf_op jit(solution)/shard_map/ppermute | solution.py:228
  22.2 1.4 copy-start.2
  22.2 1.7 copy-start.3
  22.2 2.1 copy-start.6
  23.5 7.2 %copy-start = (bf16[512,1536]{1,0:T(8,128)(2,1)}, bf16[512,1536]{1,0:T(8,128)(2,1)S(1)}, u32[]{:S(2)}) copy-start(bf16[512,1536]{1,0:T(8,128)(2,1)S(1)} %get-tuple-element.29.w_qkv.refs_2_) | copy-start | bytes 4718596
  30.7 4.4 copy-start.9
  30.7 4.7 copy-start.8
  30.7 5.8 collective-permute-start.1
  31.2 11.2 %collective-permute-start = (bf16[288,512]{1,0:T(8,128)(2,1)S(1)}, bf16[288,512]{1,0:T(8,128)(2,1)S(1)}, u32[]{:S(2)}, u32[]{:S(2)}) collective-permute-start(bf16[288,512]{1,0:T(8,128)(2,1)S(1)} %get-tuple-element.37), channel_id=1, source_target_pairs={{0,224},{1,225},{2,226},{3,227},{4,228},{5,229},{6,230},{7,231},{8... | collective-permute-start | bytes 884744 | tf_op jit(solution)/shard_map/ppermute | solution.py:228
  35.1 5.7 collective-permute-start.2
  35.4 7.0 %copy-start.1 = (bf16[576,648]{1,0:T(8,128)(2,1)S(1)}, bf16[576,648]{1,0:T(8,128)(2,1)}, u32[]{:S(2)}) copy-start(bf16[576,648]{1,0:T(8,128)(2,1)} %constant.24.clone.refs_4_.refs_5_.refs_6_) | copy-start | bytes 2239492
  35.4 7.0 %copy-start.4 = (bf16[512,512]{1,0:T(8,128)(2,1)S(1)}, bf16[512,512]{1,0:T(8,128)(2,1)}, u32[]{:S(2)}) copy-start(bf16[512,512]{1,0:T(8,128)(2,1)} %get-tuple-element.30.refs_3_) | copy-start | bytes 1572868
  58.5 77.2 %reduce-scatter.21.cloned.1.call-start = ((), (), s32[]{:S(2)}) async-start(), calls=%async_computation.10 | async-start | bytes 589824 | tf_op jit(solution)/shard_map/reduce_scatter | solution.py:249
  58.5 11.5 %copy-start.5 = (bf16[576,648]{1,0:T(8,128)(2,1)S(1)}, bf16[576,648]{1,0:T(8,128)(2,1)}, u32[]{:S(2)}) copy-start(bf16[576,648]{1,0:T(8,128)(2,1)} %constant.25.clone.refs_5_) | copy-start | bytes 2239492
  58.6 11.4 %collective-permute-start.6 = (bf16[288,512]{1,0:T(8,128)(2,1)S(1)}, bf16[288,512]{1,0:T(8,128)(2,1)S(1)}, u32[]{:S(2)}, u32[]{:S(2)}) collective-permute-start(bf16[288,512]{1,0:T(8,128)(2,1)S(1)} %get-tuple-element.33), channel_id=1, source_target_pairs={{0,32},{1,33},{2,34},{3,35},{4,36},{5,37},{6,38},{7,39},{8,40},{9,... | collective-permute-start | bytes 884744 | tf_op jit(solution)/shard_map/ppermute | solution.py:228
  60.2 7.1 %collective-permute-start.7 = (bf16[36,512]{1,0:T(8,128)(2,1)S(1)}, bf16[36,512]{1,0:T(8,128)(2,1)S(1)}, u32[]{:S(2)}, u32[]{:S(2)}) collective-permute-start(bf16[36,512]{1,0:T(8,128)(2,1)S(1)} %get-tuple-element.34), channel_id=1, source_target_pairs={{0,1},{1,2},{2,3},{3,4},{4,5},{5,6},{6,7},{7,8},{8,9},{9,10},{10,1... | collective-permute-start | bytes 110600 | tf_op jit(solution)/shard_map/ppermute | solution.py:228
  60.2 8.8 %collective-permute-start.8 = (bf16[36,512]{1,0:T(8,128)(2,1)S(1)}, bf16[36,512]{1,0:T(8,128)(2,1)S(1)}, u32[]{:S(2)}, u32[]{:S(2)}) collective-permute-start(bf16[36,512]{1,0:T(8,128)(2,1)S(1)} %get-tuple-element.35), channel_id=1, source_target_pairs={{0,33},{1,34},{2,35},{3,36},{4,37},{5,38},{6,39},{7,40},{8,41},{9,... | collective-permute-start | bytes 110600 | tf_op jit(solution)/shard_map/ppermute | solution.py:228
  86.1 98.9 %reduce-scatter.19.cloned.1.call-start = ((), (), s32[]{:S(2)}) async-start(), calls=%async_computation.9 | async-start | bytes 1769472 | tf_op jit(solution)/shard_map/reduce_scatter | solution.py:249
  86.8 146.6 %reduce-scatter.17.cloned.1.call-start = ((), (), s32[]{:S(2)}) async-start(), calls=%async_computation.8 | async-start | bytes 1769472 | tf_op jit(solution)/shard_map/reduce_scatter | solution.py:249
  87.4 258.9 %reduce-scatter.31.cloned.1.call-start = ((), (), s32[]{:S(2)}) async-start(), calls=%async_computation.15 | async-start | bytes 135168
  95.9 361.9 %reduce-scatter.29.cloned.1.call-start = ((), (), s32[]{:S(2)}) async-start(), calls=%async_computation.14 | async-start | bytes 135168
  137.3 433.8 %reduce-scatter.27.cloned.1.call-start = ((), (), s32[]{:S(2)}) async-start(), calls=%async_computation.13 | async-start | bytes 405504
  186.9 497.4 %reduce-scatter.25.cloned.1.call-start = ((), (), s32[]{:S(2)}) async-start(), calls=%async_computation.12 | async-start | bytes 405504
Sparse Core Ops, SparseCore 0:
  58.6 35.6 reduce-scatter.22
  97.0 38.6 reduce-scatter.20
  138.3 46.6 reduce-scatter.18
  187.4 45.9 reduce-scatter.16
  237.1 109.1 reduce-scatter.30
  350.5 107.2 reduce-scatter.28
  461.8 109.2 reduce-scatter.26
  575.2 109.0 reduce-scatter.24

commit v2 on v1

v2 whole, which is shorter than its diff:
```python
import functools

import jax
import jax.numpy as jnp
import numpy as np
from jax import lax
from jax.experimental import pallas as pl
from jax.experimental.pallas import tpu as pltpu
from jax.sharding import PartitionSpec as P

D = 512
HEADS = 8
HEAD_DIM = 64
LEVELS = 2
WIN_LAT = 12
WIN_LON = 6
HALF_LAT = 6
HALF_LON = 3
ROWS = 12
COLS = 24
TOKENS = LEVELS * ROWS * COLS
WINDOW = LEVELS * WIN_LAT * WIN_LON
WINDOWS = TOKENS // WINDOW
HALF = TOKENS // 2
QUAD = 4 * HEAD_DIM
LEVEL = ROWS * COLS
SEGMENT = WIN_LAT * WIN_LON
WIDE = 128
STRIP = 32
PIECES = 2 * WIDE + 2 * STRIP
EPSILON = 1e-05
MASKED = -1000000000.0
SCALE = HEAD_DIM ** (-0.5)
LARGE = 58
SMALL = 6
PEAK_FLOPS = 1_150_000_000
PEAK_BYTES = 3_690_000
F32 = jnp.float32
BF16 = jnp.bfloat16


def window_order(row, col):
    return (col // WIN_LON) * SEGMENT + row * WIN_LON + col % WIN_LON


def field_order(row, col):
    return row * COLS + col


def piece_order(row, col):
    upper = int(row < HALF_LAT)
    at = row % HALF_LAT
    if col < HALF_LON:
        return 2 * WIDE + STRIP * upper + at * HALF_LON + col
    return WIDE * upper + at * (COLS - HALF_LON) + col - HALF_LON


def half_order(row, col):
    if col >= COLS:
        return LEVEL + piece_order(row, col - COLS) - 2 * WIDE
    return LEVEL // 2 * int(row < HALF_LAT) + (row % HALF_LAT) * COLS + col


def selection(shape, pairs):
    out = np.zeros(shape, np.float32)
    for row, column in pairs:
        out[row, column] = 1
    return jnp.asarray(out, BF16)


CELLS = list(np.ndindex(ROWS, COLS))
PLAIN = [(window_order(*cell), field_order(*cell)) for cell in CELLS]
JOIN = [(window_order(*cell), piece_order(*cell)) for cell in CELLS]
STRIPS = [(piece_order(*cell) - 2 * WIDE, field_order(*cell)) for cell in CELLS if cell[1] < HALF_LON]
SHIFTED = [((r + HALF_LAT) % ROWS, c + HALF_LON) for r, c in CELLS]
SHIFT = [(window_order(*cell), piece_order(r, c % COLS)) for cell, (r, c) in zip(CELLS, SHIFTED)]
SHIFT_HALF = [(window_order(*cell), half_order(r, c)) for cell, (r, c) in zip(CELLS, SHIFTED)]


def flipped(pairs):
    return [(column, row) for row, column in pairs]


class Fetched:
    def __init__(self, source, target, sem):
        self.copy, self.target, self.waiting = pltpu.make_async_copy(source, target, sem), target, True
        self.copy.start()

    def __getitem__(self, index):
        if self.waiting:
            self.copy.wait()
            self.waiting = False
        return self.target[index]


class Stored:
    def __init__(self, source, target, sem):
        self.copy, self.source = pltpu.make_async_copy(source, target, sem), source

    def __getitem__(self, index):
        return self.source[index]

    def __setitem__(self, index, value):
        self.source[index] = value

    def flush(self):
        self.copy.start()


def dot(a, b):
    return lax.dot_general(a, b, (((1,), (0,)), ((), ())), preferred_element_type=F32)


def dot_nt(a, b):
    return lax.dot_general(a, b, (((1,), (1,)), ((), ())), preferred_element_type=F32)


def dot_tn(a, b):
    return lax.dot_general(a, b, (((0,), (0,)), ((), ())), preferred_element_type=F32)


def gathered(matrix, levels):
    parts = [dot(matrix[...], level) for level in levels]
    segments = [part[w * SEGMENT : (w + 1) * SEGMENT] for w in range(WINDOWS) for part in parts]
    return jnp.concatenate(segments, axis=0)


def scattered(matrix, values):
    parts = []
    for level in range(LEVELS):
        starts = [w * WINDOW + level * SEGMENT for w in range(WINDOWS)]
        own = jnp.concatenate([values[start : start + SEGMENT] for start in starts], axis=0)
        parts.append(dot(matrix[...], own.astype(BF16)).astype(BF16))
    return parts


def pieces_of(refs, strip_at=0):
    out = []
    for level in range(LEVELS):
        strip_start = strip_at + level * STRIP
        spans = [slice(level * WIDE, (level + 1) * WIDE)] * 2 + [slice(strip_start, strip_start + STRIP)] * 2
        out.append(jnp.concatenate([ref[span] for ref, span in zip(refs, spans)], axis=0))
    return out


def put_pieces(parts, refs):
    for level, part in enumerate(parts):
        at = 0
        for ref, size in zip(refs, (WIDE, WIDE, STRIP, STRIP)):
            ref[level * size : (level + 1) * size] = part[at : at + size]
            at += size


def layer_norm(values):
    centred = values - jnp.mean(values, axis=-1, keepdims=True)
    inverse = lax.rsqrt(jnp.mean(centred * centred, axis=-1, keepdims=True) + EPSILON)
    return centred * inverse, inverse


def stacked(part, scale):
    lane = lax.broadcasted_iota(jnp.int32, (1, QUAD), 1) // HEAD_DIM
    wide = [part * jnp.where(lane == h, scale, 0.0).astype(BF16) for h in range(4)]
    return jnp.concatenate(wide, axis=0)


def unstacked(product):
    lane = lax.broadcasted_iota(jnp.int32, (WINDOW, QUAD), 1) // HEAD_DIM
    out = product[:WINDOW]
    for h in range(1, 4):
        out = jnp.where(lane == h, product[h * WINDOW : (h + 1) * WINDOW], out)
    return out


def soft(keys_stacked, queries, bias):
    scores = dot_nt(keys_stacked, queries).reshape(4, WINDOW, WINDOW)
    if bias is not None:
        scores = scores + bias[None]
    top = jnp.max(scores, axis=1, keepdims=True)
    raised = jnp.exp(scores - top)
    return raised * (1.0 / jnp.sum(raised, axis=1, keepdims=True))


def places(w, quad):
    span = slice(w * WINDOW, (w + 1) * WINDOW)
    return span, [slice(n * D + quad * QUAD, n * D + (quad + 1) * QUAD) for n in range(3)]


def forward_kernel(
    tokens, cotangent, w_qkv, w_proj, plain, cut, strips,
    keep, tall, side, corner, values_out, normed_out, packed, probs_out, mixed,
):
    values = gathered(plain, [tokens[:LEVEL], tokens[LEVEL:]])
    values_out[...] = values.astype(BF16)
    values_out.flush()
    normed = layer_norm(values)[0].astype(BF16)
    normed_out[...] = normed
    normed_out.flush()
    packed[...] = dot(normed, w_qkv[...]).astype(BF16)
    packed.flush()
    for w in range(WINDOWS):
        for quad in range(2):
            span, at = places(w, quad)
            queries, keys, vals = [packed[span, at[n]] for n in range(3)]
            probs = soft(stacked(keys, SCALE), queries, None).astype(BF16).reshape(4 * WINDOW, WINDOW)
            probs_out[2 * w + quad] = probs
            mixed[span, at[0]] = dot_tn(probs, stacked(vals, 1.0)).astype(BF16)
    probs_out.flush()
    mixed.flush()
    first = values + dot(mixed[...], w_proj[...])
    put_pieces(scattered(cut, first), (keep, tall, side, corner))
    for level in range(LEVELS):
        part = dot(strips[...], cotangent[level * LEVEL : (level + 1) * LEVEL]).astype(BF16)
        at = slice((LEVELS + level) * STRIP, (LEVELS + level + 1) * STRIP)
        side[at] = part[:STRIP]
        corner[at] = part[STRIP:]


def attention_backward(packed, probs, probs_low, d_mixed, d_packed, span, at, keys_stacked, vals_stacked):
    d_probs = dot_nt(vals_stacked, d_mixed).reshape(4, WINDOW, WINDOW)
    inner = jnp.sum(probs * d_probs, axis=1, keepdims=True)
    d_scores = (probs * (d_probs - inner)).astype(BF16).reshape(4 * WINDOW, WINDOW)
    d_packed[span, at[0]] = dot_tn(d_scores, keys_stacked).astype(BF16)
    d_packed[span, at[1]] = (unstacked(dot(d_scores, packed[span, at[0]])) * SCALE).astype(BF16)
    d_packed[span, at[2]] = unstacked(dot(probs_low, d_mixed)).astype(BF16)


def input_gradient(values, gradient, d_packed, w_qkv):
    standard, inverse = layer_norm(values)
    d_normed = dot_nt(d_packed, w_qkv)
    d_input = inverse * (
        d_normed
        - jnp.mean(d_normed, axis=-1, keepdims=True)
        - standard * jnp.mean(d_normed * standard, axis=-1, keepdims=True)
    )
    return gradient.astype(F32) + d_input


def weight_gradients(core, normed, d_packed, mixed, gradient, grads, kept, sent):
    grads[:, :48] = dot_tn(d_packed, normed).astype(BF16).reshape(32, 48, D)
    grads[:, 48:] = dot_tn(gradient, mixed).astype(BF16).reshape(32, 16, D)
    for j in range(16):
        kept[j] = grads[2 * j + core[0]]
        sent[j] = grads[2 * j + 1 - core[0]]


def shifted_kernel(
    core, keep, tall, side, corner, cotangent, tall_g, w_qkv, w_proj, gather, gather_g, scatter, bias,
    keep_out, tall_out, side_out, corner_out, kept, sent,
    packed, d_mixed_all, mixed, d_packed, grads,
):
    sources = []
    for level in range(LEVELS):
        own = cotangent[level * LEVEL + LEVEL // 2 : (level + 1) * LEVEL]
        beside = [ref[(LEVELS + level) * STRIP : (LEVELS + level + 1) * STRIP] for ref in (side, corner)]
        sources.append(
            jnp.concatenate([own, tall_g[level * (LEVEL // 2) : (level + 1) * (LEVEL // 2)], *beside], axis=0)
        )
    gradient = gathered(gather_g, sources).astype(BF16)
    d_mixed_all[...] = dot_nt(gradient, w_proj[...]).astype(BF16)
    values = gathered(gather, pieces_of((keep, tall, side, corner)))
    normed = layer_norm(values)[0].astype(BF16)
    packed[...] = dot(normed, w_qkv[...]).astype(BF16)
    for w in range(WINDOWS):
        for quad in range(2):
            span, at = places(w, quad)
            queries, keys, vals = [packed[span, at[n]] for n in range(3)]
            keys_stacked, vals_stacked = stacked(keys, SCALE), stacked(vals, 1.0)
            probs = soft(keys_stacked, queries, bias[...])
            probs_low = probs.astype(BF16).reshape(4 * WINDOW, WINDOW)
            mixed[span, at[0]] = dot_tn(probs_low, vals_stacked).astype(BF16)
            attention_backward(
                packed, probs, probs_low, d_mixed_all[span, at[0]], d_packed, span, at, keys_stacked, vals_stacked
            )
    weight_gradients(core, normed, d_packed[...], mixed[...], gradient, grads, kept, sent)
    kept.flush()
    sent.flush()
    result = input_gradient(values, gradient, d_packed[...], w_qkv[...])
    put_pieces(scattered(scatter, result), (keep_out, tall_out, side_out, corner_out))


def plain_kernel(
    core, keep, tall, side, corner, w_proj, join, packed, probs_in, mixed, normed, values, w_qkv, unplain,
    d_tokens, kept, sent,
    d_mixed_all, grads, d_packed,
):
    gradient = gathered(join, pieces_of((keep, tall, side, corner))).astype(BF16)
    d_mixed_all[...] = dot_nt(gradient, w_proj[...]).astype(BF16)
    for w in range(WINDOWS):
        for quad in range(2):
            span, at = places(w, quad)
            keys_stacked, vals_stacked = stacked(packed[span, at[1]], SCALE), stacked(packed[span, at[2]], 1.0)
            probs_low = probs_in[2 * w + quad]
            probs = probs_low.astype(F32).reshape(4, WINDOW, WINDOW)
            attention_backward(
                packed, probs, probs_low, d_mixed_all[span, at[0]], d_packed, span, at, keys_stacked, vals_stacked
            )
    weight_gradients(core, normed[...], d_packed[...], mixed[...], gradient, grads, kept, sent)
    kept.flush()
    sent.flush()
    result = input_gradient(values[...].astype(F32), gradient, d_packed[...], w_qkv[...])
    for level, part in enumerate(scattered(unplain, result)):
        d_tokens[level * LEVEL : (level + 1) * LEVEL] = part


def swapped_halves(top, bottom):
    left = lax.broadcasted_iota(jnp.int32, top.shape, 1) < top.shape[1] // 2
    turned = [pltpu.roll(x, top.shape[1] // 2, 1) for x in (top, bottom)]
    return jnp.where(left, top, turned[1]), jnp.where(left, turned[0], bottom)


def core_sums(kept, received):
    half = kept.shape[0] // 2
    for pair in range(4):
        at = slice(pair * 128, (pair + 1) * 128)
        total = kept[:, at].astype(F32) + received[:, at].astype(F32)
        for odd, part in enumerate(swapped_halves(total[:half], total[half:])):
            yield 2 * pair + odd, part.astype(BF16)


def core_sum_kernel(kept, received, out):
    for lat, part in core_sums(kept, received):
        out[lat] = part


def core_cut_kernel(place, kept, received, *refs):
    outs, held = refs[:-1], refs[-1]
    for lat, part in core_sums(kept, received):
        held[lat // 2, lat % 2] = part
    for step, out in enumerate(outs):
        out[...] = held[lax.rem(place[0] + step, 4)]


def far_sum_kernel(place, one, two, three, four, kept, sent):
    total = one[...].astype(F32) + two[...].astype(F32) + three[...].astype(F32) + four[...].astype(F32)
    first = place[0] == 0
    kept[...] = jnp.where(first, total[0], total[1]).astype(BF16)
    sent[...] = jnp.where(first, total[1], total[0]).astype(BF16)


def lat_sum_kernel(parts, kept, received, out):
    total = parts[0].astype(F32)
    for a in range(1, 8):
        total = total + parts[a].astype(F32)
    other = kept[...].astype(F32) + received[...].astype(F32)
    for block, held in enumerate((total, other)):
        for j in range(8):
            low, high = swapped_halves(held[64 * j : 64 * j + 32], held[64 * j + 32 : 64 * j + 64])
            out[j, block] = low.astype(BF16)
            out[j + 8, block] = high.astype(BF16)


def lon_sum_kernel(parts, grad_qkv, grad_proj):
    for block in range(2):
        total = parts[0, block].astype(F32)
        for j in range(1, 16):
            total = total + parts[j, block].astype(F32)
        whole = jnp.concatenate([total, pltpu.roll(total, 64, 1)], axis=0)
        grad_qkv[block] = whole[:48, :64]
        grad_proj[block] = whole[48:, :64]


def shape(*dims, kind=BF16):
    return jax.ShapeDtypeStruct(dims, kind)


def call(kernel, name, outs, *operands, scratch=(), scalar=False, fetch=None, store=(), limit=SMALL, micros=1):
    fetch = fetch or {}
    several = outs if isinstance(outs, tuple) else (outs,)
    cut = np.cumsum([0, len(operands), len(several), len(scratch), len(fetch), len(store)])

    def body(*refs):
        ins, results, own, landing, leaving = [list(refs[a:b]) for a, b in zip(cut[:-1], cut[1:])]
        for at, (n, index) in enumerate(fetch.items()):
            ins[n] = Fetched(ins[n] if index is None else ins[n].at[index], landing[at], refs[-2].at[at])
        for at, n in enumerate(store):
            results[n] = Stored(leaving[at], results[n], refs[-1].at[at])
        kernel(*ins, *results, *own)
        for n in store:
            results[n].copy.wait()

    held = [pltpu.VMEM(dims, BF16) for dims in scratch]
    for n, index in fetch.items():
        held.append(pltpu.VMEM(operands[n].shape if index is None else operands[n].shape[1:], BF16))
    held += [pltpu.VMEM(several[n].shape, BF16) for n in store]
    if fetch or store:
        held += [pltpu.SemaphoreType.DMA((max(1, len(group)),)) for group in (fetch, store)]
    kinds = [pltpu.HBM if n in fetch else pltpu.VMEM for n in range(len(operands))]
    if scalar:
        kinds[0] = pltpu.SMEM
    specs = tuple(pl.BlockSpec(memory_space=pltpu.HBM if n in store else pltpu.VMEM) for n in range(len(several)))
    return pl.pallas_call(
        body,
        out_shape=outs,
        in_specs=[pl.BlockSpec(memory_space=kind) for kind in kinds],
        out_specs=specs if isinstance(outs, tuple) else specs[0],
        scratch_shapes=held,
        compiler_params=pltpu.CompilerParams(vmem_limit_bytes=limit * 1024 * 1024),
        cost_estimate=pl.CostEstimate(
            flops=micros * PEAK_FLOPS, bytes_accessed=micros * PEAK_BYTES, transcendentals=0
        ),
        name=name,
    )(*operands)


def moved(piece, lat, lon):
    n_lat, n_lon = lax.axis_size("lat"), lax.axis_size("lon")
    if lon == 0:
        return lax.ppermute(piece, "lat", [(i, (i + lat) % n_lat) for i in range(n_lat)])
    if lat == 0:
        return lax.ppermute(piece, "lon", [(i, (i + lon) % n_lon) for i in range(n_lon)])
    route = [
        (a * n_lon + b, (a + lat) % n_lat * n_lon + (b + lon) % n_lon)
        for a in range(n_lat)
        for b in range(n_lon)
    ]
    return lax.ppermute(piece, ("lat", "lon"), route)


def exchanged(tall, side, corner, step):
    return moved(tall, step, 0), moved(side, 0, step), moved(corner, step, step)


def core_swapped(sent):
    return lax.ppermute(sent, "lon", [(i, i ^ 1) for i in range(lax.axis_size("lon"))]).reshape(1024, D)


def core_reduced(kept, sent):
    return call(core_sum_kernel, "core_sum", shape(8, 512, 128), kept.reshape(1024, D), core_swapped(sent), limit=12)


def core_cut(kept, sent):
    place = (lax.axis_index("lat") // 2).astype(jnp.int32).reshape(1)
    return call(
        core_cut_kernel, "core_cut", (shape(2, 512, 128),) * 4, place, kept.reshape(1024, D), core_swapped(sent),
        scratch=[(4, 2, 512, 128)], scalar=True, limit=12,
    )


def far_reduced(parts):
    n = lax.axis_size("lat")
    arrived = [parts[0]]
    for step in (2, 3, 1):
        arrived.append(lax.ppermute(parts[step], "lat", [(i, (i + 2 * step) % n) for i in range(n)]))
    place = (lax.axis_index("lat") % 2).astype(jnp.int32).reshape(1)
    kept, sent = call(far_sum_kernel, "far_sum", (shape(512, 128),) * 2, place, *arrived, scalar=True)
    return kept, sent


def reduced(chunks_one, parts_two):
    kept, sent = parts_two
    received = lax.ppermute(sent, "lat", [(i, i ^ 1) for i in range(lax.axis_size("lat"))])
    arrived = lax.all_to_all(chunks_one, "lat", 0, 0, tiled=True)
    both = call(lat_sum_kernel, "lat_sum", shape(16, 2, 32, 128), arrived, kept, received)
    groups = [[2 * j + core for j in range(16)] for core in range(2)]
    arrived = lax.all_to_all(both, "lon", 0, 0, tiled=True, axis_index_groups=groups)
    grads = call(lon_sum_kernel, "lon_sum", (shape(2, 48, 64, kind=F32), shape(2, 16, 64, kind=F32)), arrived)
    return [grad.transpose(0, 2, 1) for grad in grads]


def body(tokens, cotangent, qkv_weights, proj_weights):
    plain, unplain = selection((LEVEL, LEVEL), PLAIN), selection((LEVEL, LEVEL), flipped(PLAIN))
    join, cut = selection((LEVEL, PIECES), JOIN), selection((PIECES, LEVEL), flipped(JOIN))
    shift, unshift = selection((LEVEL, PIECES), SHIFT), selection((PIECES, LEVEL), flipped(SHIFT))
    shift_half, strips = selection((LEVEL, LEVEL + 2 * STRIP), SHIFT_HALF), selection((2 * STRIP, LEVEL), STRIPS)
    core = (lax.axis_index("lon") % 2).astype(jnp.int32).reshape(1)
    last_lat = lax.axis_index("lat") == lax.axis_size("lat") - 1
    label = (np.arange(WINDOW) // WIN_LON % WIN_LAT >= HALF_LAT).astype(np.int32)
    bias = jnp.where(last_lat & (label[:, None] != label[None, :]), MASKED, 0.0).astype(F32)
    field, flat = shape(TOKENS, D), tokens.reshape(TOKENS, D)
    wide, strip, pair = [shape(LEVELS * rows, D) for rows in (WIDE, STRIP, 2 * STRIP)]
    packed_field = shape(TOKENS, 3 * D)
    half = shape(16, 64, D)

    tall_g = moved(cotangent[:, :HALF_LAT].reshape(HALF, D), -1, 0)
    flat_g = cotangent.reshape(TOKENS, D)
    keep, tall, side, corner, values, normed, packed, probs, mixed = call(
        forward_kernel,
        "forward",
        (wide, wide, pair, pair, field, field, packed_field, shape(2 * WINDOWS, 4 * WINDOW, WINDOW), field),
        flat, flat_g, qkv_weights, proj_weights, plain, cut, strips,
        fetch={4: None, 0: None, 2: 0, 3: 0, 5: None, 6: None, 1: None},
        store=(4, 5, 6, 7, 8),
        limit=LARGE,
        micros=9,
    )
    tall, side, corner = exchanged(tall, side, corner, -1)
    keep, tall, side, corner, kept_two, sent_two = call(
        shifted_kernel,
        "backward_shifted",
        (wide, wide, strip, strip, half, half),
        core, keep, tall, side, corner, flat_g, tall_g, qkv_weights, proj_weights, shift, shift_half, unshift, bias,
        scratch=[(TOKENS, 3 * D), (TOKENS, D), (TOKENS, D), (TOKENS, 3 * D), (32, 64, D)],
        scalar=True,
        fetch={5: None, 10: None, 8: 1, 9: None, 7: 1, 11: None},
        store=(4, 5),
        limit=LARGE,
        micros=18,
    )
    tall, side, corner = exchanged(tall, side, corner, 1)
    parts_two = far_reduced(core_cut(kept_two, sent_two))
    d_tokens, kept_one, sent_one = call(
        plain_kernel,
        "backward_plain",
        (field, half, half),
        core, keep, tall, side, corner, proj_weights, join, packed, probs, mixed, normed, values, qkv_weights, unplain,
        scratch=[(TOKENS, D), (32, 64, D), (TOKENS, 3 * D)],
        scalar=True,
        fetch={6: None, 5: 0, 7: None, 8: None, 10: None, 9: None, 12: 0, 11: None, 13: None},
        store=(1, 2),
        limit=LARGE,
        micros=13,
    )
    sent_one, parts_two = lax.optimization_barrier((sent_one, parts_two))
    grad_qkv, grad_proj = reduced(core_reduced(kept_one, sent_one), parts_two)
    return d_tokens.reshape(tokens.shape), grad_qkv, grad_proj


def solution(mesh):
    return jax.shard_map(
        body,
        mesh=mesh,
        in_specs=(P(None, "lat", "lon", None), P(None, "lat", "lon", None), P(), P()),
        out_specs=(P(None, "lat", "lon", None), P(None, "lat", "lon"), P(None, "lat", "lon")),
        check_vma=False,
    )
```

time: 693 us -> 123 us (0.18)
  waiting for transfers between devices: 604 us -> 20.8 us
  blocking collectives: 0 us -> 22.2 us
  between operations: 14.3 us -> 0.78 us
  starting transfers between devices: 16.3 us -> 29 us
  local copies, waits for them, and re-layouts: 16.6 us -> 4.77 us
    unnamed x12 -> x0, waiting for transfers between devices: 448 us -> none
    reduce_scatter x4 -> x0, waiting for transfers between devices: 141 us -> none  [reduce_grads(): lax.psum_scatter(x, 'lat', scatter_dimension=0, tiled=True)]
    all_to_all x0 -> x1, blocking collectives: none -> 22.2 us  [reduced(): lax.all_to_all(both, 'lon', 0, 0, tiled=True, axis_index_groups=groups)]
    ppermute x9 -> x13, starting transfers between devices: 16 us -> 23.4 us  [the longest x3 5.91 us: far_reduced(): lax.ppermute(parts[step], 'lat', [(i, (i + 2 * step) % n) for i in range(...]
    ppermute x9 -> x13, waiting for transfers between devices: 15.5 us -> 20.8 us  [the longest x1 15.2 us: reduced(): lax.ppermute(sent, 'lat', [(i, i ^ 1) for i in range(lax.axis_size('lat'))])]
    pallas_call x3 -> x8, Pallas kernels: 38.4 us -> 43.6 us  [call(): pl.pallas_call(body, out_shape=outs, in_specs=[pl.BlockSpec(memory_space=...]
  transfers between devices with their start and end apart: 17 -> 14, of which waited for: 13 -> 4; matrix products, arithmetic and copies ran while one was open for 2% -> 1% of each run, Pallas kernels for 3% -> 19%
where the time goes in v2:
time: 123 us; the launch traced here: 122 us
  Pallas kernels  43.6 us (35%)
  starting transfers between devices  29 us (24%)
  blocking collectives  22.2 us (18%)
  waiting for transfers between devices  20.8 us (17%)
  local copies, waits for them, and re-layouts  4.77 us (4%)
    pallas_call x8, Pallas kernels, call(): pl.pallas_call(body, out_shape=outs, in_specs=[pl.BlockSpec(memory_space=...  43.6 us
    all_to_all x1, blocking collectives, reduced(): lax.all_to_all(both, 'lon', 0, 0, tiled=True, axis_index_groups=groups)  22.2 us
    ppermute x1, waiting for transfers between devices, reduced(): lax.ppermute(sent, 'lat', [(i, i ^ 1) for i in range(lax.axis_size('lat'))])  15.2 us
    ppermute x3, starting transfers between devices, far_reduced(): lax.ppermute(parts[step], 'lat', [(i, (i + 2 * step) % n) for i in range(...  5.91 us
    ppermute x2, starting transfers between devices, moved(): lax.ppermute(piece, 'lon', [(i, (i + lon) % n_lon) for i in range(n_lon)])  5.74 us
    all_to_all x1, starting transfers between devices, reduced(): arrived = lax.all_to_all(chunks_one, 'lat', 0, 0, tiled=True)  5.67 us
    ppermute x2, starting transfers between devices, moved(): return lax.ppermute(piece, ('lat', 'lon'), route)  4.41 us
    ppermute x3, starting transfers between devices, moved(): lax.ppermute(piece, 'lat', [(i, (i + lat) % n_lat) for i in range(n_lat)])  4.26 us
  transfers between devices with their start and end apart: 14, of which 4 were waited for; matrix products, arithmetic and copies ran while one was open for 1% of the time, Pallas kernels for 19%

profile of v2, /device:TPU:2, one launch (start us, length us, event | category | flops | bytes accessed | tf_op | source)
XLA Modules:
  0.0 121.9 jit_solution(12832152134960802156)
XLA Ops:
  0.6 1.0 slice.3
  1.6 1.6 %collective-permute-start.3 = (bf16[288,512]{1,0:T(8,128)(2,1)S(1)}, bf16[288,512]{1,0:T(8,128)(2,1)S(1)}, u32[]{:S(2)}, u32[]{:S(2)}) collective-permute-start(bf16[288,512]{1,0:T(8,128)(2,1)S(1)} %bitcast.17), channel_id=1, source_target_pairs={{0,224},{32,0},{64,32},{96,64},{128,96},{160,128},{192,160},{224,1... | collective-permute-start | bytes 884744 | tf_op jit(solution)/shard_map/ppermute | solution.py:408
  3.2 0.0 copy-start.2
  3.2 9.0 %forward.1 = (bf16[256,512]{1,0:T(8,128)(2,1)}, bf16[256,512]{1,0:T(8,128)(2,1)}, bf16[128,512]{1,0:T(8,128)(2,1)}, bf16[128,512]{1,0:T(8,128)(2,1)}, bf16[576,5...) custom-call(bf16[576,512]{1,0:T(8,128)(2,1)} %bitcast.20, ...), custom_call_target="tpu_custom_call" | custom-call | flops 10350000128 | bytes 33210000 | tf_op jit(solution)/shard_map/forward/pallas_call | solution.py:391
  12.2 2.3 %collective-permute-start = (bf16[256,512]{1,0:T(8,128)(2,1)}, bf16[256,512]{1,0:T(8,128)(2,1)S(1)}, u32[]{:S(2)}, u32[]{:S(2)}) collective-permute-start(bf16[256,512]{1,0:T(8,128)(2,1)} %get-tuple-element.33), channel_id=1, source_target_pairs={{0,224},{32,0},{64,32},{96,64},{128,96},{160,128},{192,160},{224,1... | collective-permute-start | bytes 786440 | tf_op jit(solution)/shard_map/ppermute | solution.py:408
  14.5 5.6 %collective-permute-start.1 = (bf16[128,512]{1,0:T(8,128)(2,1)}, bf16[128,512]{1,0:T(8,128)(2,1)S(1)}, u32[]{:S(2)}, u32[]{:S(2)}) collective-permute-start(bf16[128,512]{1,0:T(8,128)(2,1)} %get-tuple-element.34), channel_id=1, source_target_pairs={{0,31},{1,0},{2,1},{3,2},{4,3},{5,4},{6,5},{7,6},{8,7},{9,8},{10,9... | collective-permute-start | bytes 393224 | tf_op jit(solution)/shard_map/ppermute | solution.py:410
  20.1 3.3 %collective-permute-start.2 = (bf16[128,512]{1,0:T(8,128)(2,1)}, bf16[128,512]{1,0:T(8,128)(2,1)S(1)}, u32[]{:S(2)}, u32[]{:S(2)}) collective-permute-start(bf16[128,512]{1,0:T(8,128)(2,1)} %get-tuple-element.35), channel_id=1, source_target_pairs={{0,255},{1,224},{2,225},{3,226},{4,227},{5,228},{6,229},{7,230},{8... | collective-permute-start | bytes 393224 | tf_op jit(solution)/shard_map/ppermute | solution.py:416
  23.4 0.0 copy-done.2
  23.4 0.7 and_select_fusion.refs_12_
  24.0 0.0 collective-permute-done.1.refs_3_
  24.0 0.0 copy-start.7
  24.1 2.1 %collective-permute-done.2.refs_4_ = bf16[128,512]{1,0:T(8,128)(2,1)S(1)} collective-permute-done((bf16[128,512]{1,0:T(8,128)(2,1)}, bf16[128,512]{1,0:T(8,128)(2,1)S(1)}, u32[]{:S(2)}, u32[]{:S(2)}) %collective-permute-start.2) | collective-permute-done | bytes 131104 | tf_op jit(solution)/shard_map/ppermute | solution.py:416
  26.2 0.0 copy-start.8
  26.2 0.0 collective-permute-done.refs_2_
  26.2 0.0 copy-start.6
  26.2 0.0 collective-permute-done.3.refs_6_
  26.2 0.0 copy-start.4
  26.2 0.0 copy-done.7
  26.2 0.6 copy-done.8
  26.9 0.1 copy-done.6
  27.0 0.1 copy-done.4
  27.0 18.4 %backward_shifted.1 = (bf16[256,512]{1,0:T(8,128)(2,1)}, bf16[256,512]{1,0:T(8,128)(2,1)}, bf16[64,512]{1,0:T(8,128)(2,1)}, bf16[64,512]{1,0:T(8,128)(2,1)}, bf1...) custom-call(s32[1]{0:T(128)} %bitcast.refs_0_, bf16[256,512]{1,0:T(8,128)(2,1)} %get-tuple-element.32.refs_1_, ...), custom_call_target="tpu_custom_call" | custom-call | flops 20700000256 | bytes 66420000 | tf_op jit(solution)/shard_map/backward_shifted/pallas_call | solution.py:391
  45.5 0.3 collective-permute-start.7
  45.8 0.4 collective-permute-start.4
  46.2 0.1 collective-permute-start.5
  46.3 1.2 collective-permute-start.6
  47.5 1.2 collective-permute-done.7
  48.7 0.0 copy-start
  48.7 1.2 %copy-done = bf16[16,64,512]{2,1,0:T(8,128)(2,1)S(1)} copy-done((bf16[16,64,512]{2,1,0:T(8,128)(2,1)S(1)}, bf16[16,64,512]{2,1,0:T(8,128)(2,1)}, u32[]{:S(2)}) %copy-start) | copy-done | bytes 1048600
  49.9 0.6 core_cut.1
  50.5 0.8 collective-permute-start.10
  51.3 2.6 %collective-permute-start.8 = (bf16[2,512,128]{2,1,0:T(8,128)(2,1)S(1)}, bf16[2,512,128]{2,1,0:T(8,128)(2,1)S(1)}, u32[]{:S(2)}, u32[]{:S(2)}) collective-permute-start(bf16[2,512,128]{2,1,0:T(8,128)(2,1)S(1)} %get-tuple-element.51), channel_id=1, source_target_pairs={{0,128},{32,160},{64,192},{96,224},{128,0},{160,32},{192,64},{224,... | collective-permute-start | bytes 786440 | tf_op jit(solution)/shard_map/ppermute | solution.py:443
  53.9 0.0 collective-permute-done.5.refs_3_
  53.9 0.0 copy-start.9
  53.9 2.5 %collective-permute-start.9 = (bf16[2,512,128]{2,1,0:T(8,128)(2,1)S(1)}, bf16[2,512,128]{2,1,0:T(8,128)(2,1)S(1)}, u32[]{:S(2)}, u32[]{:S(2)}) collective-permute-start(bf16[2,512,128]{2,1,0:T(8,128)(2,1)S(1)} %get-tuple-element.52), channel_id=1, source_target_pairs={{0,192},{32,224},{64,0},{96,32},{128,64},{160,96},{192,128},{224,1... | collective-permute-start | bytes 786440 | tf_op jit(solution)/shard_map/ppermute | solution.py:443
  56.4 0.0 collective-permute-done.6.refs_4_
  56.4 0.0 copy-start.10
  56.4 0.0 collective-permute-done.4.refs_2_
  56.4 0.0 copy-start.5
  56.4 0.0 copy-done.9
  56.4 0.6 copy-done.10
  57.0 0.1 copy-done.5
  57.1 13.1 %backward_plain.1 = (bf16[576,512]{1,0:T(8,128)(2,1)}, bf16[16,64,512]{2,1,0:T(8,128)(2,1)}, bf16[16,64,512]{2,1,0:T(8,128)(2,1)}) custom-call(s32[1]{0:T(128)} %bitcast.refs_0_, bf16[256,512]{1,0:T(8,128)(2,1)} %get-tuple-element.36.refs_1_, bf16[256,512]{1,0:T(8,128)(2,1)} %copy-done.5, bf16[64,512]{1,0:T(8,128)(2,1)} %copy-done.9, ...), custom_call_target="tpu_custom_call" | custom-call | flops 14949999616 | bytes 47970000 | tf_op jit(solution)/shard_map/backward_plain/pallas_call | solution.py:391
  70.2 0.0 copy-start.3
  70.2 0.0 copy-start.1
  70.2 0.0 collective-permute-done.10.refs_4_
  70.2 0.0 collective-permute-done.8.refs_2_
  70.3 0.0 collective-permute-done.9.refs_3_
  70.3 0.2 far_sum.1
  70.4 1.0 copy-done.3
  71.4 1.3 %collective-permute-start.11 = (bf16[16,64,512]{2,1,0:T(8,128)(2,1)S(1)}, bf16[16,64,512]{2,1,0:T(8,128)(2,1)S(1)}, u32[]{:S(2)}, u32[]{:S(2)}) collective-permute-start(bf16[16,64,512]{2,1,0:T(8,128)(2,1)S(1)} %copy-done.3), channel_id=1, source_target_pairs={{0,1},{1,0},{2,3},{3,2},{4,5},{5,4},{6,7},{7,6},{8,9},{9,8},{10,11... | collective-permute-start | bytes 3145736 | tf_op jit(solution)/shard_map/ppermute | solution.py:424
  72.7 2.3 %collective-permute-done.11 = bf16[16,64,512]{2,1,0:T(8,128)(2,1)S(1)} collective-permute-done((bf16[16,64,512]{2,1,0:T(8,128)(2,1)S(1)}, bf16[16,64,512]{2,1,0:T(8,128)(2,1)S(1)}, u32[]{:S(2)}, u32[]{:S(2)}) %collective-permute-start.11) | collective-permute-done | bytes 1048608 | tf_op jit(solution)/shard_map/ppermute | solution.py:424
  75.0 0.0 copy-done.1
  75.0 1.4 %core_sum.1 = bf16[8,512,128]{2,1,0:T(8,128)(2,1)} custom-call(bf16[1024,512]{1,0:T(8,128)(2,1)S(1)} %bitcast.16, bf16[1024,512]{1,0:T(8,128)(2,1)S(1)} %bitcast.14), custom_call_target="tpu_custom_call" | custom-call | flops 1150000000 | bytes 3690000 | tf_op jit(solution)/shard_map/core_sum/pallas_call | solution.py:391
  76.4 5.7 %all-to-all-start = ((bf16[8,512,128]{2,1,0:T(8,128)(2,1)}), bf16[8,512,128]{2,1,0:T(8,128)(2,1)S(1)}, u32[]{:S(2)}, u32[]{:S(2)}) async-start(bf16[8,512,128]{2,1,0:T(8,128)(2,1)} %core_sum.1), calls=%async_computation | async-start | bytes 2097152 | tf_op jit(solution)/shard_map/all_to_all | solution.py:452
  82.1 1.5 %collective-permute-start.12 = (bf16[512,128]{1,0:T(8,128)(2,1)S(1)}, bf16[512,128]{1,0:T(8,128)(2,1)S(1)}, u32[]{:S(2)}, u32[]{:S(2)}) collective-permute-start(bf16[512,128]{1,0:T(8,128)(2,1)S(1)} %get-tuple-element.58), channel_id=1, source_target_pairs={{0,32},{32,0},{64,96},{96,64},{128,160},{160,128},{192,224},{224,1... | collective-permute-start | bytes 393224 | tf_op jit(solution)/shard_map/ppermute | solution.py:451
  83.6 15.2 %collective-permute-done.12.refs_2_ = bf16[512,128]{1,0:T(8,128)(2,1)S(1)} collective-permute-done((bf16[512,128]{1,0:T(8,128)(2,1)S(1)}, bf16[512,128]{1,0:T(8,128)(2,1)S(1)}, u32[]{:S(2)}, u32[]{:S(2)}) %collective-permute-start.12) | collective-permute-done | bytes 131104 | tf_op jit(solution)/shard_map/ppermute | solution.py:451
  98.7 0.0 all-to-all-done.refs_0_
  98.7 0.2 lat_sum.1
  99.0 22.2 %all_to_all.10.refs_0_ = bf16[16,2,32,128]{3,2,1,0:T(8,128)(2,1)S(1)} all-to-all(bf16[16,2,32,128]{3,2,1,0:T(8,128)(2,1)S(1)} %lat_sum.1), channel_id=1, replica_groups={{0,2,4,6,8,10,12,14,16,18,20,22,24,26,28,30},{1,3,5,7,9,11,13,15,17,19,..., dimensions={0} | all-to-all | bytes 524288 | tf_op jit(solution)/shard_map/all_to_all | solution.py:455
  121.1 0.7 lon_sum.1
Async XLA Ops:
  1.6 24.6 %collective-permute-start.3 = (bf16[288,512]{1,0:T(8,128)(2,1)S(1)}, bf16[288,512]{1,0:T(8,128)(2,1)S(1)}, u32[]{:S(2)}, u32[]{:S(2)}) collective-permute-start(bf16[288,512]{1,0:T(8,128)(2,1)S(1)} %bitcast.17), channel_id=1, source_target_pairs={{0,224},{32,0},{64,32},{96,64},{128,96},{160,128},{192,160},{224,1... | collective-permute-start | bytes 884744 | tf_op jit(solution)/shard_map/ppermute | solution.py:408
  3.2 20.1 %copy-start.2 = (pred[144,144]{1,0:T(8,128)(4,1)S(1)}, pred[144,144]{1,0:T(8,128)(4,1)}, u32[]{:S(2)}) copy-start(pred[144,144]{1,0:T(8,128)(4,1)} %constant.69.clone) | copy-start | bytes 62212
  12.2 14.0 %collective-permute-start = (bf16[256,512]{1,0:T(8,128)(2,1)}, bf16[256,512]{1,0:T(8,128)(2,1)S(1)}, u32[]{:S(2)}, u32[]{:S(2)}) collective-permute-start(bf16[256,512]{1,0:T(8,128)(2,1)} %get-tuple-element.33), channel_id=1, source_target_pairs={{0,224},{32,0},{64,32},{96,64},{128,96},{160,128},{192,160},{224,1... | collective-permute-start | bytes 786440 | tf_op jit(solution)/shard_map/ppermute | solution.py:408
  14.5 9.6 %collective-permute-start.1 = (bf16[128,512]{1,0:T(8,128)(2,1)}, bf16[128,512]{1,0:T(8,128)(2,1)S(1)}, u32[]{:S(2)}, u32[]{:S(2)}) collective-permute-start(bf16[128,512]{1,0:T(8,128)(2,1)} %get-tuple-element.34), channel_id=1, source_target_pairs={{0,31},{1,0},{2,1},{3,2},{4,3},{5,4},{6,5},{7,6},{8,7},{9,8},{10,9... | collective-permute-start | bytes 393224 | tf_op jit(solution)/shard_map/ppermute | solution.py:410
  20.1 6.1 %collective-permute-start.2 = (bf16[128,512]{1,0:T(8,128)(2,1)}, bf16[128,512]{1,0:T(8,128)(2,1)S(1)}, u32[]{:S(2)}, u32[]{:S(2)}) collective-permute-start(bf16[128,512]{1,0:T(8,128)(2,1)} %get-tuple-element.35), channel_id=1, source_target_pairs={{0,255},{1,224},{2,225},{3,226},{4,227},{5,228},{6,229},{7,230},{8... | collective-permute-start | bytes 393224 | tf_op jit(solution)/shard_map/ppermute | solution.py:416
  24.0 2.2 %copy-start.7 = (bf16[128,512]{1,0:T(8,128)(2,1)}, bf16[128,512]{1,0:T(8,128)(2,1)S(1)}, u32[]{:S(2)}) copy-start(bf16[128,512]{1,0:T(8,128)(2,1)S(1)} %collective-permute-done.1.refs_3_) | copy-start | bytes 393220
  26.2 0.7 copy-start.8
  26.2 0.8 copy-start.6
  26.2 0.8 copy-start.4
  45.5 3.2 %collective-permute-start.7 = (bf16[16,64,512]{2,1,0:T(8,128)(2,1)}, bf16[16,64,512]{2,1,0:T(8,128)(2,1)S(1)}, u32[]{:S(2)}, u32[]{:S(2)}) collective-permute-start(bf16[16,64,512]{2,1,0:T(8,128)(2,1)} %get-tuple-element.49), channel_id=1, source_target_pairs={{0,1},{1,0},{2,3},{3,2},{4,5},{5,4},{6,7},{7,6},{8,9},{9,8},{10,11... | collective-permute-start | bytes 3145736 | tf_op jit(solution)/shard_map/ppermute | solution.py:424
  45.8 10.6 %collective-permute-start.4 = (bf16[256,512]{1,0:T(8,128)(2,1)}, bf16[256,512]{1,0:T(8,128)(2,1)S(1)}, u32[]{:S(2)}, u32[]{:S(2)}) collective-permute-start(bf16[256,512]{1,0:T(8,128)(2,1)} %get-tuple-element.37), channel_id=1, source_target_pairs={{0,32},{32,64},{64,96},{96,128},{128,160},{160,192},{192,224},{224... | collective-permute-start | bytes 786440 | tf_op jit(solution)/shard_map/ppermute | solution.py:408
  46.2 7.7 %collective-permute-start.5 = (bf16[64,512]{1,0:T(8,128)(2,1)}, bf16[64,512]{1,0:T(8,128)(2,1)S(1)}, u32[]{:S(2)}, u32[]{:S(2)}) collective-permute-start(bf16[64,512]{1,0:T(8,128)(2,1)} %get-tuple-element.38), channel_id=1, source_target_pairs={{0,1},{1,2},{2,3},{3,4},{4,5},{5,6},{6,7},{7,8},{8,9},{9,10},{10,1... | collective-permute-start | bytes 196616 | tf_op jit(solution)/shard_map/ppermute | solution.py:410
  46.3 10.1 %collective-permute-start.6 = (bf16[64,512]{1,0:T(8,128)(2,1)}, bf16[64,512]{1,0:T(8,128)(2,1)S(1)}, u32[]{:S(2)}, u32[]{:S(2)}) collective-permute-start(bf16[64,512]{1,0:T(8,128)(2,1)} %get-tuple-element.39), channel_id=1, source_target_pairs={{0,33},{1,34},{2,35},{3,36},{4,37},{5,38},{6,39},{7,40},{8,41},{9,... | collective-permute-start | bytes 196616 | tf_op jit(solution)/shard_map/ppermute | solution.py:416
  48.7 1.2 %copy-start = (bf16[16,64,512]{2,1,0:T(8,128)(2,1)S(1)}, bf16[16,64,512]{2,1,0:T(8,128)(2,1)}, u32[]{:S(2)}) copy-start(bf16[16,64,512]{2,1,0:T(8,128)(2,1)} %get-tuple-element.48) | copy-start | bytes 3145732
  50.5 19.8 %collective-permute-start.10 = (bf16[2,512,128]{2,1,0:T(8,128)(2,1)S(1)}, bf16[2,512,128]{2,1,0:T(8,128)(2,1)S(1)}, u32[]{:S(2)}, u32[]{:S(2)}) collective-permute-start(bf16[2,512,128]{2,1,0:T(8,128)(2,1)S(1)} %get-tuple-element.53), channel_id=1, source_target_pairs={{0,64},{32,96},{64,128},{96,160},{128,192},{160,224},{192,0},{224,... | collective-permute-start | bytes 786440 | tf_op jit(solution)/shard_map/ppermute | solution.py:443
  51.3 18.9 %collective-permute-start.8 = (bf16[2,512,128]{2,1,0:T(8,128)(2,1)S(1)}, bf16[2,512,128]{2,1,0:T(8,128)(2,1)S(1)}, u32[]{:S(2)}, u32[]{:S(2)}) collective-permute-start(bf16[2,512,128]{2,1,0:T(8,128)(2,1)S(1)} %get-tuple-element.51), channel_id=1, source_target_pairs={{0,128},{32,160},{64,192},{96,224},{128,0},{160,32},{192,64},{224,... | collective-permute-start | bytes 786440 | tf_op jit(solution)/shard_map/ppermute | solution.py:443
  53.9 2.5 %copy-start.9 = (bf16[64,512]{1,0:T(8,128)(2,1)}, bf16[64,512]{1,0:T(8,128)(2,1)S(1)}, u32[]{:S(2)}) copy-start(bf16[64,512]{1,0:T(8,128)(2,1)S(1)} %collective-permute-done.5.refs_3_) | copy-start | bytes 196612
  53.9 16.4 %collective-permute-start.9 = (bf16[2,512,128]{2,1,0:T(8,128)(2,1)S(1)}, bf16[2,512,128]{2,1,0:T(8,128)(2,1)S(1)}, u32[]{:S(2)}, u32[]{:S(2)}) collective-permute-start(bf16[2,512,128]{2,1,0:T(8,128)(2,1)S(1)} %get-tuple-element.52), channel_id=1, source_target_pairs={{0,192},{32,224},{64,0},{96,32},{128,64},{160,96},{192,128},{224,1... | collective-permute-start | bytes 786440 | tf_op jit(solution)/shard_map/ppermute | solution.py:443
  56.4 0.6 copy-start.10
  56.4 0.7 copy-start.5
  70.2 1.2 %copy-start.3 = (bf16[16,64,512]{2,1,0:T(8,128)(2,1)S(1)}, bf16[16,64,512]{2,1,0:T(8,128)(2,1)}, u32[]{:S(2)}) copy-start(bf16[16,64,512]{2,1,0:T(8,128)(2,1)} %get-tuple-element.56) | copy-start | bytes 3145732
  70.2 4.8 %copy-start.1 = (bf16[16,64,512]{2,1,0:T(8,128)(2,1)S(1)}, bf16[16,64,512]{2,1,0:T(8,128)(2,1)}, u32[]{:S(2)}) copy-start(bf16[16,64,512]{2,1,0:T(8,128)(2,1)} %get-tuple-element.46) | copy-start | bytes 3145732
  71.4 3.6 %collective-permute-start.11 = (bf16[16,64,512]{2,1,0:T(8,128)(2,1)S(1)}, bf16[16,64,512]{2,1,0:T(8,128)(2,1)S(1)}, u32[]{:S(2)}, u32[]{:S(2)}) collective-permute-start(bf16[16,64,512]{2,1,0:T(8,128)(2,1)S(1)} %copy-done.3), channel_id=1, source_target_pairs={{0,1},{1,0},{2,3},{3,2},{4,5},{5,4},{6,7},{7,6},{8,9},{9,8},{10,11... | collective-permute-start | bytes 3145736 | tf_op jit(solution)/shard_map/ppermute | solution.py:424
  76.4 22.3 %all-to-all-start = ((bf16[8,512,128]{2,1,0:T(8,128)(2,1)}), bf16[8,512,128]{2,1,0:T(8,128)(2,1)S(1)}, u32[]{:S(2)}, u32[]{:S(2)}) async-start(bf16[8,512,128]{2,1,0:T(8,128)(2,1)} %core_sum.1), calls=%async_computation | async-start | bytes 2097152 | tf_op jit(solution)/shard_map/all_to_all | solution.py:452
  82.1 16.6 %collective-permute-start.12 = (bf16[512,128]{1,0:T(8,128)(2,1)S(1)}, bf16[512,128]{1,0:T(8,128)(2,1)S(1)}, u32[]{:S(2)}, u32[]{:S(2)}) collective-permute-start(bf16[512,128]{1,0:T(8,128)(2,1)S(1)} %get-tuple-element.58), channel_id=1, source_target_pairs={{0,32},{32,0},{64,96},{96,64},{128,160},{160,128},{192,224},{224,1... | collective-permute-start | bytes 393224 | tf_op jit(solution)/shard_map/ppermute | solution.py:451

commit v3 on v2

--- a/solution.py
+++ b/solution.py
@@ -172,12 +172,14 @@
 
 
 def soft(keys_stacked, queries, bias):
-    scores = dot_nt(keys_stacked, queries).reshape(4, WINDOW, WINDOW)
-    if bias is not None:
-        scores = scores + bias[None]
-    top = jnp.max(scores, axis=1, keepdims=True)
-    raised = jnp.exp(scores - top)
-    return raised * (1.0 / jnp.sum(raised, axis=1, keepdims=True))
+    out = []
+    for h in range(4):
+        scores = dot_nt(keys_stacked[h * WINDOW : (h + 1) * WINDOW], queries)
+        if bias is not None:
+            scores = scores + bias
+        raised = jnp.exp(scores - jnp.max(scores, axis=0, keepdims=True))
+        out.append(raised * (1.0 / jnp.sum(raised, axis=0, keepdims=True)))
+    return out
 
 
 def places(w, quad):
@@ -201,7 +203,7 @@
         for quad in range(2):
             span, at = places(w, quad)
             queries, keys, vals = [packed[span, at[n]] for n in range(3)]
-            probs = soft(stacked(keys, SCALE), queries, None).astype(BF16).reshape(4 * WINDOW, WINDOW)
+            probs = jnp.concatenate(soft(stacked(keys, SCALE), queries, None), axis=0).astype(BF16)
             probs_out[2 * w + quad] = probs
             mixed[span, at[0]] = dot_tn(probs, stacked(vals, 1.0)).astype(BF16)
     probs_out.flush()
@@ -216,9 +218,12 @@
 
 
 def attention_backward(packed, probs, probs_low, d_mixed, d_packed, span, at, keys_stacked, vals_stacked):
-    d_probs = dot_nt(vals_stacked, d_mixed).reshape(4, WINDOW, WINDOW)
-    inner = jnp.sum(probs * d_probs, axis=1, keepdims=True)
-    d_scores = (probs * (d_probs - inner)).astype(BF16).reshape(4 * WINDOW, WINDOW)
+    d_scores = []
+    for h in range(4):
+        d_probs = dot_nt(vals_stacked[h * WINDOW : (h + 1) * WINDOW], d_mixed)
+        inner = jnp.sum(probs[h] * d_probs, axis=0, keepdims=True)
+        d_scores.append((probs[h] * (d_probs - inner)).astype(BF16))
+    d_scores = jnp.concatenate(d_scores, axis=0)
     d_packed[span, at[0]] = dot_tn(d_scores, keys_stacked).astype(BF16)
     d_packed[span, at[1]] = (unstacked(dot(d_scores, packed[span, at[0]])) * SCALE).astype(BF16)
     d_packed[span, at[2]] = unstacked(dot(probs_low, d_mixed)).astype(BF16)
@@ -266,7 +271,7 @@
             queries, keys, vals = [packed[span, at[n]] for n in range(3)]
             keys_stacked, vals_stacked = stacked(keys, SCALE), stacked(vals, 1.0)
             probs = soft(keys_stacked, queries, bias[...])
-            probs_low = probs.astype(BF16).reshape(4 * WINDOW, WINDOW)
+            probs_low = jnp.concatenate(probs, axis=0).astype(BF16)
             mixed[span, at[0]] = dot_tn(probs_low, vals_stacked).astype(BF16)
             attention_backward(
                 packed, probs, probs_low, d_mixed_all[span, at[0]], d_packed, span, at, keys_stacked, vals_stacked
@@ -279,25 +284,31 @@
 
 
 def plain_kernel(
-    core, keep, tall, side, corner, w_proj, join, packed, probs_in, mixed, normed, values, w_qkv, unplain,
-    d_tokens, kept, sent,
-    d_mixed_all, grads, d_packed,
+    core, keep, tall, side, corner, w_proj, join, packed, probs_in, mixed, normed,
+    gradient_out, d_packed, kept, sent,
+    d_mixed_all, grads,
 ):
     gradient = gathered(join, pieces_of((keep, tall, side, corner))).astype(BF16)
+    gradient_out[...] = gradient
+    gradient_out.flush()
     d_mixed_all[...] = dot_nt(gradient, w_proj[...]).astype(BF16)
     for w in range(WINDOWS):
         for quad in range(2):
             span, at = places(w, quad)
             keys_stacked, vals_stacked = stacked(packed[span, at[1]], SCALE), stacked(packed[span, at[2]], 1.0)
             probs_low = probs_in[2 * w + quad]
-            probs = probs_low.astype(F32).reshape(4, WINDOW, WINDOW)
+            probs = [probs_low[h * WINDOW : (h + 1) * WINDOW].astype(F32) for h in range(4)]
             attention_backward(
                 packed, probs, probs_low, d_mixed_all[span, at[0]], d_packed, span, at, keys_stacked, vals_stacked
             )
+    d_packed.flush()
     weight_gradients(core, normed[...], d_packed[...], mixed[...], gradient, grads, kept, sent)
     kept.flush()
     sent.flush()
-    result = input_gradient(values[...].astype(F32), gradient, d_packed[...], w_qkv[...])
+
+
+def finish_kernel(values, gradient, d_packed, w_qkv, unplain, d_tokens):
+    result = input_gradient(values[...].astype(F32), gradient[...], d_packed[...], w_qkv[...])
     for level, part in enumerate(scattered(unplain, result)):
         d_tokens[level * LEVEL : (level + 1) * LEVEL] = part
 
@@ -308,23 +319,32 @@
     return jnp.where(left, top, turned[1]), jnp.where(left, turned[0], bottom)
 
 
-def core_sums(kept, received):
+def core_sums(kept, received, landing, sems):
     half = kept.shape[0] // 2
-    for pair in range(4):
-        at = slice(pair * 128, (pair + 1) * 128)
-        total = kept[:, at].astype(F32) + received[:, at].astype(F32)
+    spans = [slice(pair * 128, (pair + 1) * 128) for pair in range(4)]
+    copies = [pltpu.make_async_copy(kept.at[:, at], landing.at[n], sems.at[n]) for n, at in enumerate(spans)]
+    for copy in copies:
+        copy.start()
+    for pair, at in enumerate(spans):
+        copies[pair].wait()
+        total = landing[pair].astype(F32) + received[:, at].astype(F32)
         for odd, part in enumerate(swapped_halves(total[:half], total[half:])):
             yield 2 * pair + odd, part.astype(BF16)
 
 
-def core_sum_kernel(kept, received, out):
-    for lat, part in core_sums(kept, received):
-        out[lat] = part
+def core_sum_kernel(kept, received, out, landing, made, sems):
+    leaving = []
+    for lat, part in core_sums(kept, received, landing, sems):
+        made[lat] = part
+        leaving.append(pltpu.make_async_copy(made.at[lat], out.at[lat], sems.at[4 + lat]))
+        leaving[-1].start()
+    for copy in leaving:
+        copy.wait()
 
 
 def core_cut_kernel(place, kept, received, *refs):
-    outs, held = refs[:-1], refs[-1]
-    for lat, part in core_sums(kept, received):
+    outs, (landing, held, sems) = refs[:-3], refs[-3:]
+    for lat, part in core_sums(kept, received, landing, sems):
         held[lat // 2, lat % 2] = part
     for step, out in enumerate(outs):
         out[...] = held[lax.rem(place[0] + step, 4)]
@@ -363,7 +383,7 @@
     return jax.ShapeDtypeStruct(dims, kind)
 
 
-def call(kernel, name, outs, *operands, scratch=(), scalar=False, fetch=None, store=(), limit=SMALL, micros=1):
+def call(kernel, name, outs, *operands, scratch=(), scalar=False, fetch=None, store=(), apart=(), own_out=False, limit=SMALL, micros=1):
     fetch = fetch or {}
     several = outs if isinstance(outs, tuple) else (outs,)
     cut = np.cumsum([0, len(operands), len(several), len(scratch), len(fetch), len(store)])
@@ -378,16 +398,16 @@
         for n in store:
             results[n].copy.wait()
 
-    held = [pltpu.VMEM(dims, BF16) for dims in scratch]
+    held = [pltpu.VMEM(dims, BF16) if isinstance(dims, tuple) else dims for dims in scratch]
     for n, index in fetch.items():
         held.append(pltpu.VMEM(operands[n].shape if index is None else operands[n].shape[1:], BF16))
     held += [pltpu.VMEM(several[n].shape, BF16) for n in store]
     if fetch or store:
         held += [pltpu.SemaphoreType.DMA((max(1, len(group)),)) for group in (fetch, store)]
-    kinds = [pltpu.HBM if n in fetch else pltpu.VMEM for n in range(len(operands))]
+    kinds = [pltpu.HBM if n in fetch or n in apart else pltpu.VMEM for n in range(len(operands))]
     if scalar:
         kinds[0] = pltpu.SMEM
-    specs = tuple(pl.BlockSpec(memory_space=pltpu.HBM if n in store else pltpu.VMEM) for n in range(len(several)))
+    specs = tuple(pl.BlockSpec(memory_space=pltpu.HBM if own_out or n in store else pltpu.VMEM) for n in range(len(several)))
     return pl.pallas_call(
         body,
         out_shape=outs,
@@ -425,14 +445,17 @@
 
 
 def core_reduced(kept, sent):
-    return call(core_sum_kernel, "core_sum", shape(8, 512, 128), kept.reshape(1024, D), core_swapped(sent), limit=12)
+    return call(
+        core_sum_kernel, "core_sum", shape(8, 512, 128), kept.reshape(1024, D), core_swapped(sent),
+        scratch=[(4, 1024, 128), (8, 512, 128), pltpu.SemaphoreType.DMA((12,))], apart=(0,), own_out=True, limit=12,
+    )
 
 
 def core_cut(kept, sent):
     place = (lax.axis_index("lat") // 2).astype(jnp.int32).reshape(1)
     return call(
         core_cut_kernel, "core_cut", (shape(2, 512, 128),) * 4, place, kept.reshape(1024, D), core_swapped(sent),
-        scratch=[(4, 2, 512, 128)], scalar=True, limit=12,
+        scratch=[(4, 1024, 128), (4, 2, 512, 128), pltpu.SemaphoreType.DMA((4,))], scalar=True, apart=(1,), limit=12,
     )
 
 
@@ -498,17 +521,26 @@
     )
     tall, side, corner = exchanged(tall, side, corner, 1)
     parts_two = far_reduced(core_cut(kept_two, sent_two))
-    d_tokens, kept_one, sent_one = call(
+    gradient, d_packed, kept_one, sent_one = call(
         plain_kernel,
         "backward_plain",
-        (field, half, half),
-        core, keep, tall, side, corner, proj_weights, join, packed, probs, mixed, normed, values, qkv_weights, unplain,
-        scratch=[(TOKENS, D), (32, 64, D), (TOKENS, 3 * D)],
+        (field, packed_field, half, half),
+        core, keep, tall, side, corner, proj_weights, join, packed, probs, mixed, normed,
+        scratch=[(TOKENS, D), (32, 64, D)],
         scalar=True,
-        fetch={6: None, 5: 0, 7: None, 8: None, 10: None, 9: None, 12: 0, 11: None, 13: None},
-        store=(1, 2),
+        fetch={6: None, 5: 0, 7: None, 8: None, 10: None, 9: None},
+        store=(0, 1, 2, 3),
         limit=LARGE,
-        micros=13,
+        micros=10,
+    )
+    d_tokens = call(
+        finish_kernel,
+        "finish_plain",
+        field,
+        values, gradient, d_packed, qkv_weights, unplain,
+        fetch={2: None, 3: 0, 0: None, 1: None, 4: None},
+        limit=LARGE,
+        micros=5,
     )
     sent_one, parts_two = lax.optimization_barrier((sent_one, parts_two))
     grad_qkv, grad_proj = reduced(core_reduced(kept_one, sent_one), parts_two)

time: 123 us -> 119 us (0.967)
  blocking collectives: 22.2 us -> 0 us
  starting transfers between devices: 29 us -> 38.3 us
  waiting for transfers between devices: 20.8 us -> 28.6 us
  Pallas kernels: 43.6 us -> 44.9 us
    all_to_all x1 -> x0, blocking collectives: 22.2 us -> none  [reduced(): lax.all_to_all(both, 'lon', 0, 0, tiled=True, axis_index_groups=groups)]
    all_to_all x0 -> x1, starting transfers between devices: none -> 9.35 us  [reduced(): lax.all_to_all(both, 'lon', 0, 0, tiled=True, axis_index_groups=groups)]
    all_to_all x0 -> x1, waiting for transfers between devices: none -> 7.98 us  [reduced(): lax.all_to_all(both, 'lon', 0, 0, tiled=True, axis_index_groups=groups)]
    pallas_call x8 -> x9, Pallas kernels: 43.6 us -> 44.9 us  [call(): pl.pallas_call(body, out_shape=outs, in_specs=[pl.BlockSpec(memory_space=...]
  transfers between devices with their start and end apart: 14 -> 15, of which waited for: 4 -> 5; matrix products, arithmetic and copies ran while one was open for 1% -> 1% of each run, Pallas kernels for 19% -> 21%
where the time goes in v3:
time: 119 us; the launch traced here: 118 us
  Pallas kernels  44.9 us (38%)
  starting transfers between devices  38.3 us (32%)
  waiting for transfers between devices  28.6 us (24%)
  local copies, waits for them, and re-layouts  4.82 us (4%)
    pallas_call x9, Pallas kernels, call(): pl.pallas_call(body, out_shape=outs, in_specs=[pl.BlockSpec(memory_space=...  44.9 us
    ppermute x1, waiting for transfers between devices, reduced(): lax.ppermute(sent, 'lat', [(i, i ^ 1) for i in range(lax.axis_size('lat'))])  15.2 us
    all_to_all x1, starting transfers between devices, reduced(): lax.all_to_all(both, 'lon', 0, 0, tiled=True, axis_index_groups=groups)  9.35 us
    all_to_all x1, waiting for transfers between devices, reduced(): lax.all_to_all(both, 'lon', 0, 0, tiled=True, axis_index_groups=groups)  7.98 us
    ppermute x3, starting transfers between devices, far_reduced(): lax.ppermute(parts[step], 'lat', [(i, (i + 2 * step) % n) for i in range(...  5.78 us
    ppermute x2, starting transfers between devices, moved(): lax.ppermute(piece, 'lon', [(i, (i + lon) % n_lon) for i in range(n_lon)])  5.73 us
    all_to_all x1, starting transfers between devices, reduced(): arrived = lax.all_to_all(chunks_one, 'lat', 0, 0, tiled=True)  5.68 us
    ppermute x2, starting transfers between devices, moved(): return lax.ppermute(piece, ('lat', 'lon'), route)  4.62 us
  transfers between devices with their start and end apart: 15, of which 5 were waited for; matrix products, arithmetic and copies ran while one was open for 1% of the time, Pallas kernels for 21%

profile of v3, /device:TPU:2, one launch (start us, length us, event | category | flops | bytes accessed | tf_op | source)
XLA Modules:
  0.0 118.1 jit_solution(3140853785486760952)
XLA Ops:
  0.6 1.0 slice.3
  1.6 1.6 %collective-permute-start.3 = (bf16[288,512]{1,0:T(8,128)(2,1)S(1)}, bf16[288,512]{1,0:T(8,128)(2,1)S(1)}, u32[]{:S(2)}, u32[]{:S(2)}) collective-permute-start(bf16[288,512]{1,0:T(8,128)(2,1)S(1)} %bitcast.17), channel_id=1, source_target_pairs={{0,224},{32,0},{64,32},{96,64},{128,96},{160,128},{192,160},{224,1... | collective-permute-start | bytes 884744 | tf_op jit(solution)/shard_map/ppermute | solution.py:428
  3.2 0.0 copy-start.2
  3.2 8.2 %forward.1 = (bf16[256,512]{1,0:T(8,128)(2,1)}, bf16[256,512]{1,0:T(8,128)(2,1)}, bf16[128,512]{1,0:T(8,128)(2,1)}, bf16[128,512]{1,0:T(8,128)(2,1)}, bf16[576,5...) custom-call(bf16[576,512]{1,0:T(8,128)(2,1)} %bitcast.20, ...), custom_call_target="tpu_custom_call" | custom-call | flops 10350000128 | bytes 33210000 | tf_op jit(solution)/shard_map/forward/pallas_call | solution.py:411
  11.5 2.3 %collective-permute-start = (bf16[256,512]{1,0:T(8,128)(2,1)}, bf16[256,512]{1,0:T(8,128)(2,1)S(1)}, u32[]{:S(2)}, u32[]{:S(2)}) collective-permute-start(bf16[256,512]{1,0:T(8,128)(2,1)} %get-tuple-element.35), channel_id=1, source_target_pairs={{0,224},{32,0},{64,32},{96,64},{128,96},{160,128},{192,160},{224,1... | collective-permute-start | bytes 786440 | tf_op jit(solution)/shard_map/ppermute | solution.py:428
  13.8 5.6 %collective-permute-start.1 = (bf16[128,512]{1,0:T(8,128)(2,1)}, bf16[128,512]{1,0:T(8,128)(2,1)S(1)}, u32[]{:S(2)}, u32[]{:S(2)}) collective-permute-start(bf16[128,512]{1,0:T(8,128)(2,1)} %get-tuple-element.36), channel_id=1, source_target_pairs={{0,31},{1,0},{2,1},{3,2},{4,3},{5,4},{6,5},{7,6},{8,7},{9,8},{10,9... | collective-permute-start | bytes 393224 | tf_op jit(solution)/shard_map/ppermute | solution.py:430
  19.4 3.2 %collective-permute-start.2 = (bf16[128,512]{1,0:T(8,128)(2,1)}, bf16[128,512]{1,0:T(8,128)(2,1)S(1)}, u32[]{:S(2)}, u32[]{:S(2)}) collective-permute-start(bf16[128,512]{1,0:T(8,128)(2,1)} %get-tuple-element.37), channel_id=1, source_target_pairs={{0,255},{1,224},{2,225},{3,226},{4,227},{5,228},{6,229},{7,230},{8... | collective-permute-start | bytes 393224 | tf_op jit(solution)/shard_map/ppermute | solution.py:436
  22.6 0.0 copy-done.2
  22.6 0.7 and_select_fusion.refs_12_
  23.3 0.0 collective-permute-done.1.refs_3_
  23.3 0.0 copy-start.7
  23.3 2.1 %collective-permute-done.2.refs_4_ = bf16[128,512]{1,0:T(8,128)(2,1)S(1)} collective-permute-done((bf16[128,512]{1,0:T(8,128)(2,1)}, bf16[128,512]{1,0:T(8,128)(2,1)S(1)}, u32[]{:S(2)}, u32[]{:S(2)}) %collective-permute-start.2) | collective-permute-done | bytes 131104 | tf_op jit(solution)/shard_map/ppermute | solution.py:436
  25.5 0.0 copy-start.8
  25.5 0.0 collective-permute-done.refs_2_
  25.5 0.0 copy-start.6
  25.5 0.0 collective-permute-done.3.refs_6_
  25.5 0.0 copy-start.4
  25.5 0.0 copy-done.7
  25.5 0.6 copy-done.8
  26.1 0.1 copy-done.6
  26.3 0.1 copy-done.4
  26.4 16.2 %backward_shifted.1 = (bf16[256,512]{1,0:T(8,128)(2,1)}, bf16[256,512]{1,0:T(8,128)(2,1)}, bf16[64,512]{1,0:T(8,128)(2,1)}, bf16[64,512]{1,0:T(8,128)(2,1)}, bf1...) custom-call(s32[1]{0:T(128)} %bitcast.2.refs_0_, bf16[256,512]{1,0:T(8,128)(2,1)} %get-tuple-element.34.refs_1_, ...), custom_call_target="tpu_custom_call" | custom-call | flops 20700000256 | bytes 66420000 | tf_op jit(solution)/shard_map/backward_shifted/pallas_call | solution.py:411
  42.6 0.1 collective-permute-start.7
  42.7 0.4 collective-permute-start.4
  43.1 0.1 collective-permute-start.5
  43.2 1.4 %collective-permute-start.6 = (bf16[64,512]{1,0:T(8,128)(2,1)}, bf16[64,512]{1,0:T(8,128)(2,1)S(1)}, u32[]{:S(2)}, u32[]{:S(2)}) collective-permute-start(bf16[64,512]{1,0:T(8,128)(2,1)} %get-tuple-element.41), channel_id=1, source_target_pairs={{0,33},{1,34},{2,35},{3,36},{4,37},{5,38},{6,39},{7,40},{8,41},{9,... | collective-permute-start | bytes 196616 | tf_op jit(solution)/shard_map/ppermute | solution.py:436
  44.5 1.0 collective-permute-done.7
  45.5 0.0 copy-start
  45.5 1.2 %copy-done = bf16[16,64,512]{2,1,0:T(8,128)(2,1)S(1)} copy-done((bf16[16,64,512]{2,1,0:T(8,128)(2,1)S(1)}, bf16[16,64,512]{2,1,0:T(8,128)(2,1)}, u32[]{:S(2)}) %copy-start) | copy-done | bytes 1048600
  46.8 0.9 core_cut.1
  47.7 1.1 collective-permute-start.10
  48.7 2.3 %collective-permute-start.8 = (bf16[2,512,128]{2,1,0:T(8,128)(2,1)S(1)}, bf16[2,512,128]{2,1,0:T(8,128)(2,1)S(1)}, u32[]{:S(2)}, u32[]{:S(2)}) collective-permute-start(bf16[2,512,128]{2,1,0:T(8,128)(2,1)S(1)} %get-tuple-element.53), channel_id=1, source_target_pairs={{0,128},{32,160},{64,192},{96,224},{128,0},{160,32},{192,64},{224,... | collective-permute-start | bytes 786440 | tf_op jit(solution)/shard_map/ppermute | solution.py:466
  51.1 0.0 collective-permute-done.5.refs_3_
  51.1 0.0 copy-start.9
  51.1 2.4 %collective-permute-start.9 = (bf16[2,512,128]{2,1,0:T(8,128)(2,1)S(1)}, bf16[2,512,128]{2,1,0:T(8,128)(2,1)S(1)}, u32[]{:S(2)}, u32[]{:S(2)}) collective-permute-start(bf16[2,512,128]{2,1,0:T(8,128)(2,1)S(1)} %get-tuple-element.54), channel_id=1, source_target_pairs={{0,192},{32,224},{64,0},{96,32},{128,64},{160,96},{192,128},{224,1... | collective-permute-start | bytes 786440 | tf_op jit(solution)/shard_map/ppermute | solution.py:466
  53.5 0.0 collective-permute-done.6.refs_4_
  53.5 0.0 copy-start.10
  53.5 0.0 collective-permute-done.4.refs_2_
  53.5 0.0 copy-start.5
  53.5 0.0 copy-done.9
  53.5 0.6 copy-done.10
  54.1 0.1 copy-done.5
  54.2 10.9 %backward_plain.1 = (bf16[576,512]{1,0:T(8,128)(2,1)}, bf16[576,1536]{1,0:T(8,128)(2,1)}, bf16[16,64,512]{2,1,0:T(8,128)(2,1)}, bf16[16,64,512]{2,1,0:T(8,128)(2,1)}) custom-call(s32[1]{0:T(128)} %bitcast.2.refs_0_, bf16[256,512]{1,0:T(8,128)(2,1)} %get-tuple-element.38.refs_1_, bf16[256,512]{1,0:T(8,128)(2,1)} %copy-done.5, bf16[64,512]{1,0:T(8,128)(2,1)} %copy-done.9, ...), custom_call_target="tpu_custom_call" | custom-call | flops 11500000256 | bytes 36900000 | tf_op jit(solution)/shard_map/backward_plain/pallas_call | solution.py:411
  65.1 0.0 copy-start.3
  65.2 0.0 copy-start.1
  65.2 0.0 collective-permute-done.10.refs_4_
  65.2 0.0 collective-permute-done.8.refs_2_
  65.2 0.0 collective-permute-done.9.refs_3_
  65.2 0.2 far_sum.1
  65.4 1.0 copy-done.3
  66.4 1.3 %collective-permute-start.11 = (bf16[16,64,512]{2,1,0:T(8,128)(2,1)S(1)}, bf16[16,64,512]{2,1,0:T(8,128)(2,1)S(1)}, u32[]{:S(2)}, u32[]{:S(2)}) collective-permute-start(bf16[16,64,512]{2,1,0:T(8,128)(2,1)S(1)} %copy-done.3), channel_id=1, source_target_pairs={{0,1},{1,0},{2,3},{3,2},{4,5},{5,4},{6,7},{7,6},{8,9},{9,8},{10,11... | collective-permute-start | bytes 3145736 | tf_op jit(solution)/shard_map/ppermute | solution.py:444
  67.6 2.3 %collective-permute-done.11 = bf16[16,64,512]{2,1,0:T(8,128)(2,1)S(1)} collective-permute-done((bf16[16,64,512]{2,1,0:T(8,128)(2,1)S(1)}, bf16[16,64,512]{2,1,0:T(8,128)(2,1)S(1)}, u32[]{:S(2)}, u32[]{:S(2)}) %collective-permute-start.11) | collective-permute-done | bytes 1048608 | tf_op jit(solution)/shard_map/ppermute | solution.py:444
  69.9 0.0 copy-done.1
  69.9 1.6 %core_sum.1 = bf16[8,512,128]{2,1,0:T(8,128)(2,1)} custom-call(bf16[1024,512]{1,0:T(8,128)(2,1)S(1)} %bitcast.16, bf16[1024,512]{1,0:T(8,128)(2,1)S(1)} %bitcast.14), custom_call_target="tpu_custom_call" | custom-call | flops 1150000000 | bytes 3690000 | tf_op jit(solution)/shard_map/core_sum/pallas_call | solution.py:411
  71.5 5.7 %all-to-all-start = ((bf16[8,512,128]{2,1,0:T(8,128)(2,1)}), bf16[8,512,128]{2,1,0:T(8,128)(2,1)S(1)}, u32[]{:S(2)}, u32[]{:S(2)}) async-start(bf16[8,512,128]{2,1,0:T(8,128)(2,1)} %core_sum.1), calls=%async_computation | async-start | bytes 2097152 | tf_op jit(solution)/shard_map/all_to_all | solution.py:475
  77.2 1.5 %collective-permute-start.12 = (bf16[512,128]{1,0:T(8,128)(2,1)S(1)}, bf16[512,128]{1,0:T(8,128)(2,1)S(1)}, u32[]{:S(2)}, u32[]{:S(2)}) collective-permute-start(bf16[512,128]{1,0:T(8,128)(2,1)S(1)} %get-tuple-element.60), channel_id=1, source_target_pairs={{0,32},{32,0},{64,96},{96,64},{128,160},{160,128},{192,224},{224,1... | collective-permute-start | bytes 393224 | tf_op jit(solution)/shard_map/ppermute | solution.py:474
  78.7 15.2 %collective-permute-done.12.refs_2_ = bf16[512,128]{1,0:T(8,128)(2,1)S(1)} collective-permute-done((bf16[512,128]{1,0:T(8,128)(2,1)S(1)}, bf16[512,128]{1,0:T(8,128)(2,1)S(1)}, u32[]{:S(2)}, u32[]{:S(2)}) %collective-permute-start.12) | collective-permute-done | bytes 131104 | tf_op jit(solution)/shard_map/ppermute | solution.py:474
  93.9 0.0 all-to-all-done.refs_0_
  93.9 1.0 lat_sum.1
  94.8 9.4 %all-to-all-start.1 = ((bf16[16,2,32,128]{3,2,1,0:T(8,128)(2,1)}), bf16[16,2,32,128]{3,2,1,0:T(8,128)(2,1)S(1)}, u32[]{:S(2)}, u32[]{:S(2)}) async-start(bf16[16,2,32,128]{3,2,1,0:T(8,128)(2,1)} %lat_sum.1), calls=%async_computation.1 | async-start | bytes 524288 | tf_op jit(solution)/shard_map/all_to_all | solution.py:478
  104.2 5.1 %finish_plain.1 = bf16[576,512]{1,0:T(8,128)(2,1)} custom-call(bf16[576,512]{1,0:T(8,128)(2,1)} %get-tuple-element.33.refs_0_, bf16[576,512]{1,0:T(8,128)(2,1)} %get-tuple-element.46.refs_1_, bf16[576,1536]{1,0:T(8,128)(2,1)} %get-tuple-element.47.refs_2_, bf16[2,512,1536]{2,1,0:T(8,128)(2,1)} %refs_3_.3, bf16[288,288]{1,0:T(8,128)(2,1)} %constant.62.clone.refs_4_), custom_call_target="tpu_custom_call" | custom-call | flops 5750000128 | bytes 18450000 | tf_op jit(solution)/shard_map/finish_plain/pallas_call | solution.py:411
  109.3 8.0 %all-to-all-done.1.refs_0_ = bf16[16,2,32,128]{3,2,1,0:T(8,128)(2,1)S(1)} async-done(((bf16[16,2,32,128]{3,2,1,0:T(8,128)(2,1)}), bf16[16,2,32,128]{3,2,1,0:T(8,128)(2,1)S(1)}, u32[]{:S(2)}, u32[]{:S(2)}) %all-to-all-start.1) | async-done | bytes 262176 | tf_op jit(solution)/shard_map/all_to_all | solution.py:478
  117.3 0.7 lon_sum.1
Async XLA Ops:
  1.6 23.9 %collective-permute-start.3 = (bf16[288,512]{1,0:T(8,128)(2,1)S(1)}, bf16[288,512]{1,0:T(8,128)(2,1)S(1)}, u32[]{:S(2)}, u32[]{:S(2)}) collective-permute-start(bf16[288,512]{1,0:T(8,128)(2,1)S(1)} %bitcast.17), channel_id=1, source_target_pairs={{0,224},{32,0},{64,32},{96,64},{128,96},{160,128},{192,160},{224,1... | collective-permute-start | bytes 884744 | tf_op jit(solution)/shard_map/ppermute | solution.py:428
  3.2 19.4 %copy-start.2 = (pred[144,144]{1,0:T(8,128)(4,1)S(1)}, pred[144,144]{1,0:T(8,128)(4,1)}, u32[]{:S(2)}) copy-start(pred[144,144]{1,0:T(8,128)(4,1)} %constant.69.clone) | copy-start | bytes 62212
  11.5 14.0 %collective-permute-start = (bf16[256,512]{1,0:T(8,128)(2,1)}, bf16[256,512]{1,0:T(8,128)(2,1)S(1)}, u32[]{:S(2)}, u32[]{:S(2)}) collective-permute-start(bf16[256,512]{1,0:T(8,128)(2,1)} %get-tuple-element.35), channel_id=1, source_target_pairs={{0,224},{32,0},{64,32},{96,64},{128,96},{160,128},{192,160},{224,1... | collective-permute-start | bytes 786440 | tf_op jit(solution)/shard_map/ppermute | solution.py:428
  13.8 9.6 %collective-permute-start.1 = (bf16[128,512]{1,0:T(8,128)(2,1)}, bf16[128,512]{1,0:T(8,128)(2,1)S(1)}, u32[]{:S(2)}, u32[]{:S(2)}) collective-permute-start(bf16[128,512]{1,0:T(8,128)(2,1)} %get-tuple-element.36), channel_id=1, source_target_pairs={{0,31},{1,0},{2,1},{3,2},{4,3},{5,4},{6,5},{7,6},{8,7},{9,8},{10,9... | collective-permute-start | bytes 393224 | tf_op jit(solution)/shard_map/ppermute | solution.py:430
  19.4 6.1 %collective-permute-start.2 = (bf16[128,512]{1,0:T(8,128)(2,1)}, bf16[128,512]{1,0:T(8,128)(2,1)S(1)}, u32[]{:S(2)}, u32[]{:S(2)}) collective-permute-start(bf16[128,512]{1,0:T(8,128)(2,1)} %get-tuple-element.37), channel_id=1, source_target_pairs={{0,255},{1,224},{2,225},{3,226},{4,227},{5,228},{6,229},{7,230},{8... | collective-permute-start | bytes 393224 | tf_op jit(solution)/shard_map/ppermute | solution.py:436
  23.3 2.2 %copy-start.7 = (bf16[128,512]{1,0:T(8,128)(2,1)}, bf16[128,512]{1,0:T(8,128)(2,1)S(1)}, u32[]{:S(2)}) copy-start(bf16[128,512]{1,0:T(8,128)(2,1)S(1)} %collective-permute-done.1.refs_3_) | copy-start | bytes 393220
  25.5 0.7 copy-start.8
  25.5 0.8 copy-start.6
  25.5 0.9 copy-start.4
  42.6 3.0 %collective-permute-start.7 = (bf16[16,64,512]{2,1,0:T(8,128)(2,1)}, bf16[16,64,512]{2,1,0:T(8,128)(2,1)S(1)}, u32[]{:S(2)}, u32[]{:S(2)}) collective-permute-start(bf16[16,64,512]{2,1,0:T(8,128)(2,1)} %get-tuple-element.51), channel_id=1, source_target_pairs={{0,1},{1,0},{2,3},{3,2},{4,5},{5,4},{6,7},{7,6},{8,9},{9,8},{10,11... | collective-permute-start | bytes 3145736 | tf_op jit(solution)/shard_map/ppermute | solution.py:444
  42.7 10.8 %collective-permute-start.4 = (bf16[256,512]{1,0:T(8,128)(2,1)}, bf16[256,512]{1,0:T(8,128)(2,1)S(1)}, u32[]{:S(2)}, u32[]{:S(2)}) collective-permute-start(bf16[256,512]{1,0:T(8,128)(2,1)} %get-tuple-element.39), channel_id=1, source_target_pairs={{0,32},{32,64},{64,96},{96,128},{128,160},{160,192},{192,224},{224... | collective-permute-start | bytes 786440 | tf_op jit(solution)/shard_map/ppermute | solution.py:428
  43.1 8.0 %collective-permute-start.5 = (bf16[64,512]{1,0:T(8,128)(2,1)}, bf16[64,512]{1,0:T(8,128)(2,1)S(1)}, u32[]{:S(2)}, u32[]{:S(2)}) collective-permute-start(bf16[64,512]{1,0:T(8,128)(2,1)} %get-tuple-element.40), channel_id=1, source_target_pairs={{0,1},{1,2},{2,3},{3,4},{4,5},{5,6},{6,7},{7,8},{8,9},{9,10},{10,1... | collective-permute-start | bytes 196616 | tf_op jit(solution)/shard_map/ppermute | solution.py:430
  43.2 10.3 %collective-permute-start.6 = (bf16[64,512]{1,0:T(8,128)(2,1)}, bf16[64,512]{1,0:T(8,128)(2,1)S(1)}, u32[]{:S(2)}, u32[]{:S(2)}) collective-permute-start(bf16[64,512]{1,0:T(8,128)(2,1)} %get-tuple-element.41), channel_id=1, source_target_pairs={{0,33},{1,34},{2,35},{3,36},{4,37},{5,38},{6,39},{7,40},{8,41},{9,... | collective-permute-start | bytes 196616 | tf_op jit(solution)/shard_map/ppermute | solution.py:436
  45.5 1.2 %copy-start = (bf16[16,64,512]{2,1,0:T(8,128)(2,1)S(1)}, bf16[16,64,512]{2,1,0:T(8,128)(2,1)}, u32[]{:S(2)}) copy-start(bf16[16,64,512]{2,1,0:T(8,128)(2,1)} %get-tuple-element.50) | copy-start | bytes 3145732
  47.7 17.5 %collective-permute-start.10 = (bf16[2,512,128]{2,1,0:T(8,128)(2,1)S(1)}, bf16[2,512,128]{2,1,0:T(8,128)(2,1)S(1)}, u32[]{:S(2)}, u32[]{:S(2)}) collective-permute-start(bf16[2,512,128]{2,1,0:T(8,128)(2,1)S(1)} %get-tuple-element.55), channel_id=1, source_target_pairs={{0,64},{32,96},{64,128},{96,160},{128,192},{160,224},{192,0},{224,... | collective-permute-start | bytes 786440 | tf_op jit(solution)/shard_map/ppermute | solution.py:466
  48.7 16.4 %collective-permute-start.8 = (bf16[2,512,128]{2,1,0:T(8,128)(2,1)S(1)}, bf16[2,512,128]{2,1,0:T(8,128)(2,1)S(1)}, u32[]{:S(2)}, u32[]{:S(2)}) collective-permute-start(bf16[2,512,128]{2,1,0:T(8,128)(2,1)S(1)} %get-tuple-element.53), channel_id=1, source_target_pairs={{0,128},{32,160},{64,192},{96,224},{128,0},{160,32},{192,64},{224,... | collective-permute-start | bytes 786440 | tf_op jit(solution)/shard_map/ppermute | solution.py:466
  51.1 2.4 %copy-start.9 = (bf16[64,512]{1,0:T(8,128)(2,1)}, bf16[64,512]{1,0:T(8,128)(2,1)S(1)}, u32[]{:S(2)}) copy-start(bf16[64,512]{1,0:T(8,128)(2,1)S(1)} %collective-permute-done.5.refs_3_) | copy-start | bytes 196612
  51.1 14.1 %collective-permute-start.9 = (bf16[2,512,128]{2,1,0:T(8,128)(2,1)S(1)}, bf16[2,512,128]{2,1,0:T(8,128)(2,1)S(1)}, u32[]{:S(2)}, u32[]{:S(2)}) collective-permute-start(bf16[2,512,128]{2,1,0:T(8,128)(2,1)S(1)} %get-tuple-element.54), channel_id=1, source_target_pairs={{0,192},{32,224},{64,0},{96,32},{128,64},{160,96},{192,128},{224,1... | collective-permute-start | bytes 786440 | tf_op jit(solution)/shard_map/ppermute | solution.py:466
  53.5 0.6 copy-start.10
  53.5 0.7 copy-start.5
  65.1 1.2 %copy-start.3 = (bf16[16,64,512]{2,1,0:T(8,128)(2,1)S(1)}, bf16[16,64,512]{2,1,0:T(8,128)(2,1)}, u32[]{:S(2)}) copy-start(bf16[16,64,512]{2,1,0:T(8,128)(2,1)} %get-tuple-element.58) | copy-start | bytes 3145732
  65.2 4.8 %copy-start.1 = (bf16[16,64,512]{2,1,0:T(8,128)(2,1)S(1)}, bf16[16,64,512]{2,1,0:T(8,128)(2,1)}, u32[]{:S(2)}) copy-start(bf16[16,64,512]{2,1,0:T(8,128)(2,1)} %get-tuple-element.48) | copy-start | bytes 3145732
  66.4 3.6 %collective-permute-start.11 = (bf16[16,64,512]{2,1,0:T(8,128)(2,1)S(1)}, bf16[16,64,512]{2,1,0:T(8,128)(2,1)S(1)}, u32[]{:S(2)}, u32[]{:S(2)}) collective-permute-start(bf16[16,64,512]{2,1,0:T(8,128)(2,1)S(1)} %copy-done.3), channel_id=1, source_target_pairs={{0,1},{1,0},{2,3},{3,2},{4,5},{5,4},{6,7},{7,6},{8,9},{9,8},{10,11... | collective-permute-start | bytes 3145736 | tf_op jit(solution)/shard_map/ppermute | solution.py:444
  71.5 22.3 %all-to-all-start = ((bf16[8,512,128]{2,1,0:T(8,128)(2,1)}), bf16[8,512,128]{2,1,0:T(8,128)(2,1)S(1)}, u32[]{:S(2)}, u32[]{:S(2)}) async-start(bf16[8,512,128]{2,1,0:T(8,128)(2,1)} %core_sum.1), calls=%async_computation | async-start | bytes 2097152 | tf_op jit(solution)/shard_map/all_to_all | solution.py:475
  77.2 16.6 %collective-permute-start.12 = (bf16[512,128]{1,0:T(8,128)(2,1)S(1)}, bf16[512,128]{1,0:T(8,128)(2,1)S(1)}, u32[]{:S(2)}, u32[]{:S(2)}) collective-permute-start(bf16[512,128]{1,0:T(8,128)(2,1)S(1)} %get-tuple-element.60), channel_id=1, source_target_pairs={{0,32},{32,0},{64,96},{96,64},{128,160},{160,128},{192,224},{224,1... | collective-permute-start | bytes 393224 | tf_op jit(solution)/shard_map/ppermute | solution.py:474
  94.8 22.5 %all-to-all-start.1 = ((bf16[16,2,32,128]{3,2,1,0:T(8,128)(2,1)}), bf16[16,2,32,128]{3,2,1,0:T(8,128)(2,1)S(1)}, u32[]{:S(2)}, u32[]{:S(2)}) async-start(bf16[16,2,32,128]{3,2,1,0:T(8,128)(2,1)} %lat_sum.1), calls=%async_computation.1 | async-start | bytes 524288 | tf_op jit(solution)/shard_map/all_to_all | solution.py:478

commit v4 on v3

--- a/solution.py
+++ b/solution.py
@@ -437,7 +437,9 @@
 
 
 def exchanged(tall, side, corner, step):
-    return moved(tall, step, 0), moved(side, 0, step), moved(corner, step, step)
+    corner = moved(corner, step, step)
+    side = moved(side, 0, step)
+    return moved(tall, step, 0), side, corner
 
 
 def core_swapped(sent):
@@ -503,7 +505,7 @@
         flat, flat_g, qkv_weights, proj_weights, plain, cut, strips,
         fetch={4: None, 0: None, 2: 0, 3: 0, 5: None, 6: None, 1: None},
         store=(4, 5, 6, 7, 8),
-        limit=LARGE,
+        limit=58,
         micros=9,
     )
     tall, side, corner = exchanged(tall, side, corner, -1)
@@ -516,7 +518,7 @@
         scalar=True,
         fetch={5: None, 10: None, 8: 1, 9: None, 7: 1, 11: None},
         store=(4, 5),
-        limit=LARGE,
+        limit=51,
         micros=18,
     )
     tall, side, corner = exchanged(tall, side, corner, 1)
@@ -530,7 +532,7 @@
         scalar=True,
         fetch={6: None, 5: 0, 7: None, 8: None, 10: None, 9: None},
         store=(0, 1, 2, 3),
-        limit=LARGE,
+        limit=51,
         micros=10,
     )
     d_tokens = call(

time: 119 us -> 116 us (0.975)
  Pallas kernels: 44.9 us -> 41.9 us
  waiting for transfers between devices: 28.6 us -> 30.2 us
    pallas_call x9, Pallas kernels: 44.9 us -> 41.9 us  [call(): pl.pallas_call(body, out_shape=outs, in_specs=[pl.BlockSpec(memory_space=...]
    unnamed x22 -> x28, local copies, waits for them, and re-layouts: 3.83 us -> 3.55 us
  transfers between devices with their start and end apart: 15 -> 15, of which waited for: 5 -> 6; matrix products, arithmetic and copies ran while one was open for 1% -> 0% of each run, Pallas kernels for 21% -> 21%
where the time goes in v4:
time: 116 us; the launch traced here: 115 us
  Pallas kernels  41.9 us (36%)
  starting transfers between devices  37.8 us (33%)
  waiting for transfers between devices  30.2 us (26%)
  local copies, waits for them, and re-layouts  4.54 us (4%)
    pallas_call x9, Pallas kernels, call(): pl.pallas_call(body, out_shape=outs, in_specs=[pl.BlockSpec(memory_space=...  41.9 us
    ppermute x1, waiting for transfers between devices, reduced(): lax.ppermute(sent, 'lat', [(i, i ^ 1) for i in range(lax.axis_size('lat'))])  15.2 us
    all_to_all x1, starting transfers between devices, reduced(): lax.all_to_all(both, 'lon', 0, 0, tiled=True, axis_index_groups=groups)  9.87 us
    all_to_all x1, waiting for transfers between devices, reduced(): lax.all_to_all(both, 'lon', 0, 0, tiled=True, axis_index_groups=groups)  7.99 us
    ppermute x2, starting transfers between devices, moved(): lax.ppermute(piece, 'lon', [(i, (i + lon) % n_lon) for i in range(n_lon)])  5.73 us
    all_to_all x1, starting transfers between devices, reduced(): arrived = lax.all_to_all(chunks_one, 'lat', 0, 0, tiled=True)  5.69 us
    ppermute x3, starting transfers between devices, far_reduced(): lax.ppermute(parts[step], 'lat', [(i, (i + 2 * step) % n) for i in range(...  5.21 us
    ppermute x3, starting transfers between devices, moved(): lax.ppermute(piece, 'lat', [(i, (i + lat) % n_lat) for i in range(n_lat)])  4.3 us
  transfers between devices with their start and end apart: 15, of which 6 were waited for; matrix products, arithmetic and copies ran while one was open for 0% of the time, Pallas kernels for 21%

profile of v4, /device:TPU:2, one launch (start us, length us, event | category | flops | bytes accessed | tf_op | source)
XLA Modules:
  0.0 115.3 jit_solution(12695893343053180666)
XLA Ops:
  0.6 1.0 slice.3
  1.6 1.6 %collective-permute-start.3 = (bf16[288,512]{1,0:T(8,128)(2,1)S(1)}, bf16[288,512]{1,0:T(8,128)(2,1)S(1)}, u32[]{:S(2)}, u32[]{:S(2)}) collective-permute-start(bf16[288,512]{1,0:T(8,128)(2,1)S(1)} %bitcast.17), channel_id=1, source_target_pairs={{0,224},{32,0},{64,32},{96,64},{128,96},{160,128},{192,160},{224,1... | collective-permute-start | bytes 884744 | tf_op jit(solution)/shard_map/ppermute | solution.py:428
  3.2 0.0 copy-start.12
  3.2 0.0 copy-start.2
  3.2 0.0 copy-start.4
  3.3 0.0 copy-start.5
  3.3 8.3 %forward.1 = (bf16[256,512]{1,0:T(8,128)(2,1)}, bf16[256,512]{1,0:T(8,128)(2,1)}, bf16[128,512]{1,0:T(8,128)(2,1)}, bf16[128,512]{1,0:T(8,128)(2,1)}, bf16[576,5...) custom-call(bf16[576,512]{1,0:T(8,128)(2,1)} %bitcast.20, ...), custom_call_target="tpu_custom_call" | custom-call | flops 10350000128 | bytes 33210000 | tf_op jit(solution)/shard_map/forward/pallas_call | solution.py:411
  11.6 2.3 %collective-permute-start = (bf16[256,512]{1,0:T(8,128)(2,1)}, bf16[256,512]{1,0:T(8,128)(2,1)S(1)}, u32[]{:S(2)}, u32[]{:S(2)}) collective-permute-start(bf16[256,512]{1,0:T(8,128)(2,1)} %get-tuple-element.35), channel_id=1, source_target_pairs={{0,224},{32,0},{64,32},{96,64},{128,96},{160,128},{192,160},{224,1... | collective-permute-start | bytes 786440 | tf_op jit(solution)/shard_map/ppermute | solution.py:428
  13.8 5.6 %collective-permute-start.1 = (bf16[128,512]{1,0:T(8,128)(2,1)}, bf16[128,512]{1,0:T(8,128)(2,1)S(1)}, u32[]{:S(2)}, u32[]{:S(2)}) collective-permute-start(bf16[128,512]{1,0:T(8,128)(2,1)} %get-tuple-element.36), channel_id=1, source_target_pairs={{0,31},{1,0},{2,1},{3,2},{4,3},{5,4},{6,5},{7,6},{8,7},{9,8},{10,9... | collective-permute-start | bytes 393224 | tf_op jit(solution)/shard_map/ppermute | solution.py:430
  19.5 3.2 %collective-permute-start.2 = (bf16[128,512]{1,0:T(8,128)(2,1)}, bf16[128,512]{1,0:T(8,128)(2,1)S(1)}, u32[]{:S(2)}, u32[]{:S(2)}) collective-permute-start(bf16[128,512]{1,0:T(8,128)(2,1)} %get-tuple-element.37), channel_id=1, source_target_pairs={{0,255},{1,224},{2,225},{3,226},{4,227},{5,228},{6,229},{7,230},{8... | collective-permute-start | bytes 393224 | tf_op jit(solution)/shard_map/ppermute | solution.py:436
  22.7 0.0 copy-done.12
  22.8 0.0 collective-permute-done.1.refs_3_
  22.8 2.8 %collective-permute-done.2.refs_4_ = bf16[128,512]{1,0:T(8,128)(2,1)S(1)} collective-permute-done((bf16[128,512]{1,0:T(8,128)(2,1)}, bf16[128,512]{1,0:T(8,128)(2,1)S(1)}, u32[]{:S(2)}, u32[]{:S(2)}) %collective-permute-start.2) | collective-permute-done | bytes 131104 | tf_op jit(solution)/shard_map/ppermute | solution.py:436
  25.6 0.0 collective-permute-done.refs_2_
  25.6 0.0 collective-permute-done.3.refs_6_
  25.6 0.0 copy-done.2
  25.6 0.0 copy-done.4
  25.6 0.0 copy-done.5
  25.6 0.0 copy-start.9
  25.6 0.9 copy-done.9
  26.5 0.0 copy-start.3
  26.6 14.2 %backward_shifted.1 = (bf16[256,512]{1,0:T(8,128)(2,1)S(1)}, bf16[256,512]{1,0:T(8,128)(2,1)S(1)}, bf16[64,512]{1,0:T(8,128)(2,1)S(1)}, bf16[64,512]{1,0:T(8,128...) custom-call(s32[1]{0:T(128)} %bitcast.2.refs_0_, bf16[256,512]{1,0:T(8,128)(2,1)S(1)} %copy-done.9, ...), custom_call_target="tpu_custom_call" | custom-call | flops 20700000256 | bytes 66420000 | tf_op jit(solution)/shard_map/backward_shifted/pallas_call | solution.py:411
  40.7 0.0 copy-start.10
  40.8 0.7 copy-done.10
  41.5 0.0 collective-permute-start.7
  41.5 0.4 collective-permute-start.4
  41.9 0.1 collective-permute-start.5
  42.0 1.0 collective-permute-start.6
  43.0 1.3 %collective-permute-done.7 = bf16[16,64,512]{2,1,0:T(8,128)(2,1)S(1)} collective-permute-done((bf16[16,64,512]{2,1,0:T(8,128)(2,1)}, bf16[16,64,512]{2,1,0:T(8,128)(2,1)S(1)}, u32[]{:S(2)}, u32[]{:S(2)}) %collective-permute-start.7) | collective-permute-done | bytes 1048608 | tf_op jit(solution)/shard_map/ppermute | solution.py:446
  44.3 1.2 %copy-done = bf16[16,64,512]{2,1,0:T(8,128)(2,1)S(1)} copy-done((bf16[16,64,512]{2,1,0:T(8,128)(2,1)S(1)}, bf16[16,64,512]{2,1,0:T(8,128)(2,1)}, u32[]{:S(2)}) %copy-start) | copy-done | bytes 1048600
  45.6 0.9 core_cut.1
  46.5 0.7 collective-permute-start.10
  47.2 2.7 %collective-permute-start.8 = (bf16[2,512,128]{2,1,0:T(8,128)(2,1)S(1)}, bf16[2,512,128]{2,1,0:T(8,128)(2,1)S(1)}, u32[]{:S(2)}, u32[]{:S(2)}) collective-permute-start(bf16[2,512,128]{2,1,0:T(8,128)(2,1)S(1)} %get-tuple-element.53), channel_id=1, source_target_pairs={{0,128},{32,160},{64,192},{96,224},{128,0},{160,32},{192,64},{224,... | collective-permute-start | bytes 786440 | tf_op jit(solution)/shard_map/ppermute | solution.py:468
  49.9 0.0 collective-permute-done.5.refs_3_
  49.9 1.8 %collective-permute-start.9 = (bf16[2,512,128]{2,1,0:T(8,128)(2,1)S(1)}, bf16[2,512,128]{2,1,0:T(8,128)(2,1)S(1)}, u32[]{:S(2)}, u32[]{:S(2)}) collective-permute-start(bf16[2,512,128]{2,1,0:T(8,128)(2,1)S(1)} %get-tuple-element.54), channel_id=1, source_target_pairs={{0,192},{32,224},{64,0},{96,32},{128,64},{160,96},{192,128},{224,1... | collective-permute-start | bytes 786440 | tf_op jit(solution)/shard_map/ppermute | solution.py:468
  51.7 0.0 collective-permute-done.6.refs_4_
  51.7 0.0 collective-permute-done.4.refs_2_
  51.7 0.0 copy-done.3
  51.7 0.0 copy-done.7
  51.7 0.0 copy-done.8
  51.7 0.0 copy-done.11
  51.7 10.0 %backward_plain.1 = (bf16[576,512]{1,0:T(8,128)(2,1)S(1)}, bf16[576,1536]{1,0:T(8,128)(2,1)}, bf16[16,64,512]{2,1,0:T(8,128)(2,1)}, bf16[16,64,512]{2,1,0:T(8,128)(2,1)}) custom-call(s32[1]{0:T(128)} %bitcast.2.refs_0_, bf16[256,512]{1,0:T(8,128)(2,1)S(1)} %copy-done.11, bf16[256,512]{1,0:T(8,128)(2,1)S(1)} %collective-permute-done.4.refs_2_, ...), custom_call_target="tpu_custom_call" | custom-call | flops 11500000256 | bytes 36900000 | tf_op jit(solution)/shard_map/backward_plain/pallas_call | solution.py:411
  61.7 0.0 copy-start.6
  61.7 0.0 copy-start.13
  61.7 0.0 copy-start.1
  61.7 0.0 collective-permute-done.10.refs_4_
  61.7 0.0 collective-permute-done.8.refs_2_
  61.7 0.6 collective-permute-done.9.refs_3_
  62.3 0.1 far_sum.1
  62.5 0.6 copy-done.13
  63.1 1.3 %collective-permute-start.11 = (bf16[16,64,512]{2,1,0:T(8,128)(2,1)S(1)}, bf16[16,64,512]{2,1,0:T(8,128)(2,1)S(1)}, u32[]{:S(2)}, u32[]{:S(2)}) collective-permute-start(bf16[16,64,512]{2,1,0:T(8,128)(2,1)S(1)} %copy-done.13), channel_id=1, source_target_pairs={{0,1},{1,0},{2,3},{3,2},{4,5},{5,4},{6,7},{7,6},{8,9},{9,8},{10,11... | collective-permute-start | bytes 3145736 | tf_op jit(solution)/shard_map/ppermute | solution.py:446
  64.4 2.3 %collective-permute-done.11 = bf16[16,64,512]{2,1,0:T(8,128)(2,1)S(1)} collective-permute-done((bf16[16,64,512]{2,1,0:T(8,128)(2,1)S(1)}, bf16[16,64,512]{2,1,0:T(8,128)(2,1)S(1)}, u32[]{:S(2)}, u32[]{:S(2)}) %collective-permute-start.11) | collective-permute-done | bytes 1048608 | tf_op jit(solution)/shard_map/ppermute | solution.py:446
  66.7 0.0 copy-done.6
  66.7 0.0 copy-done.1
  66.7 1.6 %core_sum.1 = bf16[8,512,128]{2,1,0:T(8,128)(2,1)} custom-call(bf16[1024,512]{1,0:T(8,128)(2,1)S(1)} %bitcast.16, bf16[1024,512]{1,0:T(8,128)(2,1)S(1)} %bitcast.14), custom_call_target="tpu_custom_call" | custom-call | flops 1150000000 | bytes 3690000 | tf_op jit(solution)/shard_map/core_sum/pallas_call | solution.py:411
  68.3 5.7 %all-to-all-start = ((bf16[8,512,128]{2,1,0:T(8,128)(2,1)}), bf16[8,512,128]{2,1,0:T(8,128)(2,1)S(1)}, u32[]{:S(2)}, u32[]{:S(2)}) async-start(bf16[8,512,128]{2,1,0:T(8,128)(2,1)} %core_sum.1), calls=%async_computation | async-start | bytes 2097152 | tf_op jit(solution)/shard_map/all_to_all | solution.py:477
  74.0 1.5 %collective-permute-start.12 = (bf16[512,128]{1,0:T(8,128)(2,1)S(1)}, bf16[512,128]{1,0:T(8,128)(2,1)S(1)}, u32[]{:S(2)}, u32[]{:S(2)}) collective-permute-start(bf16[512,128]{1,0:T(8,128)(2,1)S(1)} %get-tuple-element.60), channel_id=1, source_target_pairs={{0,32},{32,0},{64,96},{96,64},{128,160},{160,128},{192,224},{224,1... | collective-permute-start | bytes 393224 | tf_op jit(solution)/shard_map/ppermute | solution.py:476
  75.5 15.2 %collective-permute-done.12.refs_2_ = bf16[512,128]{1,0:T(8,128)(2,1)S(1)} collective-permute-done((bf16[512,128]{1,0:T(8,128)(2,1)S(1)}, bf16[512,128]{1,0:T(8,128)(2,1)S(1)}, u32[]{:S(2)}, u32[]{:S(2)}) %collective-permute-start.12) | collective-permute-done | bytes 131104 | tf_op jit(solution)/shard_map/ppermute | solution.py:476
  90.7 0.0 all-to-all-done.refs_0_
  90.7 0.9 lat_sum.1
  91.6 9.9 %all-to-all-start.1 = ((bf16[16,2,32,128]{3,2,1,0:T(8,128)(2,1)}), bf16[16,2,32,128]{3,2,1,0:T(8,128)(2,1)S(1)}, u32[]{:S(2)}, u32[]{:S(2)}) async-start(bf16[16,2,32,128]{3,2,1,0:T(8,128)(2,1)} %lat_sum.1), calls=%async_computation.1 | async-start | bytes 524288 | tf_op jit(solution)/shard_map/all_to_all | solution.py:480
  101.5 5.1 %finish_plain.1 = bf16[576,512]{1,0:T(8,128)(2,1)} custom-call(bf16[576,512]{1,0:T(8,128)(2,1)} %get-tuple-element.33.refs_0_, bf16[576,512]{1,0:T(8,128)(2,1)} %copy-done.6, bf16[576,1536]{1,0:T(8,128)(2,1)} %get-tuple-element.47.refs_2_, bf16[2,512,1536]{2,1,0:T(8,128)(2,1)} %refs_3_.3, bf16[288,288]{1,0:T(8,128)(2,1)} %constant.62.clone.refs_4_), custom_call_target="tpu_custom_call" | custom-call | flops 5750000128 | bytes 18450000 | tf_op jit(solution)/shard_map/finish_plain/pallas_call | solution.py:411
  106.6 8.0 %all-to-all-done.1.refs_0_ = bf16[16,2,32,128]{3,2,1,0:T(8,128)(2,1)S(1)} async-done(((bf16[16,2,32,128]{3,2,1,0:T(8,128)(2,1)}), bf16[16,2,32,128]{3,2,1,0:T(8,128)(2,1)S(1)}, u32[]{:S(2)}, u32[]{:S(2)}) %all-to-all-start.1) | async-done | bytes 262176 | tf_op jit(solution)/shard_map/all_to_all | solution.py:480
  114.6 0.7 lon_sum.1
  (5 shorter events, 0.0 us)
Async XLA Ops:
  1.6 24.0 %collective-permute-start.3 = (bf16[288,512]{1,0:T(8,128)(2,1)S(1)}, bf16[288,512]{1,0:T(8,128)(2,1)S(1)}, u32[]{:S(2)}, u32[]{:S(2)}) collective-permute-start(bf16[288,512]{1,0:T(8,128)(2,1)S(1)} %bitcast.17), channel_id=1, source_target_pairs={{0,224},{32,0},{64,32},{96,64},{128,96},{160,128},{192,160},{224,1... | collective-permute-start | bytes 884744 | tf_op jit(solution)/shard_map/ppermute | solution.py:428
  3.2 19.5 %copy-start.12 = (pred[144,144]{1,0:T(8,128)(4,1)S(1)}, pred[144,144]{1,0:T(8,128)(4,1)}, u32[]{:S(2)}) copy-start(pred[144,144]{1,0:T(8,128)(4,1)} %constant.69.clone) | copy-start | bytes 62212
  3.2 22.3 %copy-start.2 = (bf16[320,288]{1,0:T(8,128)(2,1)S(1)}, bf16[320,288]{1,0:T(8,128)(2,1)}, u32[]{:S(2)}) copy-start(bf16[320,288]{1,0:T(8,128)(2,1)} %constant.66.clone.refs_11_) | copy-start | bytes 552964
  3.2 22.3 %copy-start.4 = (bf16[288,320]{1,0:T(8,128)(2,1)S(1)}, bf16[288,320]{1,0:T(8,128)(2,1)}, u32[]{:S(2)}) copy-start(bf16[288,320]{1,0:T(8,128)(2,1)} %constant.65.clone.refs_9_) | copy-start | bytes 552964
  3.3 22.3 %copy-start.5 = (bf16[288,352]{1,0:T(8,128)(2,1)S(1)}, bf16[288,352]{1,0:T(8,128)(2,1)}, u32[]{:S(2)}) copy-start(bf16[288,352]{1,0:T(8,128)(2,1)} %constant.67.clone.refs_10_) | copy-start | bytes 608260
  11.6 14.0 %collective-permute-start = (bf16[256,512]{1,0:T(8,128)(2,1)}, bf16[256,512]{1,0:T(8,128)(2,1)S(1)}, u32[]{:S(2)}, u32[]{:S(2)}) collective-permute-start(bf16[256,512]{1,0:T(8,128)(2,1)} %get-tuple-element.35), channel_id=1, source_target_pairs={{0,224},{32,0},{64,32},{96,64},{128,96},{160,128},{192,160},{224,1... | collective-permute-start | bytes 786440 | tf_op jit(solution)/shard_map/ppermute | solution.py:428
  13.8 8.9 %collective-permute-start.1 = (bf16[128,512]{1,0:T(8,128)(2,1)}, bf16[128,512]{1,0:T(8,128)(2,1)S(1)}, u32[]{:S(2)}, u32[]{:S(2)}) collective-permute-start(bf16[128,512]{1,0:T(8,128)(2,1)} %get-tuple-element.36), channel_id=1, source_target_pairs={{0,31},{1,0},{2,1},{3,2},{4,3},{5,4},{6,5},{7,6},{8,7},{9,8},{10,9... | collective-permute-start | bytes 393224 | tf_op jit(solution)/shard_map/ppermute | solution.py:430
  19.5 6.1 %collective-permute-start.2 = (bf16[128,512]{1,0:T(8,128)(2,1)}, bf16[128,512]{1,0:T(8,128)(2,1)S(1)}, u32[]{:S(2)}, u32[]{:S(2)}) collective-permute-start(bf16[128,512]{1,0:T(8,128)(2,1)} %get-tuple-element.37), channel_id=1, source_target_pairs={{0,255},{1,224},{2,225},{3,226},{4,227},{5,228},{6,229},{7,230},{8... | collective-permute-start | bytes 393224 | tf_op jit(solution)/shard_map/ppermute | solution.py:436
  25.6 1.0 copy-start.9
  26.5 25.1 %copy-start.3 = (bf16[288,320]{1,0:T(8,128)(2,1)S(1)}, bf16[288,320]{1,0:T(8,128)(2,1)}, u32[]{:S(2)}) copy-start(bf16[288,320]{1,0:T(8,128)(2,1)} %constant.63.clone.refs_6_) | copy-start | bytes 552964
  26.6 25.1 %copy-start.7 = (bf16[576,512]{1,0:T(8,128)(2,1)S(1)}, bf16[576,512]{1,0:T(8,128)(2,1)}, u32[]{:S(2)}) copy-start(bf16[576,512]{1,0:T(8,128)(2,1)} %get-tuple-element.45.refs_10_) | copy-start | bytes 1769476
  26.6 25.2 %copy-start.8 = (bf16[576,512]{1,0:T(8,128)(2,1)S(1)}, bf16[576,512]{1,0:T(8,128)(2,1)}, u32[]{:S(2)}) copy-start(bf16[576,512]{1,0:T(8,128)(2,1)} %get-tuple-element.44.refs_9_) | copy-start | bytes 1769476
  40.7 0.7 copy-start.10
  41.5 2.9 %collective-permute-start.7 = (bf16[16,64,512]{2,1,0:T(8,128)(2,1)}, bf16[16,64,512]{2,1,0:T(8,128)(2,1)S(1)}, u32[]{:S(2)}, u32[]{:S(2)}) collective-permute-start(bf16[16,64,512]{2,1,0:T(8,128)(2,1)} %get-tuple-element.51), channel_id=1, source_target_pairs={{0,1},{1,0},{2,3},{3,2},{4,5},{5,4},{6,7},{7,6},{8,9},{9,8},{10,11... | collective-permute-start | bytes 3145736 | tf_op jit(solution)/shard_map/ppermute | solution.py:446
  41.5 10.2 %collective-permute-start.4 = (bf16[256,512]{1,0:T(8,128)(2,1)S(1)}, bf16[256,512]{1,0:T(8,128)(2,1)S(1)}, u32[]{:S(2)}, u32[]{:S(2)}) collective-permute-start(bf16[256,512]{1,0:T(8,128)(2,1)S(1)} %get-tuple-element.39), channel_id=1, source_target_pairs={{0,32},{32,64},{64,96},{96,128},{128,160},{160,192},{192,224},{224... | collective-permute-start | bytes 786440 | tf_op jit(solution)/shard_map/ppermute | solution.py:428
  41.9 8.0 %collective-permute-start.5 = (bf16[64,512]{1,0:T(8,128)(2,1)S(1)}, bf16[64,512]{1,0:T(8,128)(2,1)S(1)}, u32[]{:S(2)}, u32[]{:S(2)}) collective-permute-start(bf16[64,512]{1,0:T(8,128)(2,1)S(1)} %get-tuple-element.40), channel_id=1, source_target_pairs={{0,1},{1,2},{2,3},{3,4},{4,5},{5,6},{6,7},{7,8},{8,9},{9,10},{10,1... | collective-permute-start | bytes 196616 | tf_op jit(solution)/shard_map/ppermute | solution.py:430
  42.0 9.7 %collective-permute-start.6 = (bf16[64,512]{1,0:T(8,128)(2,1)S(1)}, bf16[64,512]{1,0:T(8,128)(2,1)S(1)}, u32[]{:S(2)}, u32[]{:S(2)}) collective-permute-start(bf16[64,512]{1,0:T(8,128)(2,1)S(1)} %get-tuple-element.41), channel_id=1, source_target_pairs={{0,33},{1,34},{2,35},{3,36},{4,37},{5,38},{6,39},{7,40},{8,41},{9,... | collective-permute-start | bytes 196616 | tf_op jit(solution)/shard_map/ppermute | solution.py:436
  44.3 1.2 %copy-start = (bf16[16,64,512]{2,1,0:T(8,128)(2,1)S(1)}, bf16[16,64,512]{2,1,0:T(8,128)(2,1)}, u32[]{:S(2)}) copy-start(bf16[16,64,512]{2,1,0:T(8,128)(2,1)} %get-tuple-element.50) | copy-start | bytes 3145732
  45.6 6.2 %copy-start.11 = (bf16[256,512]{1,0:T(8,128)(2,1)S(1)}, bf16[256,512]{1,0:T(8,128)(2,1)}, u32[]{:S(2)}) copy-start(bf16[256,512]{1,0:T(8,128)(2,1)} %copy-done.10) | copy-start | bytes 786436
  46.5 15.3 %collective-permute-start.10 = (bf16[2,512,128]{2,1,0:T(8,128)(2,1)S(1)}, bf16[2,512,128]{2,1,0:T(8,128)(2,1)S(1)}, u32[]{:S(2)}, u32[]{:S(2)}) collective-permute-start(bf16[2,512,128]{2,1,0:T(8,128)(2,1)S(1)} %get-tuple-element.55), channel_id=1, source_target_pairs={{0,64},{32,96},{64,128},{96,160},{128,192},{160,224},{192,0},{224,... | collective-permute-start | bytes 786440 | tf_op jit(solution)/shard_map/ppermute | solution.py:468
  47.2 14.5 %collective-permute-start.8 = (bf16[2,512,128]{2,1,0:T(8,128)(2,1)S(1)}, bf16[2,512,128]{2,1,0:T(8,128)(2,1)S(1)}, u32[]{:S(2)}, u32[]{:S(2)}) collective-permute-start(bf16[2,512,128]{2,1,0:T(8,128)(2,1)S(1)} %get-tuple-element.53), channel_id=1, source_target_pairs={{0,128},{32,160},{64,192},{96,224},{128,0},{160,32},{192,64},{224,... | collective-permute-start | bytes 786440 | tf_op jit(solution)/shard_map/ppermute | solution.py:468
  49.9 12.4 %collective-permute-start.9 = (bf16[2,512,128]{2,1,0:T(8,128)(2,1)S(1)}, bf16[2,512,128]{2,1,0:T(8,128)(2,1)S(1)}, u32[]{:S(2)}, u32[]{:S(2)}) collective-permute-start(bf16[2,512,128]{2,1,0:T(8,128)(2,1)S(1)} %get-tuple-element.54), channel_id=1, source_target_pairs={{0,192},{32,224},{64,0},{96,32},{128,64},{160,96},{192,128},{224,1... | collective-permute-start | bytes 786440 | tf_op jit(solution)/shard_map/ppermute | solution.py:468
  61.7 5.0 %copy-start.6 = (bf16[576,512]{1,0:T(8,128)(2,1)}, bf16[576,512]{1,0:T(8,128)(2,1)S(1)}, u32[]{:S(2)}) copy-start(bf16[576,512]{1,0:T(8,128)(2,1)S(1)} %get-tuple-element.46.refs_1_) | copy-start | bytes 1769476
  61.7 1.4 %copy-start.13 = (bf16[16,64,512]{2,1,0:T(8,128)(2,1)S(1)}, bf16[16,64,512]{2,1,0:T(8,128)(2,1)}, u32[]{:S(2)}) copy-start(bf16[16,64,512]{2,1,0:T(8,128)(2,1)} %get-tuple-element.58) | copy-start | bytes 3145732
  61.7 5.0 %copy-start.1 = (bf16[16,64,512]{2,1,0:T(8,128)(2,1)S(1)}, bf16[16,64,512]{2,1,0:T(8,128)(2,1)}, u32[]{:S(2)}) copy-start(bf16[16,64,512]{2,1,0:T(8,128)(2,1)} %get-tuple-element.48) | copy-start | bytes 3145732
  63.1 3.6 %collective-permute-start.11 = (bf16[16,64,512]{2,1,0:T(8,128)(2,1)S(1)}, bf16[16,64,512]{2,1,0:T(8,128)(2,1)S(1)}, u32[]{:S(2)}, u32[]{:S(2)}) collective-permute-start(bf16[16,64,512]{2,1,0:T(8,128)(2,1)S(1)} %copy-done.13), channel_id=1, source_target_pairs={{0,1},{1,0},{2,3},{3,2},{4,5},{5,4},{6,7},{7,6},{8,9},{9,8},{10,11... | collective-permute-start | bytes 3145736 | tf_op jit(solution)/shard_map/ppermute | solution.py:446
  68.3 22.3 %all-to-all-start = ((bf16[8,512,128]{2,1,0:T(8,128)(2,1)}), bf16[8,512,128]{2,1,0:T(8,128)(2,1)S(1)}, u32[]{:S(2)}, u32[]{:S(2)}) async-start(bf16[8,512,128]{2,1,0:T(8,128)(2,1)} %core_sum.1), calls=%async_computation | async-start | bytes 2097152 | tf_op jit(solution)/shard_map/all_to_all | solution.py:477
  74.0 16.6 %collective-permute-start.12 = (bf16[512,128]{1,0:T(8,128)(2,1)S(1)}, bf16[512,128]{1,0:T(8,128)(2,1)S(1)}, u32[]{:S(2)}, u32[]{:S(2)}) collective-permute-start(bf16[512,128]{1,0:T(8,128)(2,1)S(1)} %get-tuple-element.60), channel_id=1, source_target_pairs={{0,32},{32,0},{64,96},{96,64},{128,160},{160,128},{192,224},{224,1... | collective-permute-start | bytes 393224 | tf_op jit(solution)/shard_map/ppermute | solution.py:476
  91.6 23.0 %all-to-all-start.1 = ((bf16[16,2,32,128]{3,2,1,0:T(8,128)(2,1)}), bf16[16,2,32,128]{3,2,1,0:T(8,128)(2,1)S(1)}, u32[]{:S(2)}, u32[]{:S(2)}) async-start(bf16[16,2,32,128]{3,2,1,0:T(8,128)(2,1)} %lat_sum.1), calls=%async_computation.1 | async-start | bytes 524288 | tf_op jit(solution)/shard_map/all_to_all | solution.py:480

commit v5 on v4

--- a/solution.py
+++ b/solution.py
@@ -471,15 +471,17 @@
     return kept, sent
 
 
-def reduced(chunks_one, parts_two):
+def reduced(chunks_one, parts_two, d_tokens):
     kept, sent = parts_two
     received = lax.ppermute(sent, "lat", [(i, i ^ 1) for i in range(lax.axis_size("lat"))])
+    chunks_one, received = lax.optimization_barrier((chunks_one, received))
     arrived = lax.all_to_all(chunks_one, "lat", 0, 0, tiled=True)
+    arrived, d_tokens = lax.optimization_barrier((arrived, d_tokens))
     both = call(lat_sum_kernel, "lat_sum", shape(16, 2, 32, 128), arrived, kept, received)
     groups = [[2 * j + core for j in range(16)] for core in range(2)]
     arrived = lax.all_to_all(both, "lon", 0, 0, tiled=True, axis_index_groups=groups)
     grads = call(lon_sum_kernel, "lon_sum", (shape(2, 48, 64, kind=F32), shape(2, 16, 64, kind=F32)), arrived)
-    return [grad.transpose(0, 2, 1) for grad in grads]
+    return d_tokens, *[grad.transpose(0, 2, 1) for grad in grads]
 
 
 def body(tokens, cotangent, qkv_weights, proj_weights):
@@ -545,7 +547,8 @@
         micros=5,
     )
     sent_one, parts_two = lax.optimization_barrier((sent_one, parts_two))
-    grad_qkv, grad_proj = reduced(core_reduced(kept_one, sent_one), parts_two)
+    chunks_one = core_reduced(kept_one, sent_one)
+    d_tokens, grad_qkv, grad_proj = reduced(chunks_one, parts_two, d_tokens)
     return d_tokens.reshape(tokens.shape), grad_qkv, grad_proj
 
 

time: 116 us -> 114 us (0.983)
  blocking collectives: 0 us -> 23.7 us
  waiting for transfers between devices: 30.2 us -> 17.1 us
  starting transfers between devices: 37.8 us -> 26.5 us
    all_to_all x0 -> x1, blocking collectives: none -> 23.7 us  [reduced(): lax.all_to_all(both, 'lon', 0, 0, tiled=True, axis_index_groups=groups)]
    ppermute x1, waiting for transfers between devices: 15.2 us -> 1.51 us  [reduced(): lax.ppermute(sent, 'lat', [(i, i ^ 1) for i in range(lax.axis_size('lat'))])]
    all_to_all x1 -> x0, starting transfers between devices: 9.87 us -> none  [reduced(): lax.all_to_all(both, 'lon', 0, 0, tiled=True, axis_index_groups=groups)]
    all_to_all x1, waiting for transfers between devices: 0.01 us -> 8.6 us  [reduced(): arrived = lax.all_to_all(chunks_one, 'lat', 0, 0, tiled=True)]
    all_to_all x1 -> x0, waiting for transfers between devices: 7.99 us -> none  [reduced(): lax.all_to_all(both, 'lon', 0, 0, tiled=True, axis_index_groups=groups)]
    ppermute x1, starting transfers between devices: 1.47 us -> 0.01 us  [reduced(): lax.ppermute(sent, 'lat', [(i, i ^ 1) for i in range(lax.axis_size('lat'))])]
  transfers between devices with their start and end apart: 15 -> 14, of which waited for: 6 -> 6; matrix products, arithmetic and copies ran while one was open for 0% -> 0% of each run, Pallas kernels for 21% -> 23%
where the time goes in v5:
time: 114 us
  Pallas kernels  41.2 us (36%)
  starting transfers between devices  26.5 us (23%)
  blocking collectives  23.7 us (21%)
  waiting for transfers between devices  17.1 us (15%)
  local copies, waits for them, and re-layouts  4.54 us (4%)
    pallas_call x9, Pallas kernels, call(): pl.pallas_call(body, out_shape=outs, in_specs=[pl.BlockSpec(memory_space=...  41.2 us
    all_to_all x1, blocking collectives, reduced(): lax.all_to_all(both, 'lon', 0, 0, tiled=True, axis_index_groups=groups)  23.7 us
    all_to_all x1, waiting for transfers between devices, reduced(): arrived = lax.all_to_all(chunks_one, 'lat', 0, 0, tiled=True)  8.6 us
    ppermute x2, starting transfers between devices, moved(): lax.ppermute(piece, 'lon', [(i, (i + lon) % n_lon) for i in range(n_lon)])  5.73 us
    all_to_all x1, starting transfers between devices, reduced(): arrived = lax.all_to_all(chunks_one, 'lat', 0, 0, tiled=True)  5.67 us
    ppermute x3, starting transfers between devices, far_reduced(): lax.ppermute(parts[step], 'lat', [(i, (i + 2 * step) % n) for i in range(...  5.22 us
    ppermute x3, starting transfers between devices, moved(): lax.ppermute(piece, 'lat', [(i, (i + lat) % n_lat) for i in range(n_lat)])  4.3 us
    ppermute x2, starting transfers between devices, moved(): return lax.ppermute(piece, ('lat', 'lon'), route)  4.28 us
  transfers between devices with their start and end apart: 14, of which 6 were waited for; matrix products, arithmetic and copies ran while one was open for 0% of the time, Pallas kernels for 23%

profile of v5, /device:TPU:2, one launch (start us, length us, event | category | flops | bytes accessed | tf_op | source)
XLA Modules:
  0.0 113.9 jit_solution(10839409977399013795)
XLA Ops:
  0.6 1.0 slice.3
  1.6 1.6 %collective-permute-start.3 = (bf16[288,512]{1,0:T(8,128)(2,1)S(1)}, bf16[288,512]{1,0:T(8,128)(2,1)S(1)}, u32[]{:S(2)}, u32[]{:S(2)}) collective-permute-start(bf16[288,512]{1,0:T(8,128)(2,1)S(1)} %bitcast.17), channel_id=1, source_target_pairs={{0,224},{32,0},{64,32},{96,64},{128,96},{160,128},{192,160},{224,1... | collective-permute-start | bytes 884744 | tf_op jit(solution)/shard_map/ppermute | solution.py:428
  3.2 0.0 copy-start.12
  3.2 0.0 copy-start.2
  3.2 0.0 copy-start.4
  3.3 0.0 copy-start.5
  3.3 8.3 %forward.1 = (bf16[256,512]{1,0:T(8,128)(2,1)}, bf16[256,512]{1,0:T(8,128)(2,1)}, bf16[128,512]{1,0:T(8,128)(2,1)}, bf16[128,512]{1,0:T(8,128)(2,1)}, bf16[576,5...) custom-call(bf16[576,512]{1,0:T(8,128)(2,1)} %bitcast.20, ...), custom_call_target="tpu_custom_call" | custom-call | flops 10350000128 | bytes 33210000 | tf_op jit(solution)/shard_map/forward/pallas_call | solution.py:411
  11.6 2.3 %collective-permute-start = (bf16[256,512]{1,0:T(8,128)(2,1)}, bf16[256,512]{1,0:T(8,128)(2,1)S(1)}, u32[]{:S(2)}, u32[]{:S(2)}) collective-permute-start(bf16[256,512]{1,0:T(8,128)(2,1)} %get-tuple-element.38), channel_id=1, source_target_pairs={{0,224},{32,0},{64,32},{96,64},{128,96},{160,128},{192,160},{224,1... | collective-permute-start | bytes 786440 | tf_op jit(solution)/shard_map/ppermute | solution.py:428
  13.8 5.6 %collective-permute-start.1 = (bf16[128,512]{1,0:T(8,128)(2,1)}, bf16[128,512]{1,0:T(8,128)(2,1)S(1)}, u32[]{:S(2)}, u32[]{:S(2)}) collective-permute-start(bf16[128,512]{1,0:T(8,128)(2,1)} %get-tuple-element.39), channel_id=1, source_target_pairs={{0,31},{1,0},{2,1},{3,2},{4,3},{5,4},{6,5},{7,6},{8,7},{9,8},{10,9... | collective-permute-start | bytes 393224 | tf_op jit(solution)/shard_map/ppermute | solution.py:430
  19.5 3.2 %collective-permute-start.2 = (bf16[128,512]{1,0:T(8,128)(2,1)}, bf16[128,512]{1,0:T(8,128)(2,1)S(1)}, u32[]{:S(2)}, u32[]{:S(2)}) collective-permute-start(bf16[128,512]{1,0:T(8,128)(2,1)} %get-tuple-element.40), channel_id=1, source_target_pairs={{0,255},{1,224},{2,225},{3,226},{4,227},{5,228},{6,229},{7,230},{8... | collective-permute-start | bytes 393224 | tf_op jit(solution)/shard_map/ppermute | solution.py:436
  22.7 0.0 copy-done.12
  22.7 0.0 collective-permute-done.1.refs_3_
  22.8 2.8 %collective-permute-done.2.refs_4_ = bf16[128,512]{1,0:T(8,128)(2,1)S(1)} collective-permute-done((bf16[128,512]{1,0:T(8,128)(2,1)}, bf16[128,512]{1,0:T(8,128)(2,1)S(1)}, u32[]{:S(2)}, u32[]{:S(2)}) %collective-permute-start.2) | collective-permute-done | bytes 131104 | tf_op jit(solution)/shard_map/ppermute | solution.py:436
  25.6 0.0 collective-permute-done.refs_2_
  25.6 0.0 collective-permute-done.3.refs_6_
  25.6 0.0 copy-done.2
  25.6 0.0 copy-done.4
  25.6 0.0 copy-done.5
  25.6 0.0 copy-start.9
  25.6 0.9 copy-done.9
  26.5 0.0 copy-start.3
  26.5 0.0 copy-start.7
  26.5 14.2 %backward_shifted.1 = (bf16[256,512]{1,0:T(8,128)(2,1)S(1)}, bf16[256,512]{1,0:T(8,128)(2,1)S(1)}, bf16[64,512]{1,0:T(8,128)(2,1)S(1)}, bf16[64,512]{1,0:T(8,128...) custom-call(s32[1]{0:T(128)} %bitcast.refs_0_, bf16[256,512]{1,0:T(8,128)(2,1)S(1)} %copy-done.9, ...), custom_call_target="tpu_custom_call" | custom-call | flops 20700000256 | bytes 66420000 | tf_op jit(solution)/shard_map/backward_shifted/pallas_call | solution.py:411
  40.7 0.0 copy-start.10
  40.7 0.7 copy-done.10
  41.4 0.0 collective-permute-start.7
  41.4 0.4 collective-permute-start.4
  41.8 0.1 collective-permute-start.5
  41.9 1.0 collective-permute-start.6
  43.0 1.3 %collective-permute-done.7 = bf16[16,64,512]{2,1,0:T(8,128)(2,1)S(1)} collective-permute-done((bf16[16,64,512]{2,1,0:T(8,128)(2,1)}, bf16[16,64,512]{2,1,0:T(8,128)(2,1)S(1)}, u32[]{:S(2)}, u32[]{:S(2)}) %collective-permute-start.7) | collective-permute-done | bytes 1048608 | tf_op jit(solution)/shard_map/ppermute | solution.py:446
  44.3 1.2 %copy-done = bf16[16,64,512]{2,1,0:T(8,128)(2,1)S(1)} copy-done((bf16[16,64,512]{2,1,0:T(8,128)(2,1)S(1)}, bf16[16,64,512]{2,1,0:T(8,128)(2,1)}, u32[]{:S(2)}) %copy-start) | copy-done | bytes 1048600
  45.5 0.9 core_cut.1
  46.4 0.7 collective-permute-start.10
  47.2 2.7 %collective-permute-start.8 = (bf16[2,512,128]{2,1,0:T(8,128)(2,1)S(1)}, bf16[2,512,128]{2,1,0:T(8,128)(2,1)S(1)}, u32[]{:S(2)}, u32[]{:S(2)}) collective-permute-start(bf16[2,512,128]{2,1,0:T(8,128)(2,1)S(1)} %get-tuple-element.54), channel_id=1, source_target_pairs={{0,128},{32,160},{64,192},{96,224},{128,0},{160,32},{192,64},{224,... | collective-permute-start | bytes 786440 | tf_op jit(solution)/shard_map/ppermute | solution.py:468
  49.9 0.0 collective-permute-done.5.refs_3_
  49.9 1.8 %collective-permute-start.9 = (bf16[2,512,128]{2,1,0:T(8,128)(2,1)S(1)}, bf16[2,512,128]{2,1,0:T(8,128)(2,1)S(1)}, u32[]{:S(2)}, u32[]{:S(2)}) collective-permute-start(bf16[2,512,128]{2,1,0:T(8,128)(2,1)S(1)} %get-tuple-element.55), channel_id=1, source_target_pairs={{0,192},{32,224},{64,0},{96,32},{128,64},{160,96},{192,128},{224,1... | collective-permute-start | bytes 786440 | tf_op jit(solution)/shard_map/ppermute | solution.py:468
  51.7 0.0 collective-permute-done.6.refs_4_
  51.7 0.0 collective-permute-done.4.refs_2_
  51.7 0.0 copy-done.3
  51.7 0.0 copy-done.7
  51.7 0.0 copy-done.8
  51.7 0.0 copy-done.11
  51.7 10.0 %backward_plain.1 = (bf16[576,512]{1,0:T(8,128)(2,1)S(1)}, bf16[576,1536]{1,0:T(8,128)(2,1)}, bf16[16,64,512]{2,1,0:T(8,128)(2,1)}, bf16[16,64,512]{2,1,0:T(8,128)(2,1)}) custom-call(s32[1]{0:T(128)} %bitcast.refs_0_, bf16[256,512]{1,0:T(8,128)(2,1)S(1)} %copy-done.11, bf16[256,512]{1,0:T(8,128)(2,1)S(1)} %collective-permute-done.4.refs_2_, ...), custom_call_target="tpu_custom_call" | custom-call | flops 11500000256 | bytes 36900000 | tf_op jit(solution)/shard_map/backward_plain/pallas_call | solution.py:411
  61.7 0.0 copy-start.6
  61.7 0.0 copy-start.13
  61.7 0.0 copy-start.1
  61.7 0.0 collective-permute-done.10.refs_4_
  61.7 0.0 collective-permute-done.8.refs_2_
  61.7 0.6 collective-permute-done.9.refs_3_
  62.3 0.1 far_sum.1
  62.5 0.7 copy-done.13
  63.1 1.3 %collective-permute-start.11 = (bf16[16,64,512]{2,1,0:T(8,128)(2,1)S(1)}, bf16[16,64,512]{2,1,0:T(8,128)(2,1)S(1)}, u32[]{:S(2)}, u32[]{:S(2)}) collective-permute-start(bf16[16,64,512]{2,1,0:T(8,128)(2,1)S(1)} %copy-done.13), channel_id=1, source_target_pairs={{0,1},{1,0},{2,3},{3,2},{4,5},{5,4},{6,7},{7,6},{8,9},{9,8},{10,11... | collective-permute-start | bytes 3145736 | tf_op jit(solution)/shard_map/ppermute | solution.py:446
  64.4 0.0 collective-permute-start.12
  64.4 2.3 %collective-permute-done.11 = bf16[16,64,512]{2,1,0:T(8,128)(2,1)S(1)} collective-permute-done((bf16[16,64,512]{2,1,0:T(8,128)(2,1)S(1)}, bf16[16,64,512]{2,1,0:T(8,128)(2,1)S(1)}, u32[]{:S(2)}, u32[]{:S(2)}) %collective-permute-start.11) | collective-permute-done | bytes 1048608 | tf_op jit(solution)/shard_map/ppermute | solution.py:446
  66.7 0.0 copy-done.1
  66.7 1.6 %core_sum.1 = bf16[8,512,128]{2,1,0:T(8,128)(2,1)} custom-call(bf16[1024,512]{1,0:T(8,128)(2,1)S(1)} %bitcast.16, bf16[1024,512]{1,0:T(8,128)(2,1)S(1)} %bitcast.14), custom_call_target="tpu_custom_call" | custom-call | flops 1150000000 | bytes 3690000 | tf_op jit(solution)/shard_map/core_sum/pallas_call | solution.py:411
  68.3 0.0 copy-done.6
  68.3 1.5 %collective-permute-done.12.refs_2_ = bf16[512,128]{1,0:T(8,128)(2,1)S(1)} collective-permute-done((bf16[512,128]{1,0:T(8,128)(2,1)S(1)}, bf16[512,128]{1,0:T(8,128)(2,1)S(1)}, u32[]{:S(2)}, u32[]{:S(2)}) %collective-permute-start.12) | collective-permute-done | bytes 131104 | tf_op jit(solution)/shard_map/ppermute | solution.py:476
  69.8 5.7 %all-to-all-start = ((bf16[8,512,128]{2,1,0:T(8,128)(2,1)}), bf16[8,512,128]{2,1,0:T(8,128)(2,1)S(1)}, u32[]{:S(2)}, u32[]{:S(2)}) async-start(bf16[8,512,128]{2,1,0:T(8,128)(2,1)} %core_sum.1), calls=%async_computation | async-start | bytes 2097152 | tf_op jit(solution)/shard_map/all_to_all | solution.py:478
  75.5 5.1 %finish_plain.1 = bf16[576,512]{1,0:T(8,128)(2,1)} custom-call(bf16[576,512]{1,0:T(8,128)(2,1)} %get-tuple-element.62.refs_0_, bf16[576,512]{1,0:T(8,128)(2,1)} %copy-done.6, bf16[576,1536]{1,0:T(8,128)(2,1)} %get-tuple-element.64.refs_2_, bf16[2,512,1536]{2,1,0:T(8,128)(2,1)} %refs_3_.3, bf16[288,288]{1,0:T(8,128)(2,1)} %constant.62.clone.refs_4_), custom_call_target="tpu_custom_call" | custom-call | flops 5750000128 | bytes 18450000 | tf_op jit(solution)/shard_map/finish_plain/pallas_call | solution.py:411
  80.6 8.6 %all-to-all-done.refs_0_ = bf16[8,512,128]{2,1,0:T(8,128)(2,1)S(1)} async-done(((bf16[8,512,128]{2,1,0:T(8,128)(2,1)}), bf16[8,512,128]{2,1,0:T(8,128)(2,1)S(1)}, u32[]{:S(2)}, u32[]{:S(2)}) %all-to-all-start) | async-done | bytes 1048608 | tf_op jit(solution)/shard_map/all_to_all | solution.py:478
  89.2 0.2 lat_sum.1
  89.5 23.7 %all_to_all.10.refs_0_ = bf16[16,2,32,128]{3,2,1,0:T(8,128)(2,1)S(1)} all-to-all(bf16[16,2,32,128]{3,2,1,0:T(8,128)(2,1)S(1)} %lat_sum.1), channel_id=1, replica_groups={{0,2,4,6,8,10,12,14,16,18,20,22,24,26,28,30},{1,3,5,7,9,11,13,15,17,19,..., dimensions={0} | all-to-all | bytes 524288 | tf_op jit(solution)/shard_map/all_to_all | solution.py:482
  113.2 0.7 lon_sum.1
  (4 shorter events, 0.0 us)
Async XLA Ops:
  1.6 23.9 %collective-permute-start.3 = (bf16[288,512]{1,0:T(8,128)(2,1)S(1)}, bf16[288,512]{1,0:T(8,128)(2,1)S(1)}, u32[]{:S(2)}, u32[]{:S(2)}) collective-permute-start(bf16[288,512]{1,0:T(8,128)(2,1)S(1)} %bitcast.17), channel_id=1, source_target_pairs={{0,224},{32,0},{64,32},{96,64},{128,96},{160,128},{192,160},{224,1... | collective-permute-start | bytes 884744 | tf_op jit(solution)/shard_map/ppermute | solution.py:428
  3.2 19.5 %copy-start.12 = (pred[144,144]{1,0:T(8,128)(4,1)S(1)}, pred[144,144]{1,0:T(8,128)(4,1)}, u32[]{:S(2)}) copy-start(pred[144,144]{1,0:T(8,128)(4,1)} %constant.69.clone) | copy-start | bytes 62212
  3.2 22.3 %copy-start.2 = (bf16[320,288]{1,0:T(8,128)(2,1)S(1)}, bf16[320,288]{1,0:T(8,128)(2,1)}, u32[]{:S(2)}) copy-start(bf16[320,288]{1,0:T(8,128)(2,1)} %constant.66.clone.refs_11_) | copy-start | bytes 552964
  3.2 22.3 %copy-start.4 = (bf16[288,320]{1,0:T(8,128)(2,1)S(1)}, bf16[288,320]{1,0:T(8,128)(2,1)}, u32[]{:S(2)}) copy-start(bf16[288,320]{1,0:T(8,128)(2,1)} %constant.65.clone.refs_9_) | copy-start | bytes 552964
  3.3 22.3 %copy-start.5 = (bf16[288,352]{1,0:T(8,128)(2,1)S(1)}, bf16[288,352]{1,0:T(8,128)(2,1)}, u32[]{:S(2)}) copy-start(bf16[288,352]{1,0:T(8,128)(2,1)} %constant.67.clone.refs_10_) | copy-start | bytes 608260
  11.6 14.0 %collective-permute-start = (bf16[256,512]{1,0:T(8,128)(2,1)}, bf16[256,512]{1,0:T(8,128)(2,1)S(1)}, u32[]{:S(2)}, u32[]{:S(2)}) collective-permute-start(bf16[256,512]{1,0:T(8,128)(2,1)} %get-tuple-element.38), channel_id=1, source_target_pairs={{0,224},{32,0},{64,32},{96,64},{128,96},{160,128},{192,160},{224,1... | collective-permute-start | bytes 786440 | tf_op jit(solution)/shard_map/ppermute | solution.py:428
  13.8 8.9 %collective-permute-start.1 = (bf16[128,512]{1,0:T(8,128)(2,1)}, bf16[128,512]{1,0:T(8,128)(2,1)S(1)}, u32[]{:S(2)}, u32[]{:S(2)}) collective-permute-start(bf16[128,512]{1,0:T(8,128)(2,1)} %get-tuple-element.39), channel_id=1, source_target_pairs={{0,31},{1,0},{2,1},{3,2},{4,3},{5,4},{6,5},{7,6},{8,7},{9,8},{10,9... | collective-permute-start | bytes 393224 | tf_op jit(solution)/shard_map/ppermute | solution.py:430
  19.5 6.1 %collective-permute-start.2 = (bf16[128,512]{1,0:T(8,128)(2,1)}, bf16[128,512]{1,0:T(8,128)(2,1)S(1)}, u32[]{:S(2)}, u32[]{:S(2)}) collective-permute-start(bf16[128,512]{1,0:T(8,128)(2,1)} %get-tuple-element.40), channel_id=1, source_target_pairs={{0,255},{1,224},{2,225},{3,226},{4,227},{5,228},{6,229},{7,230},{8... | collective-permute-start | bytes 393224 | tf_op jit(solution)/shard_map/ppermute | solution.py:436
  25.6 1.0 copy-start.9
  26.5 25.1 %copy-start.3 = (bf16[288,320]{1,0:T(8,128)(2,1)S(1)}, bf16[288,320]{1,0:T(8,128)(2,1)}, u32[]{:S(2)}) copy-start(bf16[288,320]{1,0:T(8,128)(2,1)} %constant.63.clone.refs_6_) | copy-start | bytes 552964
  26.5 25.1 %copy-start.7 = (bf16[576,512]{1,0:T(8,128)(2,1)S(1)}, bf16[576,512]{1,0:T(8,128)(2,1)}, u32[]{:S(2)}) copy-start(bf16[576,512]{1,0:T(8,128)(2,1)} %get-tuple-element.48.refs_10_) | copy-start | bytes 1769476
  26.5 25.1 %copy-start.8 = (bf16[576,512]{1,0:T(8,128)(2,1)S(1)}, bf16[576,512]{1,0:T(8,128)(2,1)}, u32[]{:S(2)}) copy-start(bf16[576,512]{1,0:T(8,128)(2,1)} %get-tuple-element.47.refs_9_) | copy-start | bytes 1769476
  40.7 0.7 copy-start.10
  41.4 2.9 %collective-permute-start.7 = (bf16[16,64,512]{2,1,0:T(8,128)(2,1)}, bf16[16,64,512]{2,1,0:T(8,128)(2,1)S(1)}, u32[]{:S(2)}, u32[]{:S(2)}) collective-permute-start(bf16[16,64,512]{2,1,0:T(8,128)(2,1)} %get-tuple-element.52), channel_id=1, source_target_pairs={{0,1},{1,0},{2,3},{3,2},{4,5},{5,4},{6,7},{7,6},{8,9},{9,8},{10,11... | collective-permute-start | bytes 3145736 | tf_op jit(solution)/shard_map/ppermute | solution.py:446
  41.4 10.2 %collective-permute-start.4 = (bf16[256,512]{1,0:T(8,128)(2,1)S(1)}, bf16[256,512]{1,0:T(8,128)(2,1)S(1)}, u32[]{:S(2)}, u32[]{:S(2)}) collective-permute-start(bf16[256,512]{1,0:T(8,128)(2,1)S(1)} %get-tuple-element.42), channel_id=1, source_target_pairs={{0,32},{32,64},{64,96},{96,128},{128,160},{160,192},{192,224},{224... | collective-permute-start | bytes 786440 | tf_op jit(solution)/shard_map/ppermute | solution.py:428
  41.8 8.0 %collective-permute-start.5 = (bf16[64,512]{1,0:T(8,128)(2,1)S(1)}, bf16[64,512]{1,0:T(8,128)(2,1)S(1)}, u32[]{:S(2)}, u32[]{:S(2)}) collective-permute-start(bf16[64,512]{1,0:T(8,128)(2,1)S(1)} %get-tuple-element.43), channel_id=1, source_target_pairs={{0,1},{1,2},{2,3},{3,4},{4,5},{5,6},{6,7},{7,8},{8,9},{9,10},{10,1... | collective-permute-start | bytes 196616 | tf_op jit(solution)/shard_map/ppermute | solution.py:430
  41.9 9.7 %collective-permute-start.6 = (bf16[64,512]{1,0:T(8,128)(2,1)S(1)}, bf16[64,512]{1,0:T(8,128)(2,1)S(1)}, u32[]{:S(2)}, u32[]{:S(2)}) collective-permute-start(bf16[64,512]{1,0:T(8,128)(2,1)S(1)} %get-tuple-element.44), channel_id=1, source_target_pairs={{0,33},{1,34},{2,35},{3,36},{4,37},{5,38},{6,39},{7,40},{8,41},{9,... | collective-permute-start | bytes 196616 | tf_op jit(solution)/shard_map/ppermute | solution.py:436
  44.3 1.2 %copy-start = (bf16[16,64,512]{2,1,0:T(8,128)(2,1)S(1)}, bf16[16,64,512]{2,1,0:T(8,128)(2,1)}, u32[]{:S(2)}) copy-start(bf16[16,64,512]{2,1,0:T(8,128)(2,1)} %get-tuple-element.51) | copy-start | bytes 3145732
  45.5 6.2 %copy-start.11 = (bf16[256,512]{1,0:T(8,128)(2,1)S(1)}, bf16[256,512]{1,0:T(8,128)(2,1)}, u32[]{:S(2)}) copy-start(bf16[256,512]{1,0:T(8,128)(2,1)} %copy-done.10) | copy-start | bytes 786436
  46.4 15.3 %collective-permute-start.10 = (bf16[2,512,128]{2,1,0:T(8,128)(2,1)S(1)}, bf16[2,512,128]{2,1,0:T(8,128)(2,1)S(1)}, u32[]{:S(2)}, u32[]{:S(2)}) collective-permute-start(bf16[2,512,128]{2,1,0:T(8,128)(2,1)S(1)} %get-tuple-element.56), channel_id=1, source_target_pairs={{0,64},{32,96},{64,128},{96,160},{128,192},{160,224},{192,0},{224,... | collective-permute-start | bytes 786440 | tf_op jit(solution)/shard_map/ppermute | solution.py:468
  47.2 14.5 %collective-permute-start.8 = (bf16[2,512,128]{2,1,0:T(8,128)(2,1)S(1)}, bf16[2,512,128]{2,1,0:T(8,128)(2,1)S(1)}, u32[]{:S(2)}, u32[]{:S(2)}) collective-permute-start(bf16[2,512,128]{2,1,0:T(8,128)(2,1)S(1)} %get-tuple-element.54), channel_id=1, source_target_pairs={{0,128},{32,160},{64,192},{96,224},{128,0},{160,32},{192,64},{224,... | collective-permute-start | bytes 786440 | tf_op jit(solution)/shard_map/ppermute | solution.py:468
  49.9 12.4 %collective-permute-start.9 = (bf16[2,512,128]{2,1,0:T(8,128)(2,1)S(1)}, bf16[2,512,128]{2,1,0:T(8,128)(2,1)S(1)}, u32[]{:S(2)}, u32[]{:S(2)}) collective-permute-start(bf16[2,512,128]{2,1,0:T(8,128)(2,1)S(1)} %get-tuple-element.55), channel_id=1, source_target_pairs={{0,192},{32,224},{64,0},{96,32},{128,64},{160,96},{192,128},{224,1... | collective-permute-start | bytes 786440 | tf_op jit(solution)/shard_map/ppermute | solution.py:468
  61.7 6.6 %copy-start.6 = (bf16[576,512]{1,0:T(8,128)(2,1)}, bf16[576,512]{1,0:T(8,128)(2,1)S(1)}, u32[]{:S(2)}) copy-start(bf16[576,512]{1,0:T(8,128)(2,1)S(1)} %get-tuple-element.63.refs_1_) | copy-start | bytes 1769476
  61.7 1.4 %copy-start.13 = (bf16[16,64,512]{2,1,0:T(8,128)(2,1)S(1)}, bf16[16,64,512]{2,1,0:T(8,128)(2,1)}, u32[]{:S(2)}) copy-start(bf16[16,64,512]{2,1,0:T(8,128)(2,1)} %get-tuple-element.59) | copy-start | bytes 3145732
  61.7 5.0 %copy-start.1 = (bf16[16,64,512]{2,1,0:T(8,128)(2,1)S(1)}, bf16[16,64,512]{2,1,0:T(8,128)(2,1)}, u32[]{:S(2)}) copy-start(bf16[16,64,512]{2,1,0:T(8,128)(2,1)} %get-tuple-element.49) | copy-start | bytes 3145732
  63.1 3.6 %collective-permute-start.11 = (bf16[16,64,512]{2,1,0:T(8,128)(2,1)S(1)}, bf16[16,64,512]{2,1,0:T(8,128)(2,1)S(1)}, u32[]{:S(2)}, u32[]{:S(2)}) collective-permute-start(bf16[16,64,512]{2,1,0:T(8,128)(2,1)S(1)} %copy-done.13), channel_id=1, source_target_pairs={{0,1},{1,0},{2,3},{3,2},{4,5},{5,4},{6,7},{7,6},{8,9},{9,8},{10,11... | collective-permute-start | bytes 3145736 | tf_op jit(solution)/shard_map/ppermute | solution.py:446
  64.4 5.4 %collective-permute-start.12 = (bf16[512,128]{1,0:T(8,128)(2,1)S(1)}, bf16[512,128]{1,0:T(8,128)(2,1)S(1)}, u32[]{:S(2)}, u32[]{:S(2)}) collective-permute-start(bf16[512,128]{1,0:T(8,128)(2,1)S(1)} %get-tuple-element.60), channel_id=1, source_target_pairs={{0,32},{32,0},{64,96},{96,64},{128,160},{160,128},{192,224},{224,1... | collective-permute-start | bytes 393224 | tf_op jit(solution)/shard_map/ppermute | solution.py:476
  69.8 19.4 %all-to-all-start = ((bf16[8,512,128]{2,1,0:T(8,128)(2,1)}), bf16[8,512,128]{2,1,0:T(8,128)(2,1)S(1)}, u32[]{:S(2)}, u32[]{:S(2)}) async-start(bf16[8,512,128]{2,1,0:T(8,128)(2,1)} %core_sum.1), calls=%async_computation | async-start | bytes 2097152 | tf_op jit(solution)/shard_map/all_to_all | solution.py:478

commit v6 on v5

--- a/solution.py
+++ b/solution.py
@@ -534,7 +534,7 @@
         scalar=True,
         fetch={6: None, 5: 0, 7: None, 8: None, 10: None, 9: None},
         store=(0, 1, 2, 3),
-        limit=51,
+        limit=53,
         micros=10,
     )
     d_tokens = call(

time: 114 us -> 114 us (level)
    unnamed x28 -> x18, local copies, waits for them, and re-layouts: 3.55 us -> 3.15 us
where the time goes in v6:
time: 114 us; the launch traced here: 113 us
  Pallas kernels  41.3 us (36%)
  starting transfers between devices  27.2 us (24%)
  blocking collectives  23.4 us (21%)
  waiting for transfers between devices  16.3 us (14%)
  local copies, waits for them, and re-layouts  4.14 us (4%)
    pallas_call x9, Pallas kernels, call(): pl.pallas_call(body, out_shape=outs, in_specs=[pl.BlockSpec(memory_space=...  41.3 us
    all_to_all x1, blocking collectives, reduced(): lax.all_to_all(both, 'lon', 0, 0, tiled=True, axis_index_groups=groups)  23.4 us
    all_to_all x1, waiting for transfers between devices, reduced(): arrived = lax.all_to_all(chunks_one, 'lat', 0, 0, tiled=True)  8.61 us
    ppermute x2, starting transfers between devices, moved(): lax.ppermute(piece, 'lon', [(i, (i + lon) % n_lon) for i in range(n_lon)])  5.74 us
    all_to_all x1, starting transfers between devices, reduced(): arrived = lax.all_to_all(chunks_one, 'lat', 0, 0, tiled=True)  5.65 us
    ppermute x3, starting transfers between devices, far_reduced(): lax.ppermute(parts[step], 'lat', [(i, (i + 2 * step) % n) for i in range(...  5.55 us
    ppermute x2, starting transfers between devices, moved(): return lax.ppermute(piece, ('lat', 'lon'), route)  4.57 us
    ppermute x3, starting transfers between devices, moved(): lax.ppermute(piece, 'lat', [(i, (i + lat) % n_lat) for i in range(n_lat)])  4.28 us
  transfers between devices with their start and end apart: 14, of which 6 were waited for; matrix products, arithmetic and copies ran while one was open for 0% of the time, Pallas kernels for 23%

profile of v6, /device:TPU:2, one launch (start us, length us, event | category | flops | bytes accessed | tf_op | source)
XLA Modules:
  0.0 113.2 jit_solution(14862114046645212771)
XLA Ops:
  0.6 1.0 slice.3
  1.6 1.6 %collective-permute-start.3 = (bf16[288,512]{1,0:T(8,128)(2,1)S(1)}, bf16[288,512]{1,0:T(8,128)(2,1)S(1)}, u32[]{:S(2)}, u32[]{:S(2)}) collective-permute-start(bf16[288,512]{1,0:T(8,128)(2,1)S(1)} %bitcast.17), channel_id=1, source_target_pairs={{0,224},{32,0},{64,32},{96,64},{128,96},{160,128},{192,160},{224,1... | collective-permute-start | bytes 884744 | tf_op jit(solution)/shard_map/ppermute | solution.py:428
  3.2 0.0 copy-start.7
  3.2 0.0 copy-start.2
  3.2 0.0 copy-start.4
  3.3 0.0 copy-start.5
  3.3 8.3 %forward.1 = (bf16[256,512]{1,0:T(8,128)(2,1)}, bf16[256,512]{1,0:T(8,128)(2,1)}, bf16[128,512]{1,0:T(8,128)(2,1)}, bf16[128,512]{1,0:T(8,128)(2,1)}, bf16[576,5...) custom-call(bf16[576,512]{1,0:T(8,128)(2,1)} %bitcast.20, ...), custom_call_target="tpu_custom_call" | custom-call | flops 10350000128 | bytes 33210000 | tf_op jit(solution)/shard_map/forward/pallas_call | solution.py:411
  11.6 2.3 %collective-permute-start = (bf16[256,512]{1,0:T(8,128)(2,1)}, bf16[256,512]{1,0:T(8,128)(2,1)S(1)}, u32[]{:S(2)}, u32[]{:S(2)}) collective-permute-start(bf16[256,512]{1,0:T(8,128)(2,1)} %get-tuple-element.38), channel_id=1, source_target_pairs={{0,224},{32,0},{64,32},{96,64},{128,96},{160,128},{192,160},{224,1... | collective-permute-start | bytes 786440 | tf_op jit(solution)/shard_map/ppermute | solution.py:428
  13.8 5.6 %collective-permute-start.1 = (bf16[128,512]{1,0:T(8,128)(2,1)}, bf16[128,512]{1,0:T(8,128)(2,1)S(1)}, u32[]{:S(2)}, u32[]{:S(2)}) collective-permute-start(bf16[128,512]{1,0:T(8,128)(2,1)} %get-tuple-element.39), channel_id=1, source_target_pairs={{0,31},{1,0},{2,1},{3,2},{4,3},{5,4},{6,5},{7,6},{8,7},{9,8},{10,9... | collective-permute-start | bytes 393224 | tf_op jit(solution)/shard_map/ppermute | solution.py:430
  19.4 3.2 %collective-permute-start.2 = (bf16[128,512]{1,0:T(8,128)(2,1)}, bf16[128,512]{1,0:T(8,128)(2,1)S(1)}, u32[]{:S(2)}, u32[]{:S(2)}) collective-permute-start(bf16[128,512]{1,0:T(8,128)(2,1)} %get-tuple-element.40), channel_id=1, source_target_pairs={{0,255},{1,224},{2,225},{3,226},{4,227},{5,228},{6,229},{7,230},{8... | collective-permute-start | bytes 393224 | tf_op jit(solution)/shard_map/ppermute | solution.py:436
  22.7 0.0 copy-done.7
  22.7 0.0 collective-permute-done.1.refs_3_
  22.7 2.8 %collective-permute-done.2.refs_4_ = bf16[128,512]{1,0:T(8,128)(2,1)S(1)} collective-permute-done((bf16[128,512]{1,0:T(8,128)(2,1)}, bf16[128,512]{1,0:T(8,128)(2,1)S(1)}, u32[]{:S(2)}, u32[]{:S(2)}) %collective-permute-start.2) | collective-permute-done | bytes 131104 | tf_op jit(solution)/shard_map/ppermute | solution.py:436
  25.5 0.0 collective-permute-done.refs_2_
  25.5 0.0 collective-permute-done.3.refs_6_
  25.5 0.0 copy-done.2
  25.5 0.0 copy-done.4
  25.6 0.0 copy-done.5
  25.6 0.0 copy-start.6
  25.6 0.9 copy-done.6
  26.5 0.0 copy-start.3
  26.5 14.1 %backward_shifted.1 = (bf16[256,512]{1,0:T(8,128)(2,1)S(1)}, bf16[256,512]{1,0:T(8,128)(2,1)S(1)}, bf16[64,512]{1,0:T(8,128)(2,1)S(1)}, bf16[64,512]{1,0:T(8,128...) custom-call(s32[1]{0:T(128)} %bitcast.refs_0_, bf16[256,512]{1,0:T(8,128)(2,1)S(1)} %copy-done.6, ...), custom_call_target="tpu_custom_call" | custom-call | flops 20700000256 | bytes 66420000 | tf_op jit(solution)/shard_map/backward_shifted/pallas_call | solution.py:411
  40.6 0.1 collective-permute-start.7
  40.7 0.4 collective-permute-start.4
  41.1 0.1 collective-permute-start.5
  41.2 1.3 %collective-permute-start.6 = (bf16[64,512]{1,0:T(8,128)(2,1)S(1)}, bf16[64,512]{1,0:T(8,128)(2,1)S(1)}, u32[]{:S(2)}, u32[]{:S(2)}) collective-permute-start(bf16[64,512]{1,0:T(8,128)(2,1)S(1)} %get-tuple-element.44), channel_id=1, source_target_pairs={{0,33},{1,34},{2,35},{3,36},{4,37},{5,38},{6,39},{7,40},{8,41},{9,... | collective-permute-start | bytes 196616 | tf_op jit(solution)/shard_map/ppermute | solution.py:436
  42.6 1.0 collective-permute-done.7
  43.6 0.0 copy-start
  43.6 1.2 %copy-done = bf16[16,64,512]{2,1,0:T(8,128)(2,1)S(1)} copy-done((bf16[16,64,512]{2,1,0:T(8,128)(2,1)S(1)}, bf16[16,64,512]{2,1,0:T(8,128)(2,1)}, u32[]{:S(2)}) %copy-start) | copy-done | bytes 1048600
  44.8 0.9 core_cut.1
  45.7 1.0 collective-permute-start.10
  46.8 2.4 %collective-permute-start.8 = (bf16[2,512,128]{2,1,0:T(8,128)(2,1)S(1)}, bf16[2,512,128]{2,1,0:T(8,128)(2,1)S(1)}, u32[]{:S(2)}, u32[]{:S(2)}) collective-permute-start(bf16[2,512,128]{2,1,0:T(8,128)(2,1)S(1)} %get-tuple-element.54), channel_id=1, source_target_pairs={{0,128},{32,160},{64,192},{96,224},{128,0},{160,32},{192,64},{224,... | collective-permute-start | bytes 786440 | tf_op jit(solution)/shard_map/ppermute | solution.py:468
  49.1 0.0 collective-permute-done.5.refs_3_
  49.2 2.1 %collective-permute-start.9 = (bf16[2,512,128]{2,1,0:T(8,128)(2,1)S(1)}, bf16[2,512,128]{2,1,0:T(8,128)(2,1)S(1)}, u32[]{:S(2)}, u32[]{:S(2)}) collective-permute-start(bf16[2,512,128]{2,1,0:T(8,128)(2,1)S(1)} %get-tuple-element.55), channel_id=1, source_target_pairs={{0,192},{32,224},{64,0},{96,32},{128,64},{160,96},{192,128},{224,1... | collective-permute-start | bytes 786440 | tf_op jit(solution)/shard_map/ppermute | solution.py:468
  51.3 0.0 collective-permute-done.6.refs_4_
  51.3 0.0 collective-permute-done.4.refs_2_
  51.3 0.0 copy-done.3
  51.3 10.2 %backward_plain.1 = (bf16[576,512]{1,0:T(8,128)(2,1)}, bf16[576,1536]{1,0:T(8,128)(2,1)}, bf16[16,64,512]{2,1,0:T(8,128)(2,1)}, bf16[16,64,512]{2,1,0:T(8,128)(2,1)}) custom-call(s32[1]{0:T(128)} %bitcast.refs_0_, bf16[256,512]{1,0:T(8,128)(2,1)S(1)} %get-tuple-element.41.refs_1_, bf16[256,512]{1,0:T(8,128)(2,1)S(1)} %collective-permute-done.4.refs_2_, ...), custom_call_target="tpu_custom_call" | custom-call | flops 11500000256 | bytes 36900000 | tf_op jit(solution)/shard_map/backward_plain/pallas_call | solution.py:411
  61.5 0.0 copy-start.8
  61.5 0.0 copy-start.1
  61.5 0.0 collective-permute-done.10.refs_4_
  61.5 0.0 collective-permute-done.8.refs_2_
  61.5 0.1 collective-permute-done.9.refs_3_
  61.6 0.1 far_sum.1
  61.8 1.0 copy-done.8
  62.7 1.3 %collective-permute-start.11 = (bf16[16,64,512]{2,1,0:T(8,128)(2,1)S(1)}, bf16[16,64,512]{2,1,0:T(8,128)(2,1)S(1)}, u32[]{:S(2)}, u32[]{:S(2)}) collective-permute-start(bf16[16,64,512]{2,1,0:T(8,128)(2,1)S(1)} %copy-done.8), channel_id=1, source_target_pairs={{0,1},{1,0},{2,3},{3,2},{4,5},{5,4},{6,7},{7,6},{8,9},{9,8},{10,11... | collective-permute-start | bytes 3145736 | tf_op jit(solution)/shard_map/ppermute | solution.py:446
  64.0 0.0 collective-permute-start.12
  64.0 2.3 %collective-permute-done.11 = bf16[16,64,512]{2,1,0:T(8,128)(2,1)S(1)} collective-permute-done((bf16[16,64,512]{2,1,0:T(8,128)(2,1)S(1)}, bf16[16,64,512]{2,1,0:T(8,128)(2,1)S(1)}, u32[]{:S(2)}, u32[]{:S(2)}) %collective-permute-start.11) | collective-permute-done | bytes 1048608 | tf_op jit(solution)/shard_map/ppermute | solution.py:446
  66.3 0.0 copy-done.1
  66.3 1.6 %core_sum.1 = bf16[8,512,128]{2,1,0:T(8,128)(2,1)} custom-call(bf16[1024,512]{1,0:T(8,128)(2,1)S(1)} %bitcast.16, bf16[1024,512]{1,0:T(8,128)(2,1)S(1)} %bitcast.14), custom_call_target="tpu_custom_call" | custom-call | flops 1150000000 | bytes 3690000 | tf_op jit(solution)/shard_map/core_sum/pallas_call | solution.py:411
  67.9 1.5 %collective-permute-done.12.refs_2_ = bf16[512,128]{1,0:T(8,128)(2,1)S(1)} collective-permute-done((bf16[512,128]{1,0:T(8,128)(2,1)S(1)}, bf16[512,128]{1,0:T(8,128)(2,1)S(1)}, u32[]{:S(2)}, u32[]{:S(2)}) %collective-permute-start.12) | collective-permute-done | bytes 131104 | tf_op jit(solution)/shard_map/ppermute | solution.py:476
  69.4 5.7 %all-to-all-start = ((bf16[8,512,128]{2,1,0:T(8,128)(2,1)}), bf16[8,512,128]{2,1,0:T(8,128)(2,1)S(1)}, u32[]{:S(2)}, u32[]{:S(2)}) async-start(bf16[8,512,128]{2,1,0:T(8,128)(2,1)} %core_sum.1), calls=%async_computation | async-start | bytes 2097152 | tf_op jit(solution)/shard_map/all_to_all | solution.py:478
  75.1 5.1 %finish_plain.1 = bf16[576,512]{1,0:T(8,128)(2,1)} custom-call(bf16[576,512]{1,0:T(8,128)(2,1)} %get-tuple-element.62.refs_0_, bf16[576,512]{1,0:T(8,128)(2,1)} %get-tuple-element.63.refs_1_, bf16[576,1536]{1,0:T(8,128)(2,1)} %get-tuple-element.64.refs_2_, bf16[2,512,1536]{2,1,0:T(8,128)(2,1)} %refs_3_.3, bf16[288,288]{1,0:T(8,128)(2,1)} %constant.62.clone.refs_4_), custom_call_target="tpu_custom_call" | custom-call | flops 5750000128 | bytes 18450000 | tf_op jit(solution)/shard_map/finish_plain/pallas_call | solution.py:411
  80.2 8.6 %all-to-all-done.refs_0_ = bf16[8,512,128]{2,1,0:T(8,128)(2,1)S(1)} async-done(((bf16[8,512,128]{2,1,0:T(8,128)(2,1)}), bf16[8,512,128]{2,1,0:T(8,128)(2,1)S(1)}, u32[]{:S(2)}, u32[]{:S(2)}) %all-to-all-start) | async-done | bytes 1048608 | tf_op jit(solution)/shard_map/all_to_all | solution.py:478
  88.8 0.2 lat_sum.1
  89.1 23.4 %all_to_all.10.refs_0_ = bf16[16,2,32,128]{3,2,1,0:T(8,128)(2,1)S(1)} all-to-all(bf16[16,2,32,128]{3,2,1,0:T(8,128)(2,1)S(1)} %lat_sum.1), channel_id=1, replica_groups={{0,2,4,6,8,10,12,14,16,18,20,22,24,26,28,30},{1,3,5,7,9,11,13,15,17,19,..., dimensions={0} | all-to-all | bytes 524288 | tf_op jit(solution)/shard_map/all_to_all | solution.py:482
  112.5 0.7 lon_sum.1
  (1 shorter events, 0.0 us)
Async XLA Ops:
  1.6 23.9 %collective-permute-start.3 = (bf16[288,512]{1,0:T(8,128)(2,1)S(1)}, bf16[288,512]{1,0:T(8,128)(2,1)S(1)}, u32[]{:S(2)}, u32[]{:S(2)}) collective-permute-start(bf16[288,512]{1,0:T(8,128)(2,1)S(1)} %bitcast.17), channel_id=1, source_target_pairs={{0,224},{32,0},{64,32},{96,64},{128,96},{160,128},{192,160},{224,1... | collective-permute-start | bytes 884744 | tf_op jit(solution)/shard_map/ppermute | solution.py:428
  3.2 19.5 %copy-start.7 = (pred[144,144]{1,0:T(8,128)(4,1)S(1)}, pred[144,144]{1,0:T(8,128)(4,1)}, u32[]{:S(2)}) copy-start(pred[144,144]{1,0:T(8,128)(4,1)} %constant.69.clone) | copy-start | bytes 62212
  3.2 22.3 %copy-start.2 = (bf16[320,288]{1,0:T(8,128)(2,1)S(1)}, bf16[320,288]{1,0:T(8,128)(2,1)}, u32[]{:S(2)}) copy-start(bf16[320,288]{1,0:T(8,128)(2,1)} %constant.66.clone.refs_11_) | copy-start | bytes 552964
  3.2 22.3 %copy-start.4 = (bf16[288,320]{1,0:T(8,128)(2,1)S(1)}, bf16[288,320]{1,0:T(8,128)(2,1)}, u32[]{:S(2)}) copy-start(bf16[288,320]{1,0:T(8,128)(2,1)} %constant.65.clone.refs_9_) | copy-start | bytes 552964
  3.3 22.3 %copy-start.5 = (bf16[288,352]{1,0:T(8,128)(2,1)S(1)}, bf16[288,352]{1,0:T(8,128)(2,1)}, u32[]{:S(2)}) copy-start(bf16[288,352]{1,0:T(8,128)(2,1)} %constant.67.clone.refs_10_) | copy-start | bytes 608260
  11.6 14.0 %collective-permute-start = (bf16[256,512]{1,0:T(8,128)(2,1)}, bf16[256,512]{1,0:T(8,128)(2,1)S(1)}, u32[]{:S(2)}, u32[]{:S(2)}) collective-permute-start(bf16[256,512]{1,0:T(8,128)(2,1)} %get-tuple-element.38), channel_id=1, source_target_pairs={{0,224},{32,0},{64,32},{96,64},{128,96},{160,128},{192,160},{224,1... | collective-permute-start | bytes 786440 | tf_op jit(solution)/shard_map/ppermute | solution.py:428
  13.8 8.9 %collective-permute-start.1 = (bf16[128,512]{1,0:T(8,128)(2,1)}, bf16[128,512]{1,0:T(8,128)(2,1)S(1)}, u32[]{:S(2)}, u32[]{:S(2)}) collective-permute-start(bf16[128,512]{1,0:T(8,128)(2,1)} %get-tuple-element.39), channel_id=1, source_target_pairs={{0,31},{1,0},{2,1},{3,2},{4,3},{5,4},{6,5},{7,6},{8,7},{9,8},{10,9... | collective-permute-start | bytes 393224 | tf_op jit(solution)/shard_map/ppermute | solution.py:430
  19.4 6.1 %collective-permute-start.2 = (bf16[128,512]{1,0:T(8,128)(2,1)}, bf16[128,512]{1,0:T(8,128)(2,1)S(1)}, u32[]{:S(2)}, u32[]{:S(2)}) collective-permute-start(bf16[128,512]{1,0:T(8,128)(2,1)} %get-tuple-element.40), channel_id=1, source_target_pairs={{0,255},{1,224},{2,225},{3,226},{4,227},{5,228},{6,229},{7,230},{8... | collective-permute-start | bytes 393224 | tf_op jit(solution)/shard_map/ppermute | solution.py:436
  25.6 1.0 copy-start.6
  26.5 24.8 %copy-start.3 = (bf16[288,320]{1,0:T(8,128)(2,1)S(1)}, bf16[288,320]{1,0:T(8,128)(2,1)}, u32[]{:S(2)}) copy-start(bf16[288,320]{1,0:T(8,128)(2,1)} %constant.63.clone.refs_6_) | copy-start | bytes 552964
  40.6 3.0 %collective-permute-start.7 = (bf16[16,64,512]{2,1,0:T(8,128)(2,1)}, bf16[16,64,512]{2,1,0:T(8,128)(2,1)S(1)}, u32[]{:S(2)}, u32[]{:S(2)}) collective-permute-start(bf16[16,64,512]{2,1,0:T(8,128)(2,1)} %get-tuple-element.52), channel_id=1, source_target_pairs={{0,1},{1,0},{2,3},{3,2},{4,5},{5,4},{6,7},{7,6},{8,9},{9,8},{10,11... | collective-permute-start | bytes 3145736 | tf_op jit(solution)/shard_map/ppermute | solution.py:446
  40.7 10.6 %collective-permute-start.4 = (bf16[256,512]{1,0:T(8,128)(2,1)S(1)}, bf16[256,512]{1,0:T(8,128)(2,1)S(1)}, u32[]{:S(2)}, u32[]{:S(2)}) collective-permute-start(bf16[256,512]{1,0:T(8,128)(2,1)S(1)} %get-tuple-element.42), channel_id=1, source_target_pairs={{0,32},{32,64},{64,96},{96,128},{128,160},{160,192},{192,224},{224... | collective-permute-start | bytes 786440 | tf_op jit(solution)/shard_map/ppermute | solution.py:428
  41.1 8.0 %collective-permute-start.5 = (bf16[64,512]{1,0:T(8,128)(2,1)S(1)}, bf16[64,512]{1,0:T(8,128)(2,1)S(1)}, u32[]{:S(2)}, u32[]{:S(2)}) collective-permute-start(bf16[64,512]{1,0:T(8,128)(2,1)S(1)} %get-tuple-element.43), channel_id=1, source_target_pairs={{0,1},{1,2},{2,3},{3,4},{4,5},{5,6},{6,7},{7,8},{8,9},{9,10},{10,1... | collective-permute-start | bytes 196616 | tf_op jit(solution)/shard_map/ppermute | solution.py:430
  41.2 10.1 %collective-permute-start.6 = (bf16[64,512]{1,0:T(8,128)(2,1)S(1)}, bf16[64,512]{1,0:T(8,128)(2,1)S(1)}, u32[]{:S(2)}, u32[]{:S(2)}) collective-permute-start(bf16[64,512]{1,0:T(8,128)(2,1)S(1)} %get-tuple-element.44), channel_id=1, source_target_pairs={{0,33},{1,34},{2,35},{3,36},{4,37},{5,38},{6,39},{7,40},{8,41},{9,... | collective-permute-start | bytes 196616 | tf_op jit(solution)/shard_map/ppermute | solution.py:436
  43.6 1.2 %copy-start = (bf16[16,64,512]{2,1,0:T(8,128)(2,1)S(1)}, bf16[16,64,512]{2,1,0:T(8,128)(2,1)}, u32[]{:S(2)}) copy-start(bf16[16,64,512]{2,1,0:T(8,128)(2,1)} %get-tuple-element.51) | copy-start | bytes 3145732
  45.7 15.8 %collective-permute-start.10 = (bf16[2,512,128]{2,1,0:T(8,128)(2,1)S(1)}, bf16[2,512,128]{2,1,0:T(8,128)(2,1)S(1)}, u32[]{:S(2)}, u32[]{:S(2)}) collective-permute-start(bf16[2,512,128]{2,1,0:T(8,128)(2,1)S(1)} %get-tuple-element.56), channel_id=1, source_target_pairs={{0,64},{32,96},{64,128},{96,160},{128,192},{160,224},{192,0},{224,... | collective-permute-start | bytes 786440 | tf_op jit(solution)/shard_map/ppermute | solution.py:468
  46.8 14.7 %collective-permute-start.8 = (bf16[2,512,128]{2,1,0:T(8,128)(2,1)S(1)}, bf16[2,512,128]{2,1,0:T(8,128)(2,1)S(1)}, u32[]{:S(2)}, u32[]{:S(2)}) collective-permute-start(bf16[2,512,128]{2,1,0:T(8,128)(2,1)S(1)} %get-tuple-element.54), channel_id=1, source_target_pairs={{0,128},{32,160},{64,192},{96,224},{128,0},{160,32},{192,64},{224,... | collective-permute-start | bytes 786440 | tf_op jit(solution)/shard_map/ppermute | solution.py:468
  49.2 12.4 %collective-permute-start.9 = (bf16[2,512,128]{2,1,0:T(8,128)(2,1)S(1)}, bf16[2,512,128]{2,1,0:T(8,128)(2,1)S(1)}, u32[]{:S(2)}, u32[]{:S(2)}) collective-permute-start(bf16[2,512,128]{2,1,0:T(8,128)(2,1)S(1)} %get-tuple-element.55), channel_id=1, source_target_pairs={{0,192},{32,224},{64,0},{96,32},{128,64},{160,96},{192,128},{224,1... | collective-permute-start | bytes 786440 | tf_op jit(solution)/shard_map/ppermute | solution.py:468
  61.5 1.2 %copy-start.8 = (bf16[16,64,512]{2,1,0:T(8,128)(2,1)S(1)}, bf16[16,64,512]{2,1,0:T(8,128)(2,1)}, u32[]{:S(2)}) copy-start(bf16[16,64,512]{2,1,0:T(8,128)(2,1)} %get-tuple-element.59) | copy-start | bytes 3145732
  61.5 4.8 %copy-start.1 = (bf16[16,64,512]{2,1,0:T(8,128)(2,1)S(1)}, bf16[16,64,512]{2,1,0:T(8,128)(2,1)}, u32[]{:S(2)}) copy-start(bf16[16,64,512]{2,1,0:T(8,128)(2,1)} %get-tuple-element.49) | copy-start | bytes 3145732
  62.7 3.6 %collective-permute-start.11 = (bf16[16,64,512]{2,1,0:T(8,128)(2,1)S(1)}, bf16[16,64,512]{2,1,0:T(8,128)(2,1)S(1)}, u32[]{:S(2)}, u32[]{:S(2)}) collective-permute-start(bf16[16,64,512]{2,1,0:T(8,128)(2,1)S(1)} %copy-done.8), channel_id=1, source_target_pairs={{0,1},{1,0},{2,3},{3,2},{4,5},{5,4},{6,7},{7,6},{8,9},{9,8},{10,11... | collective-permute-start | bytes 3145736 | tf_op jit(solution)/shard_map/ppermute | solution.py:446
  64.0 5.4 %collective-permute-start.12 = (bf16[512,128]{1,0:T(8,128)(2,1)S(1)}, bf16[512,128]{1,0:T(8,128)(2,1)S(1)}, u32[]{:S(2)}, u32[]{:S(2)}) collective-permute-start(bf16[512,128]{1,0:T(8,128)(2,1)S(1)} %get-tuple-element.60), channel_id=1, source_target_pairs={{0,32},{32,0},{64,96},{96,64},{128,160},{160,128},{192,224},{224,1... | collective-permute-start | bytes 393224 | tf_op jit(solution)/shard_map/ppermute | solution.py:476
  69.4 19.4 %all-to-all-start = ((bf16[8,512,128]{2,1,0:T(8,128)(2,1)}), bf16[8,512,128]{2,1,0:T(8,128)(2,1)S(1)}, u32[]{:S(2)}, u32[]{:S(2)}) async-start(bf16[8,512,128]{2,1,0:T(8,128)(2,1)} %core_sum.1), calls=%async_computation | async-start | bytes 2097152 | tf_op jit(solution)/shard_map/all_to_all | solution.py:478

commit v7 on v6

--- a/solution.py
+++ b/solution.py
@@ -319,32 +319,28 @@
     return jnp.where(left, top, turned[1]), jnp.where(left, turned[0], bottom)
 
 
-def core_sums(kept, received, landing, sems):
+def core_sums(kept, received):
     half = kept.shape[0] // 2
-    spans = [slice(pair * 128, (pair + 1) * 128) for pair in range(4)]
-    copies = [pltpu.make_async_copy(kept.at[:, at], landing.at[n], sems.at[n]) for n, at in enumerate(spans)]
-    for copy in copies:
-        copy.start()
-    for pair, at in enumerate(spans):
-        copies[pair].wait()
-        total = landing[pair].astype(F32) + received[:, at].astype(F32)
+    for pair in range(4):
+        at = slice(pair * 128, (pair + 1) * 128)
+        total = kept[:, at].astype(F32) + received[:, at].astype(F32)
         for odd, part in enumerate(swapped_halves(total[:half], total[half:])):
             yield 2 * pair + odd, part.astype(BF16)
 
 
-def core_sum_kernel(kept, received, out, landing, made, sems):
+def core_sum_kernel(kept, received, out, made, sems):
     leaving = []
-    for lat, part in core_sums(kept, received, landing, sems):
+    for lat, part in core_sums(kept, received):
         made[lat] = part
-        leaving.append(pltpu.make_async_copy(made.at[lat], out.at[lat], sems.at[4 + lat]))
+        leaving.append(pltpu.make_async_copy(made.at[lat], out.at[lat], sems.at[lat]))
         leaving[-1].start()
     for copy in leaving:
         copy.wait()
 
 
 def core_cut_kernel(place, kept, received, *refs):
-    outs, (landing, held, sems) = refs[:-3], refs[-3:]
-    for lat, part in core_sums(kept, received, landing, sems):
+    outs, held = refs[:-1], refs[-1]
+    for lat, part in core_sums(kept, received):
         held[lat // 2, lat % 2] = part
     for step, out in enumerate(outs):
         out[...] = held[lax.rem(place[0] + step, 4)]
@@ -449,7 +445,7 @@
 def core_reduced(kept, sent):
     return call(
         core_sum_kernel, "core_sum", shape(8, 512, 128), kept.reshape(1024, D), core_swapped(sent),
-        scratch=[(4, 1024, 128), (8, 512, 128), pltpu.SemaphoreType.DMA((12,))], apart=(0,), own_out=True, limit=12,
+        scratch=[(8, 512, 128), pltpu.SemaphoreType.DMA((8,))], own_out=True, limit=12,
     )
 
 
@@ -457,7 +453,7 @@
     place = (lax.axis_index("lat") // 2).astype(jnp.int32).reshape(1)
     return call(
         core_cut_kernel, "core_cut", (shape(2, 512, 128),) * 4, place, kept.reshape(1024, D), core_swapped(sent),
-        scratch=[(4, 1024, 128), (4, 2, 512, 128), pltpu.SemaphoreType.DMA((4,))], scalar=True, apart=(1,), limit=12,
+        scratch=[(4, 2, 512, 128)], scalar=True, limit=12,
     )
 
 

time: 114 us -> 113 us (level)
  transfers between devices with their start and end apart: 14 -> 14, of which waited for: 6 -> 5; matrix products, arithmetic and copies ran while one was open for 0% -> 0% of each run, Pallas kernels for 23% -> 23%
where the time goes in v7:
time: 113 us
  Pallas kernels  40.6 us (36%)
  starting transfers between devices  27.5 us (24%)
  blocking collectives  23 us (20%)
  waiting for transfers between devices  16.6 us (15%)
  local copies, waits for them, and re-layouts  4.19 us (4%)
    pallas_call x9, Pallas kernels, call(): pl.pallas_call(body, out_shape=outs, in_specs=[pl.BlockSpec(memory_space=...  40.6 us
    all_to_all x1, blocking collectives, reduced(): lax.all_to_all(both, 'lon', 0, 0, tiled=True, axis_index_groups=groups)  23 us
    all_to_all x1, waiting for transfers between devices, reduced(): arrived = lax.all_to_all(chunks_one, 'lat', 0, 0, tiled=True)  8.61 us
    ppermute x3, starting transfers between devices, far_reduced(): lax.ppermute(parts[step], 'lat', [(i, (i + 2 * step) % n) for i in range(...  5.91 us
    ppermute x2, starting transfers between devices, moved(): lax.ppermute(piece, 'lon', [(i, (i + lon) % n_lon) for i in range(n_lon)])  5.74 us
    all_to_all x1, starting transfers between devices, reduced(): arrived = lax.all_to_all(chunks_one, 'lat', 0, 0, tiled=True)  5.65 us
    ppermute x2, starting transfers between devices, moved(): return lax.ppermute(piece, ('lat', 'lon'), route)  4.57 us
    ppermute x3, starting transfers between devices, moved(): lax.ppermute(piece, 'lat', [(i, (i + lat) % n_lat) for i in range(n_lat)])  4.28 us
  transfers between devices with their start and end apart: 14, of which 5 were waited for; matrix products, arithmetic and copies ran while one was open for 0% of the time, Pallas kernels for 23%

profile of v7, /device:TPU:2, one launch (start us, length us, event | category | flops | bytes accessed | tf_op | source)
XLA Modules:
  0.0 112.8 jit_solution(3660026936962098528)
XLA Ops:
  0.6 1.0 slice.3
  1.6 1.6 %collective-permute-start.3 = (bf16[288,512]{1,0:T(8,128)(2,1)S(1)}, bf16[288,512]{1,0:T(8,128)(2,1)S(1)}, u32[]{:S(2)}, u32[]{:S(2)}) collective-permute-start(bf16[288,512]{1,0:T(8,128)(2,1)S(1)} %bitcast.17), channel_id=1, source_target_pairs={{0,224},{32,0},{64,32},{96,64},{128,96},{160,128},{192,160},{224,1... | collective-permute-start | bytes 884744 | tf_op jit(solution)/shard_map/ppermute | solution.py:424
  3.2 0.0 copy-start.7
  3.2 0.0 copy-start.2
  3.2 0.0 copy-start.4
  3.3 0.0 copy-start.5
  3.3 8.3 %forward.1 = (bf16[256,512]{1,0:T(8,128)(2,1)}, bf16[256,512]{1,0:T(8,128)(2,1)}, bf16[128,512]{1,0:T(8,128)(2,1)}, bf16[128,512]{1,0:T(8,128)(2,1)}, bf16[576,5...) custom-call(bf16[576,512]{1,0:T(8,128)(2,1)} %bitcast.20, ...), custom_call_target="tpu_custom_call" | custom-call | flops 10350000128 | bytes 33210000 | tf_op jit(solution)/shard_map/forward/pallas_call | solution.py:407
  11.6 2.3 %collective-permute-start = (bf16[256,512]{1,0:T(8,128)(2,1)}, bf16[256,512]{1,0:T(8,128)(2,1)S(1)}, u32[]{:S(2)}, u32[]{:S(2)}) collective-permute-start(bf16[256,512]{1,0:T(8,128)(2,1)} %get-tuple-element.38), channel_id=1, source_target_pairs={{0,224},{32,0},{64,32},{96,64},{128,96},{160,128},{192,160},{224,1... | collective-permute-start | bytes 786440 | tf_op jit(solution)/shard_map/ppermute | solution.py:424
  13.8 5.6 %collective-permute-start.1 = (bf16[128,512]{1,0:T(8,128)(2,1)}, bf16[128,512]{1,0:T(8,128)(2,1)S(1)}, u32[]{:S(2)}, u32[]{:S(2)}) collective-permute-start(bf16[128,512]{1,0:T(8,128)(2,1)} %get-tuple-element.39), channel_id=1, source_target_pairs={{0,31},{1,0},{2,1},{3,2},{4,3},{5,4},{6,5},{7,6},{8,7},{9,8},{10,9... | collective-permute-start | bytes 393224 | tf_op jit(solution)/shard_map/ppermute | solution.py:426
  19.4 3.2 %collective-permute-start.2 = (bf16[128,512]{1,0:T(8,128)(2,1)}, bf16[128,512]{1,0:T(8,128)(2,1)S(1)}, u32[]{:S(2)}, u32[]{:S(2)}) collective-permute-start(bf16[128,512]{1,0:T(8,128)(2,1)} %get-tuple-element.40), channel_id=1, source_target_pairs={{0,255},{1,224},{2,225},{3,226},{4,227},{5,228},{6,229},{7,230},{8... | collective-permute-start | bytes 393224 | tf_op jit(solution)/shard_map/ppermute | solution.py:432
  22.7 0.0 copy-done.7
  22.7 0.0 collective-permute-done.1.refs_3_
  22.7 2.8 %collective-permute-done.2.refs_4_ = bf16[128,512]{1,0:T(8,128)(2,1)S(1)} collective-permute-done((bf16[128,512]{1,0:T(8,128)(2,1)}, bf16[128,512]{1,0:T(8,128)(2,1)S(1)}, u32[]{:S(2)}, u32[]{:S(2)}) %collective-permute-start.2) | collective-permute-done | bytes 131104 | tf_op jit(solution)/shard_map/ppermute | solution.py:432
  25.5 0.0 collective-permute-done.refs_2_
  25.5 0.0 collective-permute-done.3.refs_6_
  25.5 0.0 copy-done.2
  25.5 0.0 copy-done.4
  25.6 0.0 copy-done.5
  25.6 0.0 copy-start.6
  25.6 0.9 copy-done.6
  26.5 0.0 copy-start.3
  26.5 14.1 %backward_shifted.1 = (bf16[256,512]{1,0:T(8,128)(2,1)S(1)}, bf16[256,512]{1,0:T(8,128)(2,1)S(1)}, bf16[64,512]{1,0:T(8,128)(2,1)S(1)}, bf16[64,512]{1,0:T(8,128...) custom-call(s32[1]{0:T(128)} %bitcast.refs_0_, bf16[256,512]{1,0:T(8,128)(2,1)S(1)} %copy-done.6, ...), custom_call_target="tpu_custom_call" | custom-call | flops 20700000256 | bytes 66420000 | tf_op jit(solution)/shard_map/backward_shifted/pallas_call | solution.py:407
  40.6 0.1 collective-permute-start.7
  40.7 0.4 collective-permute-start.4
  41.1 0.1 collective-permute-start.5
  41.2 1.3 %collective-permute-start.6 = (bf16[64,512]{1,0:T(8,128)(2,1)S(1)}, bf16[64,512]{1,0:T(8,128)(2,1)S(1)}, u32[]{:S(2)}, u32[]{:S(2)}) collective-permute-start(bf16[64,512]{1,0:T(8,128)(2,1)S(1)} %get-tuple-element.44), channel_id=1, source_target_pairs={{0,33},{1,34},{2,35},{3,36},{4,37},{5,38},{6,39},{7,40},{8,41},{9,... | collective-permute-start | bytes 196616 | tf_op jit(solution)/shard_map/ppermute | solution.py:432
  42.6 1.0 collective-permute-done.7
  43.6 0.0 copy-start
  43.6 1.2 %copy-done = bf16[16,64,512]{2,1,0:T(8,128)(2,1)S(1)} copy-done((bf16[16,64,512]{2,1,0:T(8,128)(2,1)S(1)}, bf16[16,64,512]{2,1,0:T(8,128)(2,1)}, u32[]{:S(2)}) %copy-start) | copy-done | bytes 1048600
  44.8 0.6 core_cut.1
  45.4 1.0 collective-permute-start.10
  46.4 2.4 %collective-permute-start.8 = (bf16[2,512,128]{2,1,0:T(8,128)(2,1)S(1)}, bf16[2,512,128]{2,1,0:T(8,128)(2,1)S(1)}, u32[]{:S(2)}, u32[]{:S(2)}) collective-permute-start(bf16[2,512,128]{2,1,0:T(8,128)(2,1)S(1)} %get-tuple-element.54), channel_id=1, source_target_pairs={{0,128},{32,160},{64,192},{96,224},{128,0},{160,32},{192,64},{224,... | collective-permute-start | bytes 786440 | tf_op jit(solution)/shard_map/ppermute | solution.py:464
  48.8 0.0 collective-permute-done.5.refs_3_
  48.8 2.5 %collective-permute-start.9 = (bf16[2,512,128]{2,1,0:T(8,128)(2,1)S(1)}, bf16[2,512,128]{2,1,0:T(8,128)(2,1)S(1)}, u32[]{:S(2)}, u32[]{:S(2)}) collective-permute-start(bf16[2,512,128]{2,1,0:T(8,128)(2,1)S(1)} %get-tuple-element.55), channel_id=1, source_target_pairs={{0,192},{32,224},{64,0},{96,32},{128,64},{160,96},{192,128},{224,1... | collective-permute-start | bytes 786440 | tf_op jit(solution)/shard_map/ppermute | solution.py:464
  51.3 0.0 collective-permute-done.6.refs_4_
  51.3 0.0 collective-permute-done.4.refs_2_
  51.3 0.0 copy-done.3
  51.3 10.2 %backward_plain.1 = (bf16[576,512]{1,0:T(8,128)(2,1)}, bf16[576,1536]{1,0:T(8,128)(2,1)}, bf16[16,64,512]{2,1,0:T(8,128)(2,1)}, bf16[16,64,512]{2,1,0:T(8,128)(2,1)}) custom-call(s32[1]{0:T(128)} %bitcast.refs_0_, bf16[256,512]{1,0:T(8,128)(2,1)S(1)} %get-tuple-element.41.refs_1_, bf16[256,512]{1,0:T(8,128)(2,1)S(1)} %collective-permute-done.4.refs_2_, ...), custom_call_target="tpu_custom_call" | custom-call | flops 11500000256 | bytes 36900000 | tf_op jit(solution)/shard_map/backward_plain/pallas_call | solution.py:407
  61.5 0.0 copy-start.8
  61.5 0.0 copy-start.1
  61.5 0.0 collective-permute-done.10.refs_4_
  61.5 0.0 collective-permute-done.8.refs_2_
  61.5 0.0 collective-permute-done.9.refs_3_
  61.5 0.2 far_sum.1
  61.7 1.0 copy-done.8
  62.7 1.3 %collective-permute-start.11 = (bf16[16,64,512]{2,1,0:T(8,128)(2,1)S(1)}, bf16[16,64,512]{2,1,0:T(8,128)(2,1)S(1)}, u32[]{:S(2)}, u32[]{:S(2)}) collective-permute-start(bf16[16,64,512]{2,1,0:T(8,128)(2,1)S(1)} %copy-done.8), channel_id=1, source_target_pairs={{0,1},{1,0},{2,3},{3,2},{4,5},{5,4},{6,7},{7,6},{8,9},{9,8},{10,11... | collective-permute-start | bytes 3145736 | tf_op jit(solution)/shard_map/ppermute | solution.py:442
  64.0 0.0 collective-permute-start.12
  64.0 2.3 %collective-permute-done.11 = bf16[16,64,512]{2,1,0:T(8,128)(2,1)S(1)} collective-permute-done((bf16[16,64,512]{2,1,0:T(8,128)(2,1)S(1)}, bf16[16,64,512]{2,1,0:T(8,128)(2,1)S(1)}, u32[]{:S(2)}, u32[]{:S(2)}) %collective-permute-start.11) | collective-permute-done | bytes 1048608 | tf_op jit(solution)/shard_map/ppermute | solution.py:442
  66.3 0.0 copy-done.1
  66.3 1.3 %core_sum.1 = bf16[8,512,128]{2,1,0:T(8,128)(2,1)} custom-call(bf16[1024,512]{1,0:T(8,128)(2,1)S(1)} %bitcast.16, bf16[1024,512]{1,0:T(8,128)(2,1)S(1)} %bitcast.14), custom_call_target="tpu_custom_call" | custom-call | flops 1150000000 | bytes 3690000 | tf_op jit(solution)/shard_map/core_sum/pallas_call | solution.py:407
  67.6 1.8 %collective-permute-done.12.refs_2_ = bf16[512,128]{1,0:T(8,128)(2,1)S(1)} collective-permute-done((bf16[512,128]{1,0:T(8,128)(2,1)S(1)}, bf16[512,128]{1,0:T(8,128)(2,1)S(1)}, u32[]{:S(2)}, u32[]{:S(2)}) %collective-permute-start.12) | collective-permute-done | bytes 131104 | tf_op jit(solution)/shard_map/ppermute | solution.py:472
  69.4 5.7 %all-to-all-start = ((bf16[8,512,128]{2,1,0:T(8,128)(2,1)}), bf16[8,512,128]{2,1,0:T(8,128)(2,1)S(1)}, u32[]{:S(2)}, u32[]{:S(2)}) async-start(bf16[8,512,128]{2,1,0:T(8,128)(2,1)} %core_sum.1), calls=%async_computation | async-start | bytes 2097152 | tf_op jit(solution)/shard_map/all_to_all | solution.py:474
  75.1 5.1 %finish_plain.1 = bf16[576,512]{1,0:T(8,128)(2,1)} custom-call(bf16[576,512]{1,0:T(8,128)(2,1)} %get-tuple-element.62.refs_0_, bf16[576,512]{1,0:T(8,128)(2,1)} %get-tuple-element.63.refs_1_, bf16[576,1536]{1,0:T(8,128)(2,1)} %get-tuple-element.64.refs_2_, bf16[2,512,1536]{2,1,0:T(8,128)(2,1)} %refs_3_.3, bf16[288,288]{1,0:T(8,128)(2,1)} %constant.62.clone.refs_4_), custom_call_target="tpu_custom_call" | custom-call | flops 5750000128 | bytes 18450000 | tf_op jit(solution)/shard_map/finish_plain/pallas_call | solution.py:407
  80.2 8.6 %all-to-all-done.refs_0_ = bf16[8,512,128]{2,1,0:T(8,128)(2,1)S(1)} async-done(((bf16[8,512,128]{2,1,0:T(8,128)(2,1)}), bf16[8,512,128]{2,1,0:T(8,128)(2,1)S(1)}, u32[]{:S(2)}, u32[]{:S(2)}) %all-to-all-start) | async-done | bytes 1048608 | tf_op jit(solution)/shard_map/all_to_all | solution.py:474
  88.8 0.2 lat_sum.1
  89.1 23.0 %all_to_all.10.refs_0_ = bf16[16,2,32,128]{3,2,1,0:T(8,128)(2,1)S(1)} all-to-all(bf16[16,2,32,128]{3,2,1,0:T(8,128)(2,1)S(1)} %lat_sum.1), channel_id=1, replica_groups={{0,2,4,6,8,10,12,14,16,18,20,22,24,26,28,30},{1,3,5,7,9,11,13,15,17,19,..., dimensions={0} | all-to-all | bytes 524288 | tf_op jit(solution)/shard_map/all_to_all | solution.py:478
  112.1 0.7 lon_sum.1
  (1 shorter events, 0.0 us)
Async XLA Ops:
  1.6 23.9 %collective-permute-start.3 = (bf16[288,512]{1,0:T(8,128)(2,1)S(1)}, bf16[288,512]{1,0:T(8,128)(2,1)S(1)}, u32[]{:S(2)}, u32[]{:S(2)}) collective-permute-start(bf16[288,512]{1,0:T(8,128)(2,1)S(1)} %bitcast.17), channel_id=1, source_target_pairs={{0,224},{32,0},{64,32},{96,64},{128,96},{160,128},{192,160},{224,1... | collective-permute-start | bytes 884744 | tf_op jit(solution)/shard_map/ppermute | solution.py:424
  3.2 19.5 %copy-start.7 = (pred[144,144]{1,0:T(8,128)(4,1)S(1)}, pred[144,144]{1,0:T(8,128)(4,1)}, u32[]{:S(2)}) copy-start(pred[144,144]{1,0:T(8,128)(4,1)} %constant.69.clone) | copy-start | bytes 62212
  3.2 22.3 %copy-start.2 = (bf16[320,288]{1,0:T(8,128)(2,1)S(1)}, bf16[320,288]{1,0:T(8,128)(2,1)}, u32[]{:S(2)}) copy-start(bf16[320,288]{1,0:T(8,128)(2,1)} %constant.66.clone.refs_11_) | copy-start | bytes 552964
  3.2 22.3 %copy-start.4 = (bf16[288,320]{1,0:T(8,128)(2,1)S(1)}, bf16[288,320]{1,0:T(8,128)(2,1)}, u32[]{:S(2)}) copy-start(bf16[288,320]{1,0:T(8,128)(2,1)} %constant.65.clone.refs_9_) | copy-start | bytes 552964
  3.3 22.3 %copy-start.5 = (bf16[288,352]{1,0:T(8,128)(2,1)S(1)}, bf16[288,352]{1,0:T(8,128)(2,1)}, u32[]{:S(2)}) copy-start(bf16[288,352]{1,0:T(8,128)(2,1)} %constant.67.clone.refs_10_) | copy-start | bytes 608260
  11.6 14.0 %collective-permute-start = (bf16[256,512]{1,0:T(8,128)(2,1)}, bf16[256,512]{1,0:T(8,128)(2,1)S(1)}, u32[]{:S(2)}, u32[]{:S(2)}) collective-permute-start(bf16[256,512]{1,0:T(8,128)(2,1)} %get-tuple-element.38), channel_id=1, source_target_pairs={{0,224},{32,0},{64,32},{96,64},{128,96},{160,128},{192,160},{224,1... | collective-permute-start | bytes 786440 | tf_op jit(solution)/shard_map/ppermute | solution.py:424
  13.8 8.9 %collective-permute-start.1 = (bf16[128,512]{1,0:T(8,128)(2,1)}, bf16[128,512]{1,0:T(8,128)(2,1)S(1)}, u32[]{:S(2)}, u32[]{:S(2)}) collective-permute-start(bf16[128,512]{1,0:T(8,128)(2,1)} %get-tuple-element.39), channel_id=1, source_target_pairs={{0,31},{1,0},{2,1},{3,2},{4,3},{5,4},{6,5},{7,6},{8,7},{9,8},{10,9... | collective-permute-start | bytes 393224 | tf_op jit(solution)/shard_map/ppermute | solution.py:426
  19.4 6.1 %collective-permute-start.2 = (bf16[128,512]{1,0:T(8,128)(2,1)}, bf16[128,512]{1,0:T(8,128)(2,1)S(1)}, u32[]{:S(2)}, u32[]{:S(2)}) collective-permute-start(bf16[128,512]{1,0:T(8,128)(2,1)} %get-tuple-element.40), channel_id=1, source_target_pairs={{0,255},{1,224},{2,225},{3,226},{4,227},{5,228},{6,229},{7,230},{8... | collective-permute-start | bytes 393224 | tf_op jit(solution)/shard_map/ppermute | solution.py:432
  25.6 1.0 copy-start.6
  26.5 24.8 %copy-start.3 = (bf16[288,320]{1,0:T(8,128)(2,1)S(1)}, bf16[288,320]{1,0:T(8,128)(2,1)}, u32[]{:S(2)}) copy-start(bf16[288,320]{1,0:T(8,128)(2,1)} %constant.63.clone.refs_6_) | copy-start | bytes 552964
  40.6 3.0 %collective-permute-start.7 = (bf16[16,64,512]{2,1,0:T(8,128)(2,1)}, bf16[16,64,512]{2,1,0:T(8,128)(2,1)S(1)}, u32[]{:S(2)}, u32[]{:S(2)}) collective-permute-start(bf16[16,64,512]{2,1,0:T(8,128)(2,1)} %get-tuple-element.52), channel_id=1, source_target_pairs={{0,1},{1,0},{2,3},{3,2},{4,5},{5,4},{6,7},{7,6},{8,9},{9,8},{10,11... | collective-permute-start | bytes 3145736 | tf_op jit(solution)/shard_map/ppermute | solution.py:442
  40.7 10.6 %collective-permute-start.4 = (bf16[256,512]{1,0:T(8,128)(2,1)S(1)}, bf16[256,512]{1,0:T(8,128)(2,1)S(1)}, u32[]{:S(2)}, u32[]{:S(2)}) collective-permute-start(bf16[256,512]{1,0:T(8,128)(2,1)S(1)} %get-tuple-element.42), channel_id=1, source_target_pairs={{0,32},{32,64},{64,96},{96,128},{128,160},{160,192},{192,224},{224... | collective-permute-start | bytes 786440 | tf_op jit(solution)/shard_map/ppermute | solution.py:424
  41.1 7.7 %collective-permute-start.5 = (bf16[64,512]{1,0:T(8,128)(2,1)S(1)}, bf16[64,512]{1,0:T(8,128)(2,1)S(1)}, u32[]{:S(2)}, u32[]{:S(2)}) collective-permute-start(bf16[64,512]{1,0:T(8,128)(2,1)S(1)} %get-tuple-element.43), channel_id=1, source_target_pairs={{0,1},{1,2},{2,3},{3,4},{4,5},{5,6},{6,7},{7,8},{8,9},{9,10},{10,1... | collective-permute-start | bytes 196616 | tf_op jit(solution)/shard_map/ppermute | solution.py:426
  41.2 10.1 %collective-permute-start.6 = (bf16[64,512]{1,0:T(8,128)(2,1)S(1)}, bf16[64,512]{1,0:T(8,128)(2,1)S(1)}, u32[]{:S(2)}, u32[]{:S(2)}) collective-permute-start(bf16[64,512]{1,0:T(8,128)(2,1)S(1)} %get-tuple-element.44), channel_id=1, source_target_pairs={{0,33},{1,34},{2,35},{3,36},{4,37},{5,38},{6,39},{7,40},{8,41},{9,... | collective-permute-start | bytes 196616 | tf_op jit(solution)/shard_map/ppermute | solution.py:432
  43.6 1.2 %copy-start = (bf16[16,64,512]{2,1,0:T(8,128)(2,1)S(1)}, bf16[16,64,512]{2,1,0:T(8,128)(2,1)}, u32[]{:S(2)}) copy-start(bf16[16,64,512]{2,1,0:T(8,128)(2,1)} %get-tuple-element.51) | copy-start | bytes 3145732
  45.4 16.1 %collective-permute-start.10 = (bf16[2,512,128]{2,1,0:T(8,128)(2,1)S(1)}, bf16[2,512,128]{2,1,0:T(8,128)(2,1)S(1)}, u32[]{:S(2)}, u32[]{:S(2)}) collective-permute-start(bf16[2,512,128]{2,1,0:T(8,128)(2,1)S(1)} %get-tuple-element.56), channel_id=1, source_target_pairs={{0,64},{32,96},{64,128},{96,160},{128,192},{160,224},{192,0},{224,... | collective-permute-start | bytes 786440 | tf_op jit(solution)/shard_map/ppermute | solution.py:464
  46.4 15.1 %collective-permute-start.8 = (bf16[2,512,128]{2,1,0:T(8,128)(2,1)S(1)}, bf16[2,512,128]{2,1,0:T(8,128)(2,1)S(1)}, u32[]{:S(2)}, u32[]{:S(2)}) collective-permute-start(bf16[2,512,128]{2,1,0:T(8,128)(2,1)S(1)} %get-tuple-element.54), channel_id=1, source_target_pairs={{0,128},{32,160},{64,192},{96,224},{128,0},{160,32},{192,64},{224,... | collective-permute-start | bytes 786440 | tf_op jit(solution)/shard_map/ppermute | solution.py:464
  48.8 12.7 %collective-permute-start.9 = (bf16[2,512,128]{2,1,0:T(8,128)(2,1)S(1)}, bf16[2,512,128]{2,1,0:T(8,128)(2,1)S(1)}, u32[]{:S(2)}, u32[]{:S(2)}) collective-permute-start(bf16[2,512,128]{2,1,0:T(8,128)(2,1)S(1)} %get-tuple-element.55), channel_id=1, source_target_pairs={{0,192},{32,224},{64,0},{96,32},{128,64},{160,96},{192,128},{224,1... | collective-permute-start | bytes 786440 | tf_op jit(solution)/shard_map/ppermute | solution.py:464
  61.5 1.2 %copy-start.8 = (bf16[16,64,512]{2,1,0:T(8,128)(2,1)S(1)}, bf16[16,64,512]{2,1,0:T(8,128)(2,1)}, u32[]{:S(2)}) copy-start(bf16[16,64,512]{2,1,0:T(8,128)(2,1)} %get-tuple-element.59) | copy-start | bytes 3145732
  61.5 4.8 %copy-start.1 = (bf16[16,64,512]{2,1,0:T(8,128)(2,1)S(1)}, bf16[16,64,512]{2,1,0:T(8,128)(2,1)}, u32[]{:S(2)}) copy-start(bf16[16,64,512]{2,1,0:T(8,128)(2,1)} %get-tuple-element.49) | copy-start | bytes 3145732
  62.7 3.6 %collective-permute-start.11 = (bf16[16,64,512]{2,1,0:T(8,128)(2,1)S(1)}, bf16[16,64,512]{2,1,0:T(8,128)(2,1)S(1)}, u32[]{:S(2)}, u32[]{:S(2)}) collective-permute-start(bf16[16,64,512]{2,1,0:T(8,128)(2,1)S(1)} %copy-done.8), channel_id=1, source_target_pairs={{0,1},{1,0},{2,3},{3,2},{4,5},{5,4},{6,7},{7,6},{8,9},{9,8},{10,11... | collective-permute-start | bytes 3145736 | tf_op jit(solution)/shard_map/ppermute | solution.py:442
  64.0 5.4 %collective-permute-start.12 = (bf16[512,128]{1,0:T(8,128)(2,1)S(1)}, bf16[512,128]{1,0:T(8,128)(2,1)S(1)}, u32[]{:S(2)}, u32[]{:S(2)}) collective-permute-start(bf16[512,128]{1,0:T(8,128)(2,1)S(1)} %get-tuple-element.60), channel_id=1, source_target_pairs={{0,32},{32,0},{64,96},{96,64},{128,160},{160,128},{192,224},{224,1... | collective-permute-start | bytes 393224 | tf_op jit(solution)/shard_map/ppermute | solution.py:472
  69.4 19.4 %all-to-all-start = ((bf16[8,512,128]{2,1,0:T(8,128)(2,1)}), bf16[8,512,128]{2,1,0:T(8,128)(2,1)S(1)}, u32[]{:S(2)}, u32[]{:S(2)}) async-start(bf16[8,512,128]{2,1,0:T(8,128)(2,1)} %core_sum.1), calls=%async_computation | async-start | bytes 2097152 | tf_op jit(solution)/shard_map/all_to_all | solution.py:474
